TPU v7x, 32 devices: a whole 2x2x4 slice. The times are simulated.
32 devices in a mesh: range: 8 (over z, y), doppler: 4 (over x, core).
Axes of the slice: x: 2, y: 2, z: 4, core: 2. Of those that a mesh axis runs over, the one named last changes fastest.
Arguments:
- snapshots: bfloat16 [32, 4096, 384], P(None, ('range', 'doppler')), may hold values from -24 to 24
- steering: bfloat16 [32, 384, 256], P(('range', 'doppler')), may hold values from -0.3125 to 0.3125
- train_list: int32 [32, 32], P(('range', 'doppler')), may hold values from 0 to 31, each once within a row
- train_count: int32 [32], P(('range', 'doppler')), may hold values from 10 to 32, as said below
Outputs:
- beam_output: bfloat16 [32, 4096, 256], P(None, ('range', 'doppler'))
Inputs may be any that keep to these rules, and one draw needn't show every extreme that they name: `train_count`: some bin trains on all 32 blocks and some bin on 10.
All inputs are finite; a program needn't handle non-finite values.
Results may differ from a plain program's by a relative error of at most 0.0052.
Values may be sent and summed in bfloat16 or wider, within the bound.
No kernel may reach another device: no remote copies, remote signals or barrier semaphores. Data moves between devices by JAX's collectives and lax.ppermute only.
A program may use at most 128 MiB of HBM per device.

v0:
```python
import jax
import jax.numpy as jnp
from jax import lax
from jax.sharding import PartitionSpec as P

BLOCK = 128


LOADING = 0.1


def selection(train_list, train_count):
    block_total = train_list.shape[1]
    position = lax.broadcasted_iota(jnp.int32, (1, block_total, 1), 1)
    block_ids = lax.broadcasted_iota(jnp.int32, (1, 1, block_total), 2)
    matches = (train_list[:, :, None] == block_ids) & (position < train_count[:, None, None])
    return jnp.sum(matches.astype(jnp.int32), axis=1)


def solve_one(factor, rhs_block):
    inner = lax.linalg.triangular_solve(factor, rhs_block, left_side=True, lower=True)
    return lax.linalg.triangular_solve(factor, inner, left_side=True, lower=True, transpose_a=True)


def adapt(own_snaps, train_list, train_count, steering):
    own_bins, gate_total, channels = own_snaps.shape
    block_total = train_list.shape[1]
    chosen = selection(train_list, train_count)
    blocks = own_snaps.reshape(own_bins, block_total, gate_total // block_total, channels)
    masked = blocks * chosen.astype(own_snaps.dtype)[:, :, None, None]
    gram_sum = jnp.einsum("bnrd,bnre->bde", masked, blocks, preferred_element_type=jnp.float32)
    scale = (BLOCK * train_count).astype(jnp.float32)
    covariance = (
        gram_sum / scale[:, None, None] + LOADING * jnp.eye(channels, dtype=jnp.float32)[None]
    )
    factor = jnp.linalg.cholesky(covariance)
    steer_full = steering.astype(jnp.float32)
    solved = jax.vmap(solve_one)(factor, steer_full)
    response = jnp.sum(steer_full * solved, axis=1)
    return (solved / response[:, None, :]).astype(jnp.bfloat16)


def body(snapshots, steering, train_list, train_count):
    bin_total, gate_rows, channels = snapshots.shape
    own_bins = steering.shape[0]
    devices = bin_total // own_bins
    outgoing = snapshots.reshape(devices, own_bins, gate_rows, channels)
    arrived = lax.all_to_all(
        outgoing, ("range", "doppler"), split_axis=0, concat_axis=0, tiled=True
    )
    own_snaps = jnp.moveaxis(arrived, 1, 0).reshape(own_bins, devices * gate_rows, channels)
    weights = adapt(own_snaps, train_list, train_count, steering)
    return jnp.einsum(
        "bgd,bde->bge",
        snapshots,
        lax.all_gather(weights, ("range", "doppler"), axis=0, tiled=True),
        preferred_element_type=jnp.float32,
    ).astype(jnp.bfloat16)


def solution(mesh):
    placed = (
        P(None, ("range", "doppler"), None),
        P(("range", "doppler"), None, None),
        P(("range", "doppler"), None),
        P(("range", "doppler")),
    )
    return jax.shard_map(
        body,
        mesh=mesh,
        in_specs=placed,
        out_specs=P(None, ("range", "doppler"), None),
        check_vma=False,
    )
```

profile of v0, /device:TPU:0, one launch (start us, length us, event | category | flops | bytes accessed | tf_op | source)
XLA Modules:
  0.0 290.4 jit_solution(3452154459513767890)
XLA Ops:
  6.5 7.3 %all-to-all-start = ((bf16[32,1,128,384]{3,2,1,0:T(8,128)(2,1)}), bf16[32,1,128,384]{3,2,1,0:T(8,128)(2,1)S(1)}, u32[]{:S(2)}, u32[]{:S(2)}) async-start(bf16[32,1,128,384]{3,2,1,0:T(8,128)(2,1)} %bitcast.154), calls=%async_computation | async-start | bytes 6291456 | tf_op jit(solution)/shard_map/all_to_all | solution.py:48
  14.7 1.0 convert_element_type.47
  15.6 69.7 %all-to-all-done = bf16[32,1,128,384]{3,2,1,0:T(8,128)(2,1)S(1)} async-done(((bf16[32,1,128,384]{3,2,1,0:T(8,128)(2,1)}), bf16[32,1,128,384]{3,2,1,0:T(8,128)(2,1)S(1)}, u32[]{:S(2)}, u32[]{:S(2)}) %all-to-all-start) | async-done | bytes 3145760 | tf_op jit(solution)/shard_map/all_to_all | solution.py:48
  85.3 2.7 fusion.22
  88.0 1.3 copy.17
  89.3 1.1 fusion.27
  90.4 11.7 %custom-call.27 = f32[1,128,128]{2,1,0:T(8,128)S(1)} custom-call(f32[1,128,128]{2,1,0:T(8,128)S(1)} %cholesky.192), custom_call_target="Cholesky" | custom-call | tf_op jit(solution)/shard_map/jit(cholesky)/cholesky | solution.py:36
  102.2 9.8 %custom-call.28 = f32[1,1,128,128]{2,3,1,0:T(8,128)S(1)} custom-call(f32[1,1,128,128]{3,2,1,0:T(8,128)S(1)} %get-tuple-element.29), custom_call_target="InvertDiagBlocksLowerTriangular" | custom-call | tf_op jit(solution)/shard_map/jit(cholesky)/cholesky | solution.py:36
  112.6 11.8 %custom-call.29 = f32[1,128,128]{2,1,0:T(8,128)S(1)} custom-call(f32[1,128,128]{2,1,0:T(8,128)S(1)} %cholesky.196), custom_call_target="Cholesky" | custom-call | tf_op jit(solution)/shard_map/jit(cholesky)/cholesky | solution.py:36
  124.5 9.8 %custom-call.30 = f32[1,1,128,128]{2,3,1,0:T(8,128)S(1)} custom-call(f32[1,1,128,128]{3,2,1,0:T(8,128)S(1)} %get-tuple-element.26), custom_call_target="InvertDiagBlocksLowerTriangular" | custom-call | tf_op jit(solution)/shard_map/jit(cholesky)/cholesky | solution.py:36
  134.8 11.7 %custom-call.31 = f32[1,128,128]{2,1,0:T(8,128)S(1)} custom-call(f32[1,128,128]{2,1,0:T(8,128)S(1)} %fusion.16), custom_call_target="Cholesky" | custom-call | tf_op jit(solution)/shard_map/jit(cholesky)/cholesky | solution.py:36
  146.5 0.7 compare_reduce_fusion
  149.7 0.9 select_select_fusion
  150.5 10.5 %while.1 = (s32[]{:T(128)}, f32[1,384,384]{2,1,0:T(8,128)}, s32[3,2]{0,1:T(2,128)S(1)}, f32[3,1,128,128]{3,2,1,0:T(8,128)}, s32[]{:T(128)}) while((s32[]{:T(128)}, f32[1,384,384]{2,1,0:T(8,128)}, s32[3,2]{0,1:T(2,128)S(1)}, f32[3,1,128,128]{3,2,1,0:T(8,128)}, s32[]{:T(128)}) %tuple.25), condition=%wide.while_cond, body=%wide.while_body.sunk | while | flops 2 | bytes 132205 | solution.py:22
  151.2 3.1 %bitcast_dynamic-update-slice_fusion.2 = f32[3,1,128,128]{3,2,1,0:T(8,128)} fusion(f32[3,1,128,128]{3,2,1,0:T(8,128)} %get-tuple-element.71, s32[]{:T(128)S(6)} %copy.31, f32[1,384,384]{2,1,0:T(8,128)} %get-tuple-element.74, s32[]{:T(128)} %bitcast.151, s32[]{:T(128)} %bitcast.152), kind=kLoop, calls=%fused_computation.clone.1 | loop fusion | bytes 132100 | tf_op jit(solution)/shard_map/vmap()/triangular_solve
  154.9 2.8 bitcast_dynamic-update-slice_fusion.2
  158.3 2.8 bitcast_dynamic-update-slice_fusion.2
  161.1 30.9 %custom-call.32 = f32[1,3,128,128]{2,3,1,0:T(8,128)} custom-call(f32[1,3,128,128]{3,2,1,0:T(8,128)} %bitcast.162), custom_call_target="InvertDiagBlocksLowerTriangular" | custom-call | tf_op jit(solution)/shard_map/vmap()/triangular_solve | solution.py:22
  192.0 1.2 fusion.33
  193.2 1.1 fusion.12
  194.3 1.1 fusion.38
  195.5 1.2 fusion.14
  196.7 1.1 fusion.40
  197.8 1.1 fusion.39
  198.9 1.2 convolution_subtract_fusion.1
  200.1 1.1 convolution_bitcast_fusion.2
  201.2 1.3 convolution_subtract_fusion
  202.5 1.1 convolution_bitcast_fusion.1
  203.7 0.7 divide_convert_fusion
  204.4 69.0 %all-gather.2.cloned.1.call-done = bf16[32,384,256]{2,1,0:T(8,128)(2,1)} async-done(((bf16[1,384,256]{2,1,0:T(8,128)(2,1)}), bf16[32,384,256]{2,1,0:T(8,128)(2,1)}) %all-gather.2.cloned.1.call-update) | async-done | bytes 6291472 | tf_op jit(solution)/shard_map/all_gather | solution.py:56
  273.5 6.0 %convert_bitcast_fusion = bf16[32,128,256]{1,2,0:T(8,128)(2,1)} fusion(bf16[32,384,256]{2,1,0:T(8,128)(2,1)} %all-gather.2.cloned.1.call-done, bf16[32,128,384]{2,1,0:T(8,128)(2,1)S(1)} %copy-done), kind=kOutput, calls=%fused_computation.6 | convolution fusion | flops 806354944 | bytes 11534336 | tf_op jit(solution)/shard_map/bgd,bde->bge/dot_general | solution.py:53
  279.5 4.1 %copy.19 = bf16[32,128,256]{2,1,0:T(8,128)(2,1)} copy(bf16[32,128,256]{1,2,0:T(8,128)(2,1)} %convert_bitcast_fusion) | data formatting | bytes 4194304 | tf_op jit(solution)/shard_map/convert_element_type | solution.py:58
  (32 shorter events, 3.9 us)
Async XLA Ops:
  6.5 8.0 %copy-start.2 = (s32[1,32]{1,0:T(1,128)S(1)}, s32[1,32]{1,0:T(1,128)}, u32[]{:S(2)}) copy-start(s32[1,32]{1,0:T(1,128)} %param.6) | copy-start | bytes 388
  6.5 78.8 %all-to-all-start = ((bf16[32,1,128,384]{3,2,1,0:T(8,128)(2,1)}), bf16[32,1,128,384]{3,2,1,0:T(8,128)(2,1)S(1)}, u32[]{:S(2)}, u32[]{:S(2)}) async-start(bf16[32,1,128,384]{3,2,1,0:T(8,128)(2,1)} %bitcast.154), calls=%async_computation | async-start | bytes 6291456 | tf_op jit(solution)/shard_map/all_to_all | solution.py:48
  13.8 259.6 %all-gather.2.cloned.1.call-start = ((), (), s32[]{:S(2)}) async-start(), calls=%async_computation.1 | async-start | bytes 6488064 | tf_op jit(solution)/shard_map/all_gather | solution.py:56
  150.5 122.9 %copy-start = (bf16[32,128,384]{2,1,0:T(8,128)(2,1)S(1)}, bf16[32,128,384]{2,1,0:T(8,128)(2,1)}, u32[]{:S(2)}) copy-start(bf16[32,128,384]{2,1,0:T(8,128)(2,1)} %param.4) | copy-start | bytes 9437188
  192.0 11.6 %copy-start.1 = (bf16[1,384,256]{2,1,0:T(8,128)(2,1)S(1)}, bf16[1,384,256]{2,1,0:T(8,128)(2,1)}, u32[]{:S(2)}) copy-start(bf16[1,384,256]{2,1,0:T(8,128)(2,1)} %param.5) | copy-start | bytes 589828
Sparse Core Ops, SparseCore 0:
  204.6 68.8 all-gather.1
where the time goes:
time: 291 us; the launch traced here: 290 us
  waiting for transfers between devices  139 us (48%)
  other arithmetic  91.1 us (31%)
  matrix products  21.2 us (7%)
  between operations  16.1 us (6%)
  local copies, waits for them, and re-layouts  16 us (5%)
  starting transfers between devices  7.34 us (3%)
    all_to_all x1, waiting for transfers between devices, body(): lax.all_to_all(outgoing, ('range', 'doppler'), split_axis=0, concat_axis=...  69.7 us
    all_gather x1, waiting for transfers between devices, body(): lax.all_gather(weights, ('range', 'doppler'), axis=0, tiled=True)  69 us
    another operation x10, other arithmetic, adapt(): factor = jnp.linalg.cholesky(covariance)  56.3 us
    another operation x3, other arithmetic, solve_one(): lax.linalg.triangular_solve(factor, inner, left_side=True, lower=True, tr...  31.8 us
    another operation x9, local copies, waits for them, and re-layouts  10.5 us
    all_to_all x1, starting transfers between devices, body(): lax.all_to_all(outgoing, ('range', 'doppler'), split_axis=0, concat_axis=...  7.3 us
    dot_general x1, matrix products, body(): jnp.einsum('bgd,bde->bge', snapshots, lax.all_gather(weights, ('range', '...  6.04 us
  transfers between devices with their start and end apart: 2, of which 2 were waited for; matrix products, arithmetic and copies ran while one was open for 0% of the time, Pallas kernels for 0%

commit v1 on v0

v1 whole, which is shorter than its diff:
```python
import jax
import jax.numpy as jnp
from jax import lax
from jax.experimental import pallas as pl
from jax.experimental.pallas import tpu as pltpu
from jax.sharding import Mesh
from jax.sharding import PartitionSpec as P

BLOCK = 128
LOADING = 0.1
EDGE = 128
STEP = 16
INNER = ("inner", "doppler")


def selection(train_list, train_count):
    block_total = train_list.shape[1]
    position = lax.broadcasted_iota(jnp.int32, (1, block_total, 1), 1)
    block_ids = lax.broadcasted_iota(jnp.int32, (1, 1, block_total), 2)
    matches = (train_list[:, :, None] == block_ids) & (position < train_count[:, None, None])
    return jnp.sum(matches.astype(jnp.int32), axis=1)


def partial_gram(blocks, chosen):
    masked = blocks * chosen.astype(blocks.dtype)[:, None, None]
    flat = (blocks.shape[0] * blocks.shape[1], blocks.shape[2])
    return lax.dot_general(
        masked.reshape(flat), blocks.reshape(flat), (((0,), (0,)), ((), ())),
        preferred_element_type=jnp.float32,
    )


def pack(gram):
    size = gram.shape[0]
    return jnp.concatenate([gram[i : i + 128, i:] for i in range(0, size, 128)], axis=1)


def fine(a, b, dims=(((1,), (0,)), ((), ()))):
    return lax.dot_general(
        a, b, dims, precision=lax.Precision.HIGHEST, preferred_element_type=jnp.float32
    )


def thirds(x):
    hi = x.astype(jnp.bfloat16)
    rest = x - hi.astype(jnp.float32)
    mid = rest.astype(jnp.bfloat16)
    low = (rest - mid.astype(jnp.float32)).astype(jnp.bfloat16)
    return hi, mid, low


def outer(a, b):
    ah, am, al = thirds(a)
    bh, bm, bl = thirds(b)
    left = jnp.concatenate([ah, ah, ah, am, am, al], axis=0)
    right = jnp.concatenate([bh, bm, bl, bh, bm, bh], axis=0)
    return lax.dot_general(
        left, right, (((0,), (0,)), ((), ())), preferred_element_type=jnp.float32
    )


def negative_inverse(strips):
    sub = lax.broadcasted_iota(jnp.int32, (STEP, EDGE), 0)
    lane = lax.broadcasted_iota(jnp.int32, (STEP, EDGE), 1)
    full = (STEP, EDGE)
    for p in range(EDGE // STEP):
        rows = strips[p]
        at = p * STEP
        inside = (lane >= at) & (lane < at + STEP)
        swept = jnp.where(inside, jnp.where(lane == sub + at, -1.0, 0.0), rows)
        cols = [jnp.broadcast_to(rows[:, at + i : at + i + 1], full) for i in range(STEP)]
        solved = swept
        for k in range(STEP):
            here = sub == k
            inv = 1.0 / jnp.broadcast_to(cols[k][k : k + 1], full)
            factor = jnp.where(here, 1.0, -cols[k])
            solved = jnp.where(here, 0.0, solved) + factor * (
                jnp.broadcast_to(solved[k : k + 1], full) * inv
            )
            for i in range(k + 1, STEP):
                cols[i] = jnp.where(here, 0.0, cols[i]) + factor * (
                    jnp.broadcast_to(cols[i][k : k + 1], full) * inv
                )
        change = outer(swept, solved)
        strips = [
            (jnp.zeros(full, jnp.float32) if q == p else jnp.where(inside, 0.0, strips[q]))
            - change[q * STEP : (q + 1) * STEP]
            for q in range(EDGE // STEP)
        ]
    return jnp.concatenate(strips, axis=0)


def solve_kernel(count_ref, own_ref, other_ref, steer_ref, out_ref, work):
    size = own_ref.shape[0]
    parts = size // EDGE
    inv_scale = 1.0 / (BLOCK * count_ref[0]).astype(jnp.float32)
    at = 0
    for i in range(parts):
        width = size - i * EDGE
        rows = pl.ds(i * EDGE, EDGE)
        strip = (own_ref[rows, pl.ds(i * EDGE, width)] + other_ref[:, pl.ds(at, width)]) * inv_scale
        r = lax.broadcasted_iota(jnp.int32, (EDGE, width), 0)
        c = lax.broadcasted_iota(jnp.int32, (EDGE, width), 1)
        work[rows, pl.ds(i * EDGE, width)] = strip + jnp.where(r == c, LOADING, 0.0)
        at += width
    beams = steer_ref.shape[1]
    work[:, pl.ds(size, beams)] = steer_ref[...].astype(jnp.float32)
    total = size + beams
    made = []
    for i in range(parts):
        rows = pl.ds(i * EDGE, EDGE)
        strips = [
            work[pl.ds(i * EDGE + q * STEP, STEP), pl.ds(i * EDGE, EDGE)]
            for q in range(EDGE // STEP)
        ]
        minus = negative_inverse(strips)
        right = work[rows, pl.ds((i + 1) * EDGE, total - (i + 1) * EDGE)]
        p = -fine(minus, right)
        made.append(p)
        for j in range(i + 1, parts):
            lhs = work[rows, pl.ds(j * EDGE, EDGE)]
            cut = p[:, (j - i - 1) * EDGE :]
            span = pl.ds(j * EDGE, total - j * EDGE)
            target = pl.ds(j * EDGE, EDGE)
            work[target, span] = work[target, span] - fine(lhs, cut, (((0,), (0,)), ((), ())))
    found = [None] * parts
    for i in reversed(range(parts)):
        x = made[i][:, (parts - i - 1) * EDGE :]
        for j in range(i + 1, parts):
            x = x - fine(made[i][:, (j - i - 1) * EDGE : (j - i) * EDGE], found[j])
        found[i] = x
    response = 0.0
    for i in range(parts):
        steer = steer_ref[pl.ds(i * EDGE, EDGE), :].astype(jnp.float32)
        response = response + jnp.sum(steer * found[i], axis=0, keepdims=True)
    for i in range(parts):
        out_ref[pl.ds(i * EDGE, EDGE), :] = (found[i] / response).astype(out_ref.dtype)


def make_weights(count, own, other, steering):
    size, beams = steering.shape
    vmem = pl.BlockSpec(memory_space=pltpu.VMEM)
    return pl.pallas_call(
        solve_kernel,
        out_shape=jax.ShapeDtypeStruct((size, beams), jnp.bfloat16),
        in_specs=[pl.BlockSpec(memory_space=pltpu.SMEM), vmem, vmem, vmem],
        out_specs=vmem,
        scratch_shapes=[pltpu.VMEM((size, size + beams), jnp.float32)],
        compiler_params=pltpu.CompilerParams(vmem_limit_bytes=32 * 1024 * 1024),
        cost_estimate=pl.CostEstimate(flops=10**9, bytes_accessed=2 * 10**6, transcendentals=0),
    )(count, own, other, steering)


def body(halves, snapshots, steering, train_list, train_count):
    bin_total, gate_rows, channels = snapshots.shape
    half = lax.axis_index("half")
    group = bin_total // halves
    peers = [(0, 1), (1, 0)]
    by_half = snapshots.reshape(halves, group, gate_rows, channels)

    def fetch(which):
        out = lax.dynamic_index_in_dim(by_half, which, 0, keepdims=False)
        return lax.all_to_all(out, INNER, split_axis=0, concat_axis=0, tiled=True)

    chosen_all = selection(train_list, train_count)[0].reshape(halves, group)
    own_chosen = lax.dynamic_index_in_dim(chosen_all, half, 0, keepdims=False)
    give_chosen = lax.dynamic_index_in_dim(chosen_all, 1 - half, 0, keepdims=False)
    other_chosen = lax.ppermute(give_chosen, "half", peers)

    other_blocks = fetch(1 - half)
    other_gram = partial_gram(other_blocks, other_chosen)
    arrived = lax.ppermute(pack(other_gram), "half", peers)
    own_blocks = fetch(half)
    own_gram = partial_gram(own_blocks, own_chosen)
    weights = make_weights(train_count, own_gram, arrived, steering[0])
    other_weights = lax.ppermute(weights, "half", peers)

    def beams(blocks, w):
        made = jnp.einsum("ngd,de->nge", blocks, w, preferred_element_type=jnp.float32)
        return lax.all_to_all(
            made.astype(jnp.bfloat16), INNER, split_axis=0, concat_axis=0, tiled=True
        )

    own_out = beams(own_blocks, weights)
    other_out = beams(other_blocks, other_weights)
    first = half == 0
    return jnp.concatenate(
        [jnp.where(first, own_out, other_out), jnp.where(first, other_out, own_out)], axis=0
    )


def solution(mesh):
    ranges, dopplers = mesh.devices.shape
    halves = 2
    cut = Mesh(
        mesh.devices.reshape(halves, ranges // halves, dopplers), ("half", "inner", "doppler")
    )
    every = ("half", "inner", "doppler")

    def run(*args):
        return body(halves, *args)

    return jax.shard_map(
        run,
        mesh=cut,
        in_specs=(P(None, every, None), P(every, None, None), P(every, None), P(every)),
        out_specs=P(None, every, None),
        check_vma=False,
    )
```

time: 291 us -> 142 us (0.49)
  other arithmetic: 91.1 us -> 1.79 us
  waiting for transfers between devices: 139 us -> 60.4 us
  blocking collectives: 0 us -> 27.9 us
  starting transfers between devices: 7.34 us -> 24.9 us
  between operations: 16.1 us -> 0.76 us
  Pallas kernels: 0 us -> 12.7 us
  matrix products: 21.2 us -> 8.82 us
  local copies, waits for them, and re-layouts: 16 us -> 4.54 us
    another operation x13 -> x0, other arithmetic: 88.1 us -> none  [the longest x10 56.3 us: adapt(): factor = jnp.linalg.cholesky(covariance)]
    all_gather x1 -> x0, waiting for transfers between devices: 69 us -> none  [body(): lax.all_gather(weights, ('range', 'doppler'), axis=0, tiled=True)]
    all_to_all x1 -> x3, waiting for transfers between devices: 69.7 us -> 18.4 us  [the longest x2 18.2 us: beams(): lax.all_to_all(made.astype(jnp.bfloat16), INNER, split_axis=0, concat_axi...]
    ppermute x0 -> x3, waiting for transfers between devices: none -> 42 us  [the longest x1 14.6 us: body(): other_chosen = lax.ppermute(give_chosen, 'half', peers)]
    all_to_all x0 -> x1, blocking collectives: none -> 27.9 us  [fetch(): return lax.all_to_all(out, INNER, split_axis=0, concat_axis=0, tiled=True)]
    pallas_call x0 -> x1, Pallas kernels: none -> 12.7 us  [make_weights(): pl.pallas_call(solve_kernel, out_shape=jax.ShapeDtypeStruct((size, beams)...]
    another operation x14 -> x0, matrix products: 12.5 us -> none  [the longest x5 5.76 us: solve_one(): lax.linalg.triangular_solve(factor, rhs_block, left_side=True, lower=True)]
    another operation x13 -> x1, local copies, waits for them, and re-layouts: 10.6 us -> 0.08 us  [body(): chosen_all = selection(train_list, train_count)[0].reshape(halves, group)]
  transfers between devices with their start and end apart: 2 -> 6, of which waited for: 2 -> 6; matrix products, arithmetic and copies ran while one was open for 0% -> 4% of each run, Pallas kernels for 0% -> 0%
where the time goes in v1:
time: 142 us
  waiting for transfers between devices  60.4 us (43%)
  blocking collectives  27.9 us (20%)
  starting transfers between devices  24.9 us (18%)
  Pallas kernels  12.7 us (9%)
  matrix products  8.82 us (6%)
  local copies, waits for them, and re-layouts  4.54 us (3%)
  other arithmetic  1.79 us (1%)
    all_to_all x1, blocking collectives, fetch(): return lax.all_to_all(out, INNER, split_axis=0, concat_axis=0, tiled=True)  27.9 us
    all_to_all x2, waiting for transfers between devices, beams(): lax.all_to_all(made.astype(jnp.bfloat16), INNER, split_axis=0, concat_axi...  18.2 us
    ppermute x1, waiting for transfers between devices, body(): other_chosen = lax.ppermute(give_chosen, 'half', peers)  14.6 us
    ppermute x1, waiting for transfers between devices, body(): arrived = lax.ppermute(pack(other_gram), 'half', peers)  14 us
    ppermute x1, waiting for transfers between devices, body(): other_weights = lax.ppermute(weights, 'half', peers)  13.3 us
    pallas_call x1, Pallas kernels, make_weights(): pl.pallas_call(solve_kernel, out_shape=jax.ShapeDtypeStruct((size, beams)...  12.7 us
    all_to_all x2, starting transfers between devices, beams(): lax.all_to_all(made.astype(jnp.bfloat16), INNER, split_axis=0, concat_axi...  11.1 us
    dot_general x2, matrix products, beams(): jnp.einsum('ngd,de->nge', blocks, w, preferred_element_type=jnp.float32)  4.8 us
  transfers between devices with their start and end apart: 6, of which 6 were waited for; matrix products, arithmetic and copies ran while one was open for 4% of the time, Pallas kernels for 0%

profile of v1, /device:TPU:0, one launch (start us, length us, event | category | flops | bytes accessed | tf_op | source)
XLA Modules:
  0.0 141.7 jit_solution(8722341012496196230)
XLA Ops:
  0.0 3.5 %dynamic-slice_bitcast_fusion = (bf16[16,128,384]{2,1,0:T(8,128)(2,1)}, bf16[1,16,128,384]{3,2,1,0:T(8,128)(2,1)S(1)}) fusion(bf16[2,16,128,384]{3,2,1,0:T(8,128)(2,1)} %bitcast.31, s32[]{:T(128)S(6)} %select_n.23, s32[]{:T(128)S(6)} %select_n.24), kind=kLoop, calls=%fused_computation.5 | loop fusion | bytes 6291464 | tf_op jit(solution)/shard_map/jit(dynamic_index_in_dim)/squeeze | solution.py:162
  3.5 0.9 copy.13
  4.4 27.9 %all_to_all.20 = bf16[16,128,384]{1,2,0:T(8,128)(2,1)S(1)} all-to-all(bf16[16,128,384]{1,2,0:T(8,128)(2,1)S(1)} %bitcast.30), channel_id=1, replica_groups=mesh['half'=2,'inner'=4,'doppler'=4] {'inner','doppler'}, dimensions={0} | all-to-all | bytes 3145728 | tf_op jit(solution)/shard_map/all_to_all | solution.py:163
  32.3 0.0 copy-start.1
  32.3 4.5 %all-to-all-start = ((bf16[16,128,384]{2,1,0:T(8,128)(2,1)}), bf16[16,128,384]{2,1,0:T(8,128)(2,1)}, u32[]{:S(2)}, u32[]{:S(2)}) async-start(bf16[16,128,384]{2,1,0:T(8,128)(2,1)} %get-tuple-element.5), calls=%async_computation | async-start | bytes 3145728 | tf_op jit(solution)/shard_map/all_to_all | solution.py:163
  37.5 0.0 copy-done.1
  37.5 0.1 convert_reduce_fusion
  37.6 0.1 reshape_squeeze.3
  37.7 2.6 %collective-permute-start = (s32[16]{0:T(128)S(1)}, s32[16]{0:T(128)S(1)}, u32[]{:S(2)}, u32[]{:S(2)}) collective-permute-start(s32[16]{0:T(128)S(1)} %get-tuple-element.9), channel_id=1, source_target_pairs={{0,16},{16,0},{1,17},{17,1},{2,18},{18,2},{3,19},{19,3},{4,20},{20... | collective-permute-start | bytes 200 | tf_op jit(solution)/shard_map/ppermute | solution.py:168
  40.3 14.6 %collective-permute-done = s32[16]{0:T(128)S(1)} collective-permute-done((s32[16]{0:T(128)S(1)}, s32[16]{0:T(128)S(1)}, u32[]{:S(2)}, u32[]{:S(2)}) %collective-permute-start) | collective-permute-done | bytes 96 | tf_op jit(solution)/shard_map/ppermute | solution.py:168
  55.0 1.0 fusion.7
  56.1 3.3 %collective-permute-start.1 = (f32[128,768]{1,0:T(8,128)S(1)}, f32[128,768]{1,0:T(8,128)S(1)}, u32[]{:S(2)}, u32[]{:S(2)}) collective-permute-start(f32[128,768]{1,0:T(8,128)S(1)} %pad_maximum_fusion.1), channel_id=1, source_target_pairs={{0,16},{16,0},{1,17},{17,1},{2,18},{18,2},{3,19},{19,3},{4,20},{20... | collective-permute-start | bytes 1179656 | tf_op jit(solution)/shard_map/ppermute | solution.py:172
  59.4 0.2 all-to-all-done
  59.6 0.0 copy-start
  59.6 3.0 %fusion.4.own_ref = f32[384,384]{1,0:T(8,128)S(1)} fusion(bf16[16,128,384]{2,1,0:T(8,128)(2,1)} %all-to-all-done, bf16[16]{0:T(256)(128)(2,1)S(1)} %get-tuple-element.10), kind=kOutput, calls=%fused_computation.8 | convolution fusion | flops 604766208 | bytes 2162720 | tf_op jit(solution)/shard_map/dot_general | solution.py:27
  62.6 14.0 %collective-permute-done.1.other_ref = f32[128,768]{1,0:T(8,128)S(1)} collective-permute-done((f32[128,768]{1,0:T(8,128)S(1)}, f32[128,768]{1,0:T(8,128)S(1)}, u32[]{:S(2)}, u32[]{:S(2)}) %collective-permute-start.1) | collective-permute-done | bytes 393248 | tf_op jit(solution)/shard_map/ppermute | solution.py:172
  76.6 0.0 copy-done
  76.6 12.7 %shard_map.49 = bf16[384,256]{1,0:T(8,128)(2,1)S(1)} custom-call(s32[1]{0:T(128)} %copy.26.count_ref, f32[384,384]{1,0:T(8,128)S(1)} %fusion.4.own_ref, f32[128,768]{1,0:T(8,128)S(1)} %collective-permute-done.1.other_ref, bf16[384,256]{1,0:T(8,128)(2,1)S(1)} %bitcast.29), custom_call_target="tpu_custom_call" | custom-call | flops 1000000000 | bytes 2000000 | tf_op jit(solution)/shard_map/pallas_call | solution.py:143
  89.3 3.1 %convolution_convert_fusion.1 = bf16[16,128,256]{2,1,0:T(8,128)(2,1)} fusion(bf16[16,128,384]{2,1,0:T(8,128)(2,1)} %all-to-all-done, bf16[384,256]{1,0:T(8,128)(2,1)S(1)} %shard_map.49), kind=kOutput, calls=%fused_computation.7 | convolution fusion | flops 403177472 | bytes 2818048 | tf_op jit(solution)/shard_map/ngd,de->nge/dot_general | solution.py:179
  92.4 4.7 %all-to-all-start.2 = ((bf16[16,128,256]{2,1,0:T(8,128)(2,1)}), bf16[16,128,256]{2,1,0:T(8,128)(2,1)S(1)}, u32[]{:S(2)}, u32[]{:S(2)}) async-start(bf16[16,128,256]{2,1,0:T(8,128)(2,1)} %convolution_convert_fusion.1), calls=%async_computation.2 | async-start | bytes 2097152 | tf_op jit(solution)/shard_map/all_to_all | solution.py:180
  97.1 3.3 %collective-permute-start.2 = (bf16[384,256]{1,0:T(8,128)(2,1)S(1)}, bf16[384,256]{1,0:T(8,128)(2,1)S(1)}, u32[]{:S(2)}, u32[]{:S(2)}) collective-permute-start(bf16[384,256]{1,0:T(8,128)(2,1)S(1)} %shard_map.49), channel_id=1, source_target_pairs={{0,16},{16,0},{1,17},{17,1},{2,18},{18,2},{3,19},{19,3},{4,20},{20... | collective-permute-start | bytes 589832 | tf_op jit(solution)/shard_map/ppermute | solution.py:176
  100.4 13.3 %collective-permute-done.2 = bf16[384,256]{1,0:T(8,128)(2,1)S(1)} collective-permute-done((bf16[384,256]{1,0:T(8,128)(2,1)S(1)}, bf16[384,256]{1,0:T(8,128)(2,1)S(1)}, u32[]{:S(2)}, u32[]{:S(2)}) %collective-permute-start.2) | collective-permute-done | bytes 196640 | tf_op jit(solution)/shard_map/ppermute | solution.py:176
  113.8 1.7 %convolution_convert_fusion = bf16[16,128,256]{2,1,0:T(8,128)(2,1)} fusion(bf16[16,128,384]{1,2,0:T(8,128)(2,1)S(1)} %all_to_all.20, bf16[384,256]{1,0:T(8,128)(2,1)S(1)} %collective-permute-done.2), kind=kOutput, calls=%fused_computation.6 | convolution fusion | flops 403177472 | bytes 2818048 | tf_op jit(solution)/shard_map/ngd,de->nge/dot_general | solution.py:179
  115.5 2.0 %all-to-all-done.2 = bf16[16,128,256]{2,1,0:T(8,128)(2,1)S(1)} async-done(((bf16[16,128,256]{2,1,0:T(8,128)(2,1)}), bf16[16,128,256]{2,1,0:T(8,128)(2,1)S(1)}, u32[]{:S(2)}, u32[]{:S(2)}) %all-to-all-start.2) | async-done | bytes 1048608 | tf_op jit(solution)/shard_map/all_to_all | solution.py:180
  117.5 6.3 %all-to-all-start.3 = ((bf16[16,128,256]{2,1,0:T(8,128)(2,1)}), bf16[16,128,256]{2,1,0:T(8,128)(2,1)S(1)}, u32[]{:S(2)}, u32[]{:S(2)}) async-start(bf16[16,128,256]{2,1,0:T(8,128)(2,1)} %convolution_convert_fusion), calls=%async_computation.3 | async-start | bytes 2097152 | tf_op jit(solution)/shard_map/all_to_all | solution.py:180
  123.9 16.2 %all-to-all-done.3 = bf16[16,128,256]{2,1,0:T(8,128)(2,1)S(1)} async-done(((bf16[16,128,256]{2,1,0:T(8,128)(2,1)}), bf16[16,128,256]{2,1,0:T(8,128)(2,1)S(1)}, u32[]{:S(2)}, u32[]{:S(2)}) %all-to-all-start.3) | async-done | bytes 1048608 | tf_op jit(solution)/shard_map/all_to_all | solution.py:180
  140.1 0.1 broadcast_select_fusion.1
  140.2 1.5 %pad_maximum_fusion = bf16[32,128,256]{2,1,0:T(8,128)(2,1)} fusion(bf16[16,128,256]{2,1,0:T(8,128)(2,1)S(1)} %get-tuple-element.8, bf16[16,128,256]{2,1,0:T(8,128)(2,1)S(1)} %get-tuple-element.7), kind=kLoop, calls=%fused_computation.4 | loop fusion | flops 1048576 | bytes 4194304 | tf_op jit(solution)/shard_map/concatenate | solution.py:187
  (7 shorter events, 0.1 us)
Async XLA Ops:
  32.3 5.2 %copy-start.1 = (s32[1,32]{1,0:T(1,128)S(1)}, s32[1,32]{1,0:T(1,128)}, u32[]{:S(2)}) copy-start(s32[1,32]{1,0:T(1,128)} %param.6) | copy-start | bytes 388
  32.3 27.3 %all-to-all-start = ((bf16[16,128,384]{2,1,0:T(8,128)(2,1)}), bf16[16,128,384]{2,1,0:T(8,128)(2,1)}, u32[]{:S(2)}, u32[]{:S(2)}) async-start(bf16[16,128,384]{2,1,0:T(8,128)(2,1)} %get-tuple-element.5), calls=%async_computation | async-start | bytes 3145728 | tf_op jit(solution)/shard_map/all_to_all | solution.py:163
  37.7 17.3 %collective-permute-start = (s32[16]{0:T(128)S(1)}, s32[16]{0:T(128)S(1)}, u32[]{:S(2)}, u32[]{:S(2)}) collective-permute-start(s32[16]{0:T(128)S(1)} %get-tuple-element.9), channel_id=1, source_target_pairs={{0,16},{16,0},{1,17},{17,1},{2,18},{18,2},{3,19},{19,3},{4,20},{20... | collective-permute-start | bytes 200 | tf_op jit(solution)/shard_map/ppermute | solution.py:168
  56.1 20.5 %collective-permute-start.1 = (f32[128,768]{1,0:T(8,128)S(1)}, f32[128,768]{1,0:T(8,128)S(1)}, u32[]{:S(2)}, u32[]{:S(2)}) collective-permute-start(f32[128,768]{1,0:T(8,128)S(1)} %pad_maximum_fusion.1), channel_id=1, source_target_pairs={{0,16},{16,0},{1,17},{17,1},{2,18},{18,2},{3,19},{19,3},{4,20},{20... | collective-permute-start | bytes 1179656 | tf_op jit(solution)/shard_map/ppermute | solution.py:172
  59.6 17.0 %copy-start = (bf16[1,384,256]{2,1,0:T(8,128)(2,1)S(1)}, bf16[1,384,256]{2,1,0:T(8,128)(2,1)}, u32[]{:S(2)}) copy-start(bf16[1,384,256]{2,1,0:T(8,128)(2,1)} %param.5) | copy-start | bytes 589828
  92.4 25.1 %all-to-all-start.2 = ((bf16[16,128,256]{2,1,0:T(8,128)(2,1)}), bf16[16,128,256]{2,1,0:T(8,128)(2,1)S(1)}, u32[]{:S(2)}, u32[]{:S(2)}) async-start(bf16[16,128,256]{2,1,0:T(8,128)(2,1)} %convolution_convert_fusion.1), calls=%async_computation.2 | async-start | bytes 2097152 | tf_op jit(solution)/shard_map/all_to_all | solution.py:180
  97.1 16.6 %collective-permute-start.2 = (bf16[384,256]{1,0:T(8,128)(2,1)S(1)}, bf16[384,256]{1,0:T(8,128)(2,1)S(1)}, u32[]{:S(2)}, u32[]{:S(2)}) collective-permute-start(bf16[384,256]{1,0:T(8,128)(2,1)S(1)} %shard_map.49), channel_id=1, source_target_pairs={{0,16},{16,0},{1,17},{17,1},{2,18},{18,2},{3,19},{19,3},{4,20},{20... | collective-permute-start | bytes 589832 | tf_op jit(solution)/shard_map/ppermute | solution.py:176
  117.5 22.5 %all-to-all-start.3 = ((bf16[16,128,256]{2,1,0:T(8,128)(2,1)}), bf16[16,128,256]{2,1,0:T(8,128)(2,1)S(1)}, u32[]{:S(2)}, u32[]{:S(2)}) async-start(bf16[16,128,256]{2,1,0:T(8,128)(2,1)} %convolution_convert_fusion), calls=%async_computation.3 | async-start | bytes 2097152 | tf_op jit(solution)/shard_map/all_to_all | solution.py:180

commit v2 on v1

v2 whole, which is shorter than its diff:
```python
import jax
import jax.numpy as jnp
from jax import lax
from jax.experimental import pallas as pl
from jax.experimental.pallas import tpu as pltpu
from jax.sharding import Mesh
from jax.sharding import PartitionSpec as P

BLOCK = 128
LOADING = 0.1
EDGE = 128
STEP = 16
INNER = ("inner", "doppler")


def gram_kernel(base_ref, list_ref, count_ref, blocks_ref, out_ref, chosen):
    step = pl.program_id(0)
    count, _, rows, size = blocks_ref.shape

    @pl.when(step == 0)
    def _():
        for p in range(list_ref.shape[1]):
            chosen[list_ref[0, p]] = (p < count_ref[0]).astype(jnp.int32)

    first = base_ref[0] + step * count
    every = [blocks_ref[n, 0] for n in range(count)]
    kept = [
        jnp.where(chosen[first + n] > 0, x, jnp.zeros_like(x)) for n, x in enumerate(every)
    ]
    every = jnp.concatenate(every, axis=0)
    kept = jnp.concatenate(kept, axis=0)
    def product(lo, hi):
        return lax.dot_general(
            kept[:, lo:hi], every[:, lo:], (((0,), (0,)), ((), ())),
            preferred_element_type=jnp.float32,
        )

    at = 0
    for lo in range(0, size, 2 * EDGE):
        hi = min(lo + 2 * EDGE, size)
        part = product(lo, hi)
        for i in range(lo, hi, EDGE):
            width = size - i
            out_ref[:, pl.ds(at, width)] = part[i - lo : i - lo + EDGE, i - lo :]
            at += width


def partial_gram(base, lists, counts, blocks, which, chunks=1):
    group, _, rows, size = blocks.shape
    parts = size // EDGE
    smem = pl.BlockSpec(memory_space=pltpu.SMEM)
    wide = EDGE * parts * (parts + 1) // 2
    return pl.pallas_call(
        gram_kernel,
        out_shape=jax.ShapeDtypeStruct((EDGE, wide), jnp.float32),
        grid=(chunks,),
        in_specs=[smem, smem, smem, pl.BlockSpec((group // chunks, 1, rows, size), lambda i: (i, which, 0, 0))],
        out_specs=pl.BlockSpec((EDGE, wide), lambda i: (0, 0)),
        scratch_shapes=[pltpu.SMEM((lists.shape[1],), jnp.int32)],
        compiler_params=pltpu.CompilerParams(vmem_limit_bytes=16 * 1024 * 1024),
        cost_estimate=pl.CostEstimate(
            flops=2 * group * rows * size * size, bytes_accessed=2 * group * rows * size, transcendentals=0
        ),
    )(base, lists, counts, blocks)


def fine(a, b, dims=(((1,), (0,)), ((), ()))):
    return lax.dot_general(
        a, b, dims, precision=lax.Precision.HIGHEST, preferred_element_type=jnp.float32
    )


def thirds(x):
    hi = x.astype(jnp.bfloat16)
    rest = x - hi.astype(jnp.float32)
    mid = rest.astype(jnp.bfloat16)
    low = (rest - mid.astype(jnp.float32)).astype(jnp.bfloat16)
    return hi, mid, low


def outer(a, b):
    ah, am, al = thirds(a)
    bh, bm, bl = thirds(b)
    left = jnp.concatenate([ah, ah, ah, am, am, al], axis=0)
    right = jnp.concatenate([bh, bm, bl, bh, bm, bh], axis=0)
    return lax.dot_general(
        left, right, (((0,), (0,)), ((), ())), preferred_element_type=jnp.float32
    )


def eliminate(rows, cols):
    full = (STEP, EDGE)
    sub = lax.broadcasted_iota(jnp.int32, full, 0)

    def row(x, k):
        return jnp.broadcast_to(x[k : k + 1], full)

    cols = list(cols)
    for k in range(0, STEP, 2):
        one, two = sub == k, sub == k + 1
        here = one | two
        a, b, c = row(cols[k], k), row(cols[k + 1], k), row(cols[k + 1], k + 1)
        inv = 1.0 / (a * c - b * b)
        first = jnp.where(one, 1.0, jnp.where(two, 0.0, -cols[k]))
        second = jnp.where(two, 1.0, jnp.where(one, 0.0, -cols[k + 1]))

        def step(x):
            r, s = row(x, k), row(x, k + 1)
            up = (c * r - b * s) * inv
            down = (a * s - b * r) * inv
            return (jnp.where(here, 0.0, x) + first * up) + second * down

        for i in range(k + 2, STEP):
            cols[i] = step(cols[i])
        rows = step(rows)
    return rows


def negative_inverse(strips):
    full = (STEP, EDGE)
    panels = EDGE // STEP
    sub = lax.broadcasted_iota(jnp.int32, full, 0)
    lane = lax.broadcasted_iota(jnp.int32, full, 1)

    def spread(x, at):
        return [jnp.broadcast_to(x[:, at + i : at + i + 1], full) for i in range(STEP)]

    rows = strips[0]
    for p in range(panels):
        at = p * STEP
        inside = (lane >= at) & (lane < at + STEP)
        swept = jnp.where(inside, jnp.where(lane == sub + at, -1.0, 0.0), rows)
        weights = spread(strips[p + 1], at) if p + 1 < panels else None
        solved = eliminate(swept, spread(rows, at))
        if weights is not None:
            terms = [w * jnp.broadcast_to(solved[k : k + 1], full) for k, w in enumerate(weights)]
            while len(terms) > 1:
                terms = [x + y for x, y in zip(terms[::2], terms[1::2])]
            rows = jnp.where(inside, 0.0, strips[p + 1]) - terms[0]
        change = outer(swept, solved)
        strips = [
            rows
            if q == p + 1
            else (jnp.zeros(full, jnp.float32) if q == p else jnp.where(inside, 0.0, strips[q]))
            - change[q * STEP : (q + 1) * STEP]
            for q in range(panels)
        ]
    return jnp.concatenate(strips, axis=0)


def solve_kernel(count_ref, own_ref, other_ref, steer_ref, out_ref, work):
    size = steer_ref.shape[0]
    parts = size // EDGE
    inv_scale = 1.0 / (BLOCK * count_ref[0]).astype(jnp.float32)
    at = 0
    for i in range(parts):
        width = size - i * EDGE
        rows = pl.ds(i * EDGE, EDGE)
        strip = (own_ref[:, pl.ds(at, width)] + other_ref[:, pl.ds(at, width)]) * inv_scale
        r = lax.broadcasted_iota(jnp.int32, (EDGE, width), 0)
        c = lax.broadcasted_iota(jnp.int32, (EDGE, width), 1)
        work[rows, pl.ds(i * EDGE, width)] = strip + jnp.where(r == c, LOADING, 0.0)
        at += width
    beams = steer_ref.shape[1]
    work[:, pl.ds(size, beams)] = steer_ref[...].astype(jnp.float32)
    total = size + beams
    made = []
    for i in range(parts):
        rows = pl.ds(i * EDGE, EDGE)
        strips = [
            work[pl.ds(i * EDGE + q * STEP, STEP), pl.ds(i * EDGE, EDGE)]
            for q in range(EDGE // STEP)
        ]
        minus = negative_inverse(strips)
        right = work[rows, pl.ds((i + 1) * EDGE, total - (i + 1) * EDGE)]
        p = -fine(minus, right)
        made.append(p)
        for j in range(i + 1, parts):
            lhs = work[rows, pl.ds(j * EDGE, EDGE)]
            cut = p[:, (j - i - 1) * EDGE :]
            span = pl.ds(j * EDGE, total - j * EDGE)
            target = pl.ds(j * EDGE, EDGE)
            work[target, span] = work[target, span] - fine(lhs, cut, (((0,), (0,)), ((), ())))
    found = [None] * parts
    for i in reversed(range(parts)):
        x = made[i][:, (parts - i - 1) * EDGE :]
        for j in range(i + 1, parts):
            x = x - fine(made[i][:, (j - i - 1) * EDGE : (j - i) * EDGE], found[j])
        found[i] = x
    response = 0.0
    for i in range(parts):
        steer = steer_ref[pl.ds(i * EDGE, EDGE), :].astype(jnp.float32)
        response = response + jnp.sum(steer * found[i], axis=0, keepdims=True)
    for i in range(parts):
        out_ref[pl.ds(i * EDGE, EDGE), :] = (found[i] / response).astype(out_ref.dtype)


def make_weights(count, own, other, steering):
    size, beams = steering.shape
    vmem = pl.BlockSpec(memory_space=pltpu.VMEM)
    return pl.pallas_call(
        solve_kernel,
        out_shape=jax.ShapeDtypeStruct((size, beams), jnp.bfloat16),
        in_specs=[pl.BlockSpec(memory_space=pltpu.SMEM), vmem, vmem, vmem],
        out_specs=vmem,
        scratch_shapes=[pltpu.VMEM((size, size + beams), jnp.float32)],
        compiler_params=pltpu.CompilerParams(vmem_limit_bytes=16 * 1024 * 1024),
        cost_estimate=pl.CostEstimate(flops=10**9, bytes_accessed=2 * 10**6, transcendentals=0),
    )(count, own, other, steering)


def split_kernel(which_ref, x_ref, out_ref):
    out_ref[:, 0] = x_ref[0]


def split(x, which):
    halves, count, rows, wide = x.shape
    chunk = count // 4
    return pl.pallas_call(
        split_kernel,
        out_shape=jax.ShapeDtypeStruct((count, halves, rows, wide), x.dtype),
        grid_spec=pltpu.PrefetchScalarGridSpec(
            num_scalar_prefetch=1,
            grid=(halves, 4),
            in_specs=[pl.BlockSpec((1, chunk, rows, wide), lambda s, i, which: (which[s], i, 0, 0))],
            out_specs=pl.BlockSpec((chunk, 1, rows, wide), lambda s, i, which: (i, s, 0, 0)),
        ),
        compiler_params=pltpu.CompilerParams(vmem_limit_bytes=16 * 1024 * 1024),
        cost_estimate=pl.CostEstimate(flops=0, bytes_accessed=2 * x.size, transcendentals=0),
    )(which, x)


def body(halves, snapshots, steering, train_list, train_count):
    bin_total, gate_rows, channels = snapshots.shape
    half = lax.axis_index("half")
    group = bin_total // halves
    peers = [(0, 1), (1, 0)]
    which = jnp.stack([half, 1 - half]).astype(jnp.int32)
    base = (half * group).astype(jnp.int32)[None]

    def exchange(x):
        return lax.all_to_all(x, INNER, split_axis=0, concat_axis=0, tiled=True)

    other_list = lax.ppermute(train_list, "half", peers)
    other_count = lax.ppermute(train_count, "half", peers)
    outgoing = split(snapshots.reshape(halves, group, gate_rows, channels), which)
    outgoing, other_list, other_count, base, which = lax.optimization_barrier(
        (outgoing, other_list, other_count, base, which)
    )
    blocks = exchange(outgoing)

    other_gram = partial_gram(base, other_list, other_count, blocks, 1)
    arrived = lax.ppermute(other_gram, "half", peers)
    own_gram = partial_gram(base, train_list, train_count, blocks, 0)
    weights = make_weights(train_count, own_gram, arrived, steering[0])
    other_weights = lax.ppermute(weights, "half", peers)

    def beams(x, w):
        made = jnp.einsum("ngd,de->nge", x, w, preferred_element_type=jnp.float32)
        return made.astype(jnp.bfloat16)

    made = jnp.stack([beams(blocks[:, 0], weights), beams(blocks[:, 1], other_weights)], axis=1)
    made, here, there = lax.optimization_barrier((made, half, 1 - half))
    out = jnp.moveaxis(exchange(made), 1, 0)
    sets = [
        lax.dynamic_index_in_dim(out, at, 0, keepdims=False, allow_negative_indices=False)
        for at in (here, there)
    ]
    return jnp.concatenate(sets, axis=0)


def solution(mesh):
    ranges, dopplers = mesh.devices.shape
    halves = 2
    cut = Mesh(
        mesh.devices.reshape(halves, ranges // halves, dopplers), ("half", "inner", "doppler")
    )
    every = ("half", "inner", "doppler")

    def run(*args):
        return body(halves, *args)

    return jax.shard_map(
        run,
        mesh=cut,
        in_specs=(P(None, every, None), P(every, None, None), P(every, None), P(every)),
        out_specs=P(None, every, None),
        check_vma=False,
    )
```

time: 142 us -> 128 us (0.901)
  blocking collectives: 27.9 us -> 73.7 us
  waiting for transfers between devices: 60.4 us -> 26.3 us
  starting transfers between devices: 24.9 us -> 5.91 us
  matrix products: 8.82 us -> 1.4 us
  Pallas kernels: 12.7 us -> 16.1 us
  local copies, waits for them, and re-layouts: 4.54 us -> 2.24 us
    all_to_all x1 -> x2, blocking collectives: 27.9 us -> 73.7 us  [exchange(): return lax.all_to_all(x, INNER, split_axis=0, concat_axis=0, tiled=True)]
    all_to_all x3 -> x0, waiting for transfers between devices: 18.4 us -> none  [the longest x2 18.2 us: beams(): lax.all_to_all(made.astype(jnp.bfloat16), INNER, split_axis=0, concat_axi...]
    all_to_all x3 -> x0, starting transfers between devices: 15.6 us -> none  [the longest x2 11.1 us: beams(): lax.all_to_all(made.astype(jnp.bfloat16), INNER, split_axis=0, concat_axi...]
    ppermute x2 -> x3, waiting for transfers between devices: 28.7 us -> 17 us  [the longest x1 15.8 us: body(): arrived = lax.ppermute(other_gram, 'half', peers)]
    dot_general x4 -> x2, matrix products: 8.82 us -> 1.4 us  [beams(): made = jnp.einsum('ngd,de->nge', x, w, preferred_element_type=jnp.float32)]
    pallas_call x0 -> x3, Pallas kernels: none -> 4.98 us  [the longest x2 3.67 us: partial_gram(): pl.pallas_call(gram_kernel, out_shape=jax.ShapeDtypeStruct((EDGE, wide),...]
    ppermute x1, waiting for transfers between devices: 13.3 us -> 9.3 us  [body(): other_weights = lax.ppermute(weights, 'half', peers)]
    squeeze x1, local copies, waits for them, and re-layouts: 3.47 us -> 0.14 us  [body(): lax.dynamic_index_in_dim(out, at, 0, keepdims=False, allow_negative_indic...]
  transfers between devices with their start and end apart: 6 -> 4, of which waited for: 6 -> 3; matrix products, arithmetic and copies ran while one was open for 4% -> 1% of each run, Pallas kernels for 0% -> 2%
where the time goes in v2:
time: 128 us
  blocking collectives  73.7 us (58%)
  waiting for transfers between devices  26.3 us (21%)
  Pallas kernels  16.1 us (13%)
  starting transfers between devices  5.91 us (5%)
  local copies, waits for them, and re-layouts  2.24 us (2%)
  other arithmetic  1.77 us (1%)
  matrix products  1.4 us (1%)
    all_to_all x2, blocking collectives, exchange(): return lax.all_to_all(x, INNER, split_axis=0, concat_axis=0, tiled=True)  73.7 us
    ppermute x1, waiting for transfers between devices, body(): arrived = lax.ppermute(other_gram, 'half', peers)  15.8 us
    pallas_call x1, Pallas kernels, make_weights(): pl.pallas_call(solve_kernel, out_shape=jax.ShapeDtypeStruct((size, beams)...  11.1 us
    ppermute x1, waiting for transfers between devices, body(): other_weights = lax.ppermute(weights, 'half', peers)  9.3 us
    ppermute x1, starting transfers between devices, body(): other_list = lax.ppermute(train_list, 'half', peers)  4.04 us
    pallas_call x2, Pallas kernels, partial_gram(): pl.pallas_call(gram_kernel, out_shape=jax.ShapeDtypeStruct((EDGE, wide),...  3.67 us
  transfers between devices with their start and end apart: 4, of which 3 were waited for; matrix products, arithmetic and copies ran while one was open for 1% of the time, Pallas kernels for 2%

profile of v2, /device:TPU:0, one launch (start us, length us, event | category | flops | bytes accessed | tf_op | source)
XLA Modules:
  0.0 128.2 jit_solution(2677012181646649687)
XLA Ops:
  0.0 4.0 %collective-permute-start = (s32[1,32]{1,0:T(1,128)}, s32[1,32]{1,0:T(1,128)S(1)}, u32[]{:S(2)}, u32[]{:S(2)}) collective-permute-start(s32[1,32]{1,0:T(1,128)} %list_ref.1), channel_id=1, source_target_pairs={{0,16},{16,0},{1,17},{17,1},{2,18},{18,2},{3,19},{19,3},{4,20},{20... | collective-permute-start | bytes 392 | tf_op jit(solution)/shard_map/ppermute | solution.py:244
  4.0 0.0 collective-permute-start.1
  4.1 0.1 pad_add_fusion.which_ref
  4.1 0.0 copy-start
  4.1 1.9 %copy-done = bf16[32,128,384]{2,1,0:T(8,128)(2,1)S(1)} copy-done((bf16[32,128,384]{2,1,0:T(8,128)(2,1)S(1)}, bf16[32,128,384]{2,1,0:T(8,128)(2,1)}, u32[]{:S(2)}) %copy-start) | copy-done | bytes 3145752
  6.0 1.3 %shard_map.46 = bf16[16,2,128,384]{3,2,1,0:T(8,128)(2,1)S(1)} custom-call(s32[2]{0:T(128)S(1)} %pad_add_fusion.which_ref, bf16[2,16,128,384]{3,2,1,0:T(8,128)(2,1)S(1)} %bitcast.33), custom_call_target="tpu_custom_call" | custom-call | bytes 3145728 | tf_op jit(solution)/shard_map/pallas_call | solution.py:219
  7.4 1.2 collective-permute-done.1.count_ref
  8.6 0.0 collective-permute-done.list_ref
  8.6 43.3 %all_to_all.10.blocks_ref = bf16[16,2,128,384]{3,2,1,0:T(8,128)(2,1)S(1)} all-to-all(bf16[16,2,128,384]{3,2,1,0:T(8,128)(2,1)S(1)} %shard_map.46), channel_id=1, replica_groups=mesh['half'=2,'inner'=4,'doppler'=4] {'inner','doppler'}, dimensions={0} | all-to-all | bytes 6291456 | tf_op jit(solution)/shard_map/all_to_all | solution.py:242
  51.8 0.0 copy-start.1
  51.8 2.2 %shard_map.48 = f32[128,768]{1,0:T(8,128)S(1)} custom-call(s32[1]{0:T(128)} %bitcast.3.base_ref, s32[1,32]{1,0:T(1,128)S(1)} %collective-permute-done.list_ref, s32[1]{0:T(128)} %collective-permute-done.1.count_ref, bf16[16,2,128,384]{3,2,1,0:T(8,128)(2,1)S(1)} %all_to_all.10.blocks_ref), custom_call_target="tpu_custom_call" | custom-call | flops 603979776 | bytes 1572864 | tf_op jit(solution)/shard_map/pallas_call | solution.py:53
  54.0 0.0 copy-start.2
  54.0 1.8 %collective-permute-start.2 = (f32[128,768]{1,0:T(8,128)S(1)}, f32[128,768]{1,0:T(8,128)S(1)}, u32[]{:S(2)}, u32[]{:S(2)}) collective-permute-start(f32[128,768]{1,0:T(8,128)S(1)} %shard_map.48), channel_id=1, source_target_pairs={{0,16},{16,0},{1,17},{17,1},{2,18},{18,2},{3,19},{19,3},{4,20},{20... | collective-permute-start | bytes 1179656 | tf_op jit(solution)/shard_map/ppermute | solution.py:253
  56.5 0.0 copy-done.1
  56.5 1.5 %shard_map.47.own_ref = f32[128,768]{1,0:T(8,128)S(1)} custom-call(s32[1]{0:T(128)} %bitcast.3.base_ref, s32[1,32]{1,0:T(1,128)S(1)} %copy-done.1, s32[1]{0:T(128)S(6)} %copy.6.count_ref, bf16[16,2,128,384]{3,2,1,0:T(8,128)(2,1)S(1)} %all_to_all.10.blocks_ref), custom_call_target="tpu_custom_call" | custom-call | flops 603979776 | bytes 1572864 | tf_op jit(solution)/shard_map/pallas_call | solution.py:53
  58.0 15.8 %collective-permute-done.2.other_ref = f32[128,768]{1,0:T(8,128)S(1)} collective-permute-done((f32[128,768]{1,0:T(8,128)S(1)}, f32[128,768]{1,0:T(8,128)S(1)}, u32[]{:S(2)}, u32[]{:S(2)}) %collective-permute-start.2) | collective-permute-done | bytes 393248 | tf_op jit(solution)/shard_map/ppermute | solution.py:253
  73.8 0.0 copy-done.2
  73.8 11.1 %shard_map.49 = bf16[384,256]{1,0:T(8,128)(2,1)S(1)} custom-call(s32[1]{0:T(128)S(6)} %copy.6.count_ref, f32[128,768]{1,0:T(8,128)S(1)} %shard_map.47.own_ref, f32[128,768]{1,0:T(8,128)S(1)} %collective-permute-done.2.other_ref, bf16[384,256]{1,0:T(8,128)(2,1)S(1)} %bitcast.34), custom_call_target="tpu_custom_call" | custom-call | flops 1000000000 | bytes 2000000 | tf_op jit(solution)/shard_map/pallas_call | solution.py:201
  84.9 0.1 collective-permute-start.3
  85.0 0.7 fusion.5
  85.7 9.3 %collective-permute-done.3 = bf16[384,256]{1,0:T(8,128)(2,1)S(1)} collective-permute-done((bf16[384,256]{1,0:T(8,128)(2,1)S(1)}, bf16[384,256]{1,0:T(8,128)(2,1)S(1)}, u32[]{:S(2)}, u32[]{:S(2)}) %collective-permute-start.3) | collective-permute-done | bytes 196640 | tf_op jit(solution)/shard_map/ppermute | solution.py:256
  95.0 0.7 fusion.4
  95.7 0.2 pad_maximum_fusion
  95.9 0.2 copy.5
  96.1 30.4 %all_to_all.11 = bf16[16,2,128,256]{3,2,1,0:T(8,128)(2,1)S(1)} all-to-all(bf16[16,2,128,256]{3,2,1,0:T(8,128)(2,1)S(1)} %copy.5), channel_id=1, replica_groups=mesh['half'=2,'inner'=4,'doppler'=4] {'inner','doppler'}, dimensions={0} | all-to-all | bytes 4194304 | tf_op jit(solution)/shard_map/all_to_all | solution.py:242
  126.5 0.1 dynamic-slice_bitcast_fusion.1
  126.7 1.5 %pad_maximum_fusion.1 = bf16[32,128,256]{2,1,0:T(8,128)(2,1)} fusion(bf16[16,128,256]{2,1,0:T(8,128)(2,1)S(1)} %get-tuple-element.20, bf16[16,128,256]{2,1,0:T(8,128)(2,1)S(1)} %get-tuple-element.19), kind=kLoop, calls=%fused_computation.1 | loop fusion | flops 1048576 | bytes 4194304 | tf_op jit(solution)/shard_map/concatenate | solution.py:269
Async XLA Ops:
  0.0 8.6 %collective-permute-start = (s32[1,32]{1,0:T(1,128)}, s32[1,32]{1,0:T(1,128)S(1)}, u32[]{:S(2)}, u32[]{:S(2)}) collective-permute-start(s32[1,32]{1,0:T(1,128)} %list_ref.1), channel_id=1, source_target_pairs={{0,16},{16,0},{1,17},{17,1},{2,18},{18,2},{3,19},{19,3},{4,20},{20... | collective-permute-start | bytes 392 | tf_op jit(solution)/shard_map/ppermute | solution.py:244
  4.0 4.5 %collective-permute-start.1 = (s32[1]{0:T(128)}, s32[1]{0:T(128)}, u32[]{:S(2)}, u32[]{:S(2)}) collective-permute-start(s32[1]{0:T(128)} %param.7), channel_id=1, source_target_pairs={{0,16},{16,0},{1,17},{17,1},{2,18},{18,2},{3,19},{19,3},{4,20},{20... | collective-permute-start | bytes 20 | tf_op jit(solution)/shard_map/ppermute | solution.py:245
  4.1 1.9 %copy-start = (bf16[32,128,384]{2,1,0:T(8,128)(2,1)S(1)}, bf16[32,128,384]{2,1,0:T(8,128)(2,1)}, u32[]{:S(2)}) copy-start(bf16[32,128,384]{2,1,0:T(8,128)(2,1)} %param.4) | copy-start | bytes 9437188
  51.8 4.6 %copy-start.1 = (s32[1,32]{1,0:T(1,128)S(1)}, s32[1,32]{1,0:T(1,128)}, u32[]{:S(2)}) copy-start(s32[1,32]{1,0:T(1,128)} %list_ref.1) | copy-start | bytes 388
  54.0 19.8 %copy-start.2 = (bf16[1,384,256]{2,1,0:T(8,128)(2,1)S(1)}, bf16[1,384,256]{2,1,0:T(8,128)(2,1)}, u32[]{:S(2)}) copy-start(bf16[1,384,256]{2,1,0:T(8,128)(2,1)} %param.5) | copy-start | bytes 589828
  54.0 19.7 %collective-permute-start.2 = (f32[128,768]{1,0:T(8,128)S(1)}, f32[128,768]{1,0:T(8,128)S(1)}, u32[]{:S(2)}, u32[]{:S(2)}) collective-permute-start(f32[128,768]{1,0:T(8,128)S(1)} %shard_map.48), channel_id=1, source_target_pairs={{0,16},{16,0},{1,17},{17,1},{2,18},{18,2},{3,19},{19,3},{4,20},{20... | collective-permute-start | bytes 1179656 | tf_op jit(solution)/shard_map/ppermute | solution.py:253
  84.9 10.1 %collective-permute-start.3 = (bf16[384,256]{1,0:T(8,128)(2,1)S(1)}, bf16[384,256]{1,0:T(8,128)(2,1)S(1)}, u32[]{:S(2)}, u32[]{:S(2)}) collective-permute-start(bf16[384,256]{1,0:T(8,128)(2,1)S(1)} %shard_map.49), channel_id=1, source_target_pairs={{0,16},{16,0},{1,17},{17,1},{2,18},{18,2},{3,19},{19,3},{4,20},{20... | collective-permute-start | bytes 589832 | tf_op jit(solution)/shard_map/ppermute | solution.py:256

commit v3 on v2

--- a/solution.py
+++ b/solution.py
@@ -10,58 +10,95 @@
 LOADING = 0.1
 EDGE = 128
 STEP = 16
+PACKED = 4 * EDGE + EDGE // 2 + 8
 INNER = ("inner", "doppler")
+EVERY = ("half",) + INNER
+VMEM_BYTES = 16 * 1024 * 1024
+SPLIT_BYTES = 16 * 1024 * 1024
+
+
+def edge_iota(dim, rows=EDGE):
+    return lax.broadcasted_iota(jnp.int32, (rows, EDGE), dim)
 
 
 def gram_kernel(base_ref, list_ref, count_ref, blocks_ref, out_ref, chosen):
-    step = pl.program_id(0)
-    count, _, rows, size = blocks_ref.shape
-
-    @pl.when(step == 0)
-    def _():
-        for p in range(list_ref.shape[1]):
-            chosen[list_ref[0, p]] = (p < count_ref[0]).astype(jnp.int32)
-
-    first = base_ref[0] + step * count
-    every = [blocks_ref[n, 0] for n in range(count)]
+    group, _, rows, size = blocks_ref.shape
+    for p in range(list_ref.shape[1]):
+        chosen[list_ref[0, p]] = (p < count_ref[0]).astype(jnp.int32)
+    every = [blocks_ref[n, 0] for n in range(group)]
     kept = [
-        jnp.where(chosen[first + n] > 0, x, jnp.zeros_like(x)) for n, x in enumerate(every)
+        jnp.where(chosen[base_ref[0] + n] > 0, x, jnp.zeros_like(x)) for n, x in enumerate(every)
     ]
     every = jnp.concatenate(every, axis=0)
     kept = jnp.concatenate(kept, axis=0)
-    def product(lo, hi):
+
+    def strip(i):
         return lax.dot_general(
-            kept[:, lo:hi], every[:, lo:], (((0,), (0,)), ((), ())),
+            kept[:, i * EDGE : (i + 1) * EDGE], every[:, i * EDGE :], (((0,), (0,)), ((), ())),
             preferred_element_type=jnp.float32,
         )
 
-    at = 0
-    for lo in range(0, size, 2 * EDGE):
-        hi = min(lo + 2 * EDGE, size)
-        part = product(lo, hi)
-        for i in range(lo, hi, EDGE):
-            width = size - i
-            out_ref[:, pl.ds(at, width)] = part[i - lo : i - lo + EDGE, i - lo :]
-            at += width
-
-
-def partial_gram(base, lists, counts, blocks, which, chunks=1):
+    half = EDGE // 2
+    r, c = edge_iota(0), edge_iota(1)
+    zero, one, two = strip(0), strip(1), strip(2)
+    out_ref[pl.ds(0, EDGE), :] = zero[:, EDGE : 2 * EDGE]
+    out_ref[pl.ds(EDGE, EDGE), :] = zero[:, 2 * EDGE :]
+    out_ref[pl.ds(2 * EDGE, EDGE), :] = one[:, EDGE:]
+    out_ref[pl.ds(3 * EDGE, EDGE), :] = jnp.where(r <= c, zero[:, :EDGE], one[:, :EDGE])
+    low = pltpu.roll(two[half:], half, axis=1)
+    rh, ch = r[:half], c[:half]
+    out_ref[pl.ds(4 * EDGE, half), :] = jnp.where((ch < half) & (rh > ch), low, two[:half])
+    first = jnp.sum(jnp.where(r == c, one[:, :EDGE], 0.0), axis=0, keepdims=True)
+    second = jnp.sum(jnp.where(rh == ch, low, 0.0), axis=0, keepdims=True)
+    s = edge_iota(0, 8)
+    out_ref[pl.ds(4 * EDGE + half, 8), :] = jnp.where(s == 0, first, jnp.where(s == 1, second, 0.0))
+
+
+def partial_gram(which, base, lists, counts, blocks):
     group, _, rows, size = blocks.shape
-    parts = size // EDGE
     smem = pl.BlockSpec(memory_space=pltpu.SMEM)
-    wide = EDGE * parts * (parts + 1) // 2
     return pl.pallas_call(
         gram_kernel,
-        out_shape=jax.ShapeDtypeStruct((EDGE, wide), jnp.float32),
-        grid=(chunks,),
-        in_specs=[smem, smem, smem, pl.BlockSpec((group // chunks, 1, rows, size), lambda i: (i, which, 0, 0))],
-        out_specs=pl.BlockSpec((EDGE, wide), lambda i: (0, 0)),
+        out_shape=jax.ShapeDtypeStruct((PACKED, EDGE), jnp.float32),
+        grid=(1,),
+        in_specs=[
+            smem, smem, smem, pl.BlockSpec((group, 1, rows, size), lambda i: (0, which, 0, 0))
+        ],
+        out_specs=pl.BlockSpec((PACKED, EDGE), lambda i: (0, 0)),
         scratch_shapes=[pltpu.SMEM((lists.shape[1],), jnp.int32)],
-        compiler_params=pltpu.CompilerParams(vmem_limit_bytes=16 * 1024 * 1024),
+        compiler_params=pltpu.CompilerParams(vmem_limit_bytes=2 * VMEM_BYTES),
         cost_estimate=pl.CostEstimate(
-            flops=2 * group * rows * size * size, bytes_accessed=2 * group * rows * size, transcendentals=0
+            flops=2 * group * rows * size * size,
+            bytes_accessed=2 * group * rows * size,
+            transcendentals=0,
         ),
     )(base, lists, counts, blocks)
+
+
+def unpack(packed):
+    half = EDGE // 2
+    r, c = edge_iota(0), edge_iota(1)
+    both = packed[3 * EDGE : 4 * EDGE]
+    turned = both.T
+    diag = packed[4 * EDGE + half : 4 * EDGE + half + 8]
+    zero = jnp.where(r <= c, both, turned)
+    one = jnp.where(r > c, both, jnp.where(r < c, turned, diag[0:1]))
+    top = packed[4 * EDGE : 4 * EDGE + half]
+    side = jnp.concatenate([top, jnp.zeros_like(top)], axis=0).T
+    rh, ch = r[:half], c[:half]
+    upper = jnp.where((ch < half) & (rh > ch), side[:half], top)
+    low = jnp.where(
+        rh > ch,
+        top,
+        jnp.where(rh < ch, side[:half], diag[1:2]),
+    )
+    lower = jnp.where(ch < half, side[half:], pltpu.roll(low, half, axis=1))
+    two = jnp.concatenate([upper, lower], axis=0)
+    return [
+        jnp.concatenate([zero, packed[:EDGE], packed[EDGE : 2 * EDGE]], axis=1),
+        jnp.concatenate([one, packed[2 * EDGE : 3 * EDGE]], axis=1),
+        two,
+    ]
 
 
 def fine(a, b, dims=(((1,), (0,)), ((), ()))):
@@ -152,15 +189,13 @@
     size = steer_ref.shape[0]
     parts = size // EDGE
     inv_scale = 1.0 / (BLOCK * count_ref[0]).astype(jnp.float32)
-    at = 0
+    strips = unpack(own_ref[...] + other_ref[...])
     for i in range(parts):
         width = size - i * EDGE
         rows = pl.ds(i * EDGE, EDGE)
-        strip = (own_ref[:, pl.ds(at, width)] + other_ref[:, pl.ds(at, width)]) * inv_scale
         r = lax.broadcasted_iota(jnp.int32, (EDGE, width), 0)
         c = lax.broadcasted_iota(jnp.int32, (EDGE, width), 1)
-        work[rows, pl.ds(i * EDGE, width)] = strip + jnp.where(r == c, LOADING, 0.0)
-        at += width
+        work[rows, pl.ds(i * EDGE, width)] = strips[i] * inv_scale + jnp.where(r == c, LOADING, 0.0)
     beams = steer_ref.shape[1]
     work[:, pl.ds(size, beams)] = steer_ref[...].astype(jnp.float32)
     total = size + beams
@@ -204,7 +239,7 @@
         in_specs=[pl.BlockSpec(memory_space=pltpu.SMEM), vmem, vmem, vmem],
         out_specs=vmem,
         scratch_shapes=[pltpu.VMEM((size, size + beams), jnp.float32)],
-        compiler_params=pltpu.CompilerParams(vmem_limit_bytes=16 * 1024 * 1024),
+        compiler_params=pltpu.CompilerParams(vmem_limit_bytes=VMEM_BYTES),
         cost_estimate=pl.CostEstimate(flops=10**9, bytes_accessed=2 * 10**6, transcendentals=0),
     )(count, own, other, steering)
 
@@ -213,45 +248,50 @@
     out_ref[:, 0] = x_ref[0]
 
 
-def split(x, which):
-    halves, count, rows, wide = x.shape
-    chunk = count // 4
+def split(which, x):
+    halves, group, rows, wide = x.shape
+    chunks = 4
     return pl.pallas_call(
         split_kernel,
-        out_shape=jax.ShapeDtypeStruct((count, halves, rows, wide), x.dtype),
+        out_shape=jax.ShapeDtypeStruct((group, halves, rows, wide), x.dtype),
         grid_spec=pltpu.PrefetchScalarGridSpec(
             num_scalar_prefetch=1,
-            grid=(halves, 4),
-            in_specs=[pl.BlockSpec((1, chunk, rows, wide), lambda s, i, which: (which[s], i, 0, 0))],
-            out_specs=pl.BlockSpec((chunk, 1, rows, wide), lambda s, i, which: (i, s, 0, 0)),
+            grid=(halves, chunks),
+            in_specs=[
+                pl.BlockSpec(
+                    (1, group // chunks, rows, wide), lambda s, i, which: (which[s], i, 0, 0)
+                )
+            ],
+            out_specs=pl.BlockSpec(
+                (group // chunks, 1, rows, wide), lambda s, i, which: (i, s, 0, 0)
+            ),
         ),
-        compiler_params=pltpu.CompilerParams(vmem_limit_bytes=16 * 1024 * 1024),
+        compiler_params=pltpu.CompilerParams(vmem_limit_bytes=SPLIT_BYTES),
         cost_estimate=pl.CostEstimate(flops=0, bytes_accessed=2 * x.size, transcendentals=0),
     )(which, x)
 
 
 def body(halves, snapshots, steering, train_list, train_count):
     bin_total, gate_rows, channels = snapshots.shape
-    half = lax.axis_index("half")
+    half = lax.axis_index("half").astype(jnp.int32)
     group = bin_total // halves
+    order, base = jnp.stack([half, 1 - half]), half[None] * group
     peers = [(0, 1), (1, 0)]
-    which = jnp.stack([half, 1 - half]).astype(jnp.int32)
-    base = (half * group).astype(jnp.int32)[None]
 
     def exchange(x):
         return lax.all_to_all(x, INNER, split_axis=0, concat_axis=0, tiled=True)
 
     other_list = lax.ppermute(train_list, "half", peers)
     other_count = lax.ppermute(train_count, "half", peers)
-    outgoing = split(snapshots.reshape(halves, group, gate_rows, channels), which)
-    outgoing, other_list, other_count, base, which = lax.optimization_barrier(
-        (outgoing, other_list, other_count, base, which)
+    outgoing = split(order, snapshots.reshape(halves, group, gate_rows, channels))
+    outgoing, other_list, other_count, base = lax.optimization_barrier(
+        (outgoing, other_list, other_count, base)
     )
     blocks = exchange(outgoing)
 
-    other_gram = partial_gram(base, other_list, other_count, blocks, 1)
+    other_gram = partial_gram(1, base, other_list, other_count, blocks)
     arrived = lax.ppermute(other_gram, "half", peers)
-    own_gram = partial_gram(base, train_list, train_count, blocks, 0)
+    own_gram = partial_gram(0, base, train_list, train_count, blocks)
     weights = make_weights(train_count, own_gram, arrived, steering[0])
     other_weights = lax.ppermute(weights, "half", peers)
 
@@ -272,10 +312,7 @@
 def solution(mesh):
     ranges, dopplers = mesh.devices.shape
     halves = 2
-    cut = Mesh(
-        mesh.devices.reshape(halves, ranges // halves, dopplers), ("half", "inner", "doppler")
-    )
-    every = ("half", "inner", "doppler")
+    cut = Mesh(mesh.devices.reshape(halves, ranges // halves, dopplers), EVERY)
 
     def run(*args):
         return body(halves, *args)
@@ -283,7 +320,7 @@
     return jax.shard_map(
         run,
         mesh=cut,
-        in_specs=(P(None, every, None), P(every, None, None), P(every, None), P(every)),
-        out_specs=P(None, every, None),
+        in_specs=(P(None, EVERY, None), P(EVERY, None, None), P(EVERY, None), P(EVERY)),
+        out_specs=P(None, EVERY, None),
         check_vma=False,
     )

time: 128 us -> 125 us (0.977)
  waiting for transfers between devices: 26.3 us -> 22.4 us
    ppermute x1, waiting for transfers between devices: 15.8 us -> 11.8 us  [body(): arrived = lax.ppermute(other_gram, 'half', peers)]
where the time goes in v3:
time: 125 us; the launch traced here: 124 us
  blocking collectives  73.7 us (59%)
  waiting for transfers between devices  22.4 us (18%)
  Pallas kernels  16.2 us (13%)
  starting transfers between devices  5.91 us (5%)
  local copies, waits for them, and re-layouts  2.24 us (2%)
  other arithmetic  1.77 us (1%)
  matrix products  1.4 us (1%)
    all_to_all x2, blocking collectives, exchange(): return lax.all_to_all(x, INNER, split_axis=0, concat_axis=0, tiled=True)  73.7 us
    ppermute x1, waiting for transfers between devices, body(): arrived = lax.ppermute(other_gram, 'half', peers)  11.8 us
    pallas_call x1, Pallas kernels, make_weights(): pl.pallas_call(solve_kernel, out_shape=jax.ShapeDtypeStruct((size, beams)...  11.3 us
    ppermute x1, waiting for transfers between devices, body(): other_weights = lax.ppermute(weights, 'half', peers)  9.31 us
    ppermute x1, starting transfers between devices, body(): other_list = lax.ppermute(train_list, 'half', peers)  4.04 us
    pallas_call x2, Pallas kernels, partial_gram(): pl.pallas_call(gram_kernel, out_shape=jax.ShapeDtypeStruct((PACKED, EDGE)...  3.55 us
  transfers between devices with their start and end apart: 4, of which 3 were waited for; matrix products, arithmetic and copies ran while one was open for 1% of the time, Pallas kernels for 2%

profile of v3, /device:TPU:0, one launch (start us, length us, event | category | flops | bytes accessed | tf_op | source)
XLA Modules:
  0.0 124.3 jit_solution(12895173080139544262)
XLA Ops:
  0.0 4.0 %collective-permute-start = (s32[1,32]{1,0:T(1,128)}, s32[1,32]{1,0:T(1,128)S(1)}, u32[]{:S(2)}, u32[]{:S(2)}) collective-permute-start(s32[1,32]{1,0:T(1,128)} %list_ref.1), channel_id=1, source_target_pairs={{0,16},{16,0},{1,17},{17,1},{2,18},{18,2},{3,19},{19,3},{4,20},{20... | collective-permute-start | bytes 392 | tf_op jit(solution)/shard_map/ppermute | solution.py:284
  4.0 0.0 collective-permute-start.1
  4.1 0.1 pad_add_fusion.which_ref
  4.1 0.0 copy-start
  4.1 1.9 %copy-done = bf16[32,128,384]{2,1,0:T(8,128)(2,1)S(1)} copy-done((bf16[32,128,384]{2,1,0:T(8,128)(2,1)S(1)}, bf16[32,128,384]{2,1,0:T(8,128)(2,1)}, u32[]{:S(2)}) %copy-start) | copy-done | bytes 3145752
  6.0 1.3 %shard_map.46 = bf16[16,2,128,384]{3,2,1,0:T(8,128)(2,1)S(1)} custom-call(s32[2]{0:T(128)S(1)} %pad_add_fusion.which_ref, bf16[2,16,128,384]{3,2,1,0:T(8,128)(2,1)S(1)} %bitcast.32), custom_call_target="tpu_custom_call" | custom-call | bytes 3145728 | tf_op jit(solution)/shard_map/pallas_call | solution.py:254
  7.4 1.2 collective-permute-done.1.count_ref
  8.6 0.0 collective-permute-done.list_ref
  8.6 43.3 %all_to_all.10.blocks_ref = bf16[16,2,128,384]{3,2,1,0:T(8,128)(2,1)S(1)} all-to-all(bf16[16,2,128,384]{3,2,1,0:T(8,128)(2,1)S(1)} %shard_map.46), channel_id=1, replica_groups=mesh['half'=2,'inner'=4,'doppler'=4] {'inner','doppler'}, dimensions={0} | all-to-all | bytes 6291456 | tf_op jit(solution)/shard_map/all_to_all | solution.py:282
  51.8 0.0 copy-start.1
  51.8 2.1 %shard_map.48 = f32[584,128]{1,0:T(8,128)S(1)} custom-call(s32[1]{0:T(128)S(6)} %mul.3.base_ref, s32[1,32]{1,0:T(1,128)S(1)} %collective-permute-done.list_ref, s32[1]{0:T(128)} %collective-permute-done.1.count_ref, bf16[16,2,128,384]{3,2,1,0:T(8,128)(2,1)S(1)} %all_to_all.10.blocks_ref), custom_call_target="tpu_custom_call" | custom-call | flops 603979776 | bytes 1572864 | tf_op jit(solution)/shard_map/pallas_call | solution.py:60
  54.0 0.0 copy-start.2
  54.0 1.8 %collective-permute-start.2 = (f32[584,128]{1,0:T(8,128)S(1)}, f32[584,128]{1,0:T(8,128)S(1)}, u32[]{:S(2)}, u32[]{:S(2)}) collective-permute-start(f32[584,128]{1,0:T(8,128)S(1)} %shard_map.48), channel_id=1, source_target_pairs={{0,16},{16,0},{1,17},{17,1},{2,18},{18,2},{3,19},{19,3},{4,20},{20... | collective-permute-start | bytes 897032 | tf_op jit(solution)/shard_map/ppermute | solution.py:293
  56.4 0.0 copy-done.1
  56.4 1.4 %shard_map.47.own_ref = f32[584,128]{1,0:T(8,128)S(1)} custom-call(s32[1]{0:T(128)S(6)} %mul.3.base_ref, s32[1,32]{1,0:T(1,128)S(1)} %copy-done.1, s32[1]{0:T(128)S(6)} %copy.6.count_ref, bf16[16,2,128,384]{3,2,1,0:T(8,128)(2,1)S(1)} %all_to_all.10.blocks_ref), custom_call_target="tpu_custom_call" | custom-call | flops 603979776 | bytes 1572864 | tf_op jit(solution)/shard_map/pallas_call | solution.py:60
  57.8 11.8 %collective-permute-done.2.other_ref = f32[584,128]{1,0:T(8,128)S(1)} collective-permute-done((f32[584,128]{1,0:T(8,128)S(1)}, f32[584,128]{1,0:T(8,128)S(1)}, u32[]{:S(2)}, u32[]{:S(2)}) %collective-permute-start.2) | collective-permute-done | bytes 299040 | tf_op jit(solution)/shard_map/ppermute | solution.py:293
  69.7 0.0 copy-done.2
  69.7 11.3 %shard_map.49 = bf16[384,256]{1,0:T(8,128)(2,1)S(1)} custom-call(s32[1]{0:T(128)S(6)} %copy.6.count_ref, f32[584,128]{1,0:T(8,128)S(1)} %shard_map.47.own_ref, f32[584,128]{1,0:T(8,128)S(1)} %collective-permute-done.2.other_ref, bf16[384,256]{1,0:T(8,128)(2,1)S(1)} %bitcast.33), custom_call_target="tpu_custom_call" | custom-call | flops 1000000000 | bytes 2000000 | tf_op jit(solution)/shard_map/pallas_call | solution.py:236
  81.0 0.1 collective-permute-start.3
  81.1 0.7 fusion.5
  81.8 9.3 %collective-permute-done.3 = bf16[384,256]{1,0:T(8,128)(2,1)S(1)} collective-permute-done((bf16[384,256]{1,0:T(8,128)(2,1)S(1)}, bf16[384,256]{1,0:T(8,128)(2,1)S(1)}, u32[]{:S(2)}, u32[]{:S(2)}) %collective-permute-start.3) | collective-permute-done | bytes 196640 | tf_op jit(solution)/shard_map/ppermute | solution.py:296
  91.1 0.7 fusion.4
  91.8 0.2 pad_maximum_fusion
  92.0 0.2 copy.5
  92.2 30.4 %all_to_all.11 = bf16[16,2,128,256]{3,2,1,0:T(8,128)(2,1)S(1)} all-to-all(bf16[16,2,128,256]{3,2,1,0:T(8,128)(2,1)S(1)} %copy.5), channel_id=1, replica_groups=mesh['half'=2,'inner'=4,'doppler'=4] {'inner','doppler'}, dimensions={0} | all-to-all | bytes 4194304 | tf_op jit(solution)/shard_map/all_to_all | solution.py:282
  122.6 0.1 dynamic-slice_bitcast_fusion.1
  122.8 1.5 %pad_maximum_fusion.1 = bf16[32,128,256]{2,1,0:T(8,128)(2,1)} fusion(bf16[16,128,256]{2,1,0:T(8,128)(2,1)S(1)} %get-tuple-element.20, bf16[16,128,256]{2,1,0:T(8,128)(2,1)S(1)} %get-tuple-element.19), kind=kLoop, calls=%fused_computation.1 | loop fusion | flops 1048576 | bytes 4194304 | tf_op jit(solution)/shard_map/concatenate | solution.py:309
Async XLA Ops:
  0.0 8.6 %collective-permute-start = (s32[1,32]{1,0:T(1,128)}, s32[1,32]{1,0:T(1,128)S(1)}, u32[]{:S(2)}, u32[]{:S(2)}) collective-permute-start(s32[1,32]{1,0:T(1,128)} %list_ref.1), channel_id=1, source_target_pairs={{0,16},{16,0},{1,17},{17,1},{2,18},{18,2},{3,19},{19,3},{4,20},{20... | collective-permute-start | bytes 392 | tf_op jit(solution)/shard_map/ppermute | solution.py:284
  4.0 4.5 %collective-permute-start.1 = (s32[1]{0:T(128)}, s32[1]{0:T(128)}, u32[]{:S(2)}, u32[]{:S(2)}) collective-permute-start(s32[1]{0:T(128)} %param.7), channel_id=1, source_target_pairs={{0,16},{16,0},{1,17},{17,1},{2,18},{18,2},{3,19},{19,3},{4,20},{20... | collective-permute-start | bytes 20 | tf_op jit(solution)/shard_map/ppermute | solution.py:285
  4.1 1.9 %copy-start = (bf16[32,128,384]{2,1,0:T(8,128)(2,1)S(1)}, bf16[32,128,384]{2,1,0:T(8,128)(2,1)}, u32[]{:S(2)}) copy-start(bf16[32,128,384]{2,1,0:T(8,128)(2,1)} %param.4) | copy-start | bytes 9437188
  51.8 4.6 %copy-start.1 = (s32[1,32]{1,0:T(1,128)S(1)}, s32[1,32]{1,0:T(1,128)}, u32[]{:S(2)}) copy-start(s32[1,32]{1,0:T(1,128)} %list_ref.1) | copy-start | bytes 388
  54.0 15.7 %copy-start.2 = (bf16[1,384,256]{2,1,0:T(8,128)(2,1)S(1)}, bf16[1,384,256]{2,1,0:T(8,128)(2,1)}, u32[]{:S(2)}) copy-start(bf16[1,384,256]{2,1,0:T(8,128)(2,1)} %param.5) | copy-start | bytes 589828
  54.0 15.7 %collective-permute-start.2 = (f32[584,128]{1,0:T(8,128)S(1)}, f32[584,128]{1,0:T(8,128)S(1)}, u32[]{:S(2)}, u32[]{:S(2)}) collective-permute-start(f32[584,128]{1,0:T(8,128)S(1)} %shard_map.48), channel_id=1, source_target_pairs={{0,16},{16,0},{1,17},{17,1},{2,18},{18,2},{3,19},{19,3},{4,20},{20... | collective-permute-start | bytes 897032 | tf_op jit(solution)/shard_map/ppermute | solution.py:293
  81.0 10.1 %collective-permute-start.3 = (bf16[384,256]{1,0:T(8,128)(2,1)S(1)}, bf16[384,256]{1,0:T(8,128)(2,1)S(1)}, u32[]{:S(2)}, u32[]{:S(2)}) collective-permute-start(bf16[384,256]{1,0:T(8,128)(2,1)S(1)} %shard_map.49), channel_id=1, source_target_pairs={{0,16},{16,0},{1,17},{17,1},{2,18},{18,2},{3,19},{19,3},{4,20},{20... | collective-permute-start | bytes 589832 | tf_op jit(solution)/shard_map/ppermute | solution.py:296

commit v4 on v3

--- a/solution.py
+++ b/solution.py
@@ -1,3 +1,5 @@
+import functools
+
 import jax
 import jax.numpy as jnp
 from jax import lax
@@ -21,11 +23,11 @@
     return lax.broadcasted_iota(jnp.int32, (rows, EDGE), dim)
 
 
-def gram_kernel(base_ref, list_ref, count_ref, blocks_ref, out_ref, chosen):
+def gram_kernel(which, base_ref, list_ref, count_ref, blocks_ref, out_ref, chosen):
     group, _, rows, size = blocks_ref.shape
     for p in range(list_ref.shape[1]):
         chosen[list_ref[0, p]] = (p < count_ref[0]).astype(jnp.int32)
-    every = [blocks_ref[n, 0] for n in range(group)]
+    every = [blocks_ref[n, which] for n in range(group)]
     kept = [
         jnp.where(chosen[base_ref[0] + n] > 0, x, jnp.zeros_like(x)) for n, x in enumerate(every)
     ]
@@ -57,16 +59,14 @@
 def partial_gram(which, base, lists, counts, blocks):
     group, _, rows, size = blocks.shape
     smem = pl.BlockSpec(memory_space=pltpu.SMEM)
+    vmem = pl.BlockSpec(memory_space=pltpu.VMEM)
     return pl.pallas_call(
-        gram_kernel,
+        functools.partial(gram_kernel, which),
         out_shape=jax.ShapeDtypeStruct((PACKED, EDGE), jnp.float32),
-        grid=(1,),
-        in_specs=[
-            smem, smem, smem, pl.BlockSpec((group, 1, rows, size), lambda i: (0, which, 0, 0))
-        ],
-        out_specs=pl.BlockSpec((PACKED, EDGE), lambda i: (0, 0)),
+        in_specs=[smem, smem, smem, vmem],
+        out_specs=vmem,
         scratch_shapes=[pltpu.SMEM((lists.shape[1],), jnp.int32)],
-        compiler_params=pltpu.CompilerParams(vmem_limit_bytes=2 * VMEM_BYTES),
+        compiler_params=pltpu.CompilerParams(vmem_limit_bytes=3 * VMEM_BYTES),
         cost_estimate=pl.CostEstimate(
             flops=2 * group * rows * size * size,
             bytes_accessed=2 * group * rows * size,
@@ -141,11 +141,12 @@
         first = jnp.where(one, 1.0, jnp.where(two, 0.0, -cols[k]))
         second = jnp.where(two, 1.0, jnp.where(one, 0.0, -cols[k + 1]))
 
+        left = (first * c - second * b) * inv
+        after = (second * a - first * b) * inv
+
         def step(x):
             r, s = row(x, k), row(x, k + 1)
-            up = (c * r - b * s) * inv
-            down = (a * s - b * r) * inv
-            return (jnp.where(here, 0.0, x) + first * up) + second * down
+            return jnp.where(here, 0.0, x) + (left * r + after * s)
 
         for i in range(k + 2, STEP):
             cols[i] = step(cols[i])
@@ -160,7 +161,12 @@
     lane = lax.broadcasted_iota(jnp.int32, full, 1)
 
     def spread(x, at):
-        return [jnp.broadcast_to(x[:, at + i : at + i + 1], full) for i in range(STEP)]
+        return [
+            jnp.take_along_axis(
+                x, jnp.full(full, at + i, jnp.int32), axis=1, mode="promise_in_bounds"
+            )
+            for i in range(STEP)
+        ]
 
     rows = strips[0]
     for p in range(panels):
@@ -185,42 +191,41 @@
     return jnp.concatenate(strips, axis=0)
 
 
-def solve_kernel(count_ref, own_ref, other_ref, steer_ref, out_ref, work):
-    size = steer_ref.shape[0]
+def solve_kernel(count_ref, own_ref, other_ref, steer_ref, out_ref):
+    size, beams = steer_ref.shape
     parts = size // EDGE
     inv_scale = 1.0 / (BLOCK * count_ref[0]).astype(jnp.float32)
     strips = unpack(own_ref[...] + other_ref[...])
+    loading = jnp.where(edge_iota(0) == edge_iota(1), LOADING, 0.0)
+    rest = []
     for i in range(parts):
-        width = size - i * EDGE
-        rows = pl.ds(i * EDGE, EDGE)
-        r = lax.broadcasted_iota(jnp.int32, (EDGE, width), 0)
-        c = lax.broadcasted_iota(jnp.int32, (EDGE, width), 1)
-        work[rows, pl.ds(i * EDGE, width)] = strips[i] * inv_scale + jnp.where(r == c, LOADING, 0.0)
-    beams = steer_ref.shape[1]
-    work[:, pl.ds(size, beams)] = steer_ref[...].astype(jnp.float32)
-    total = size + beams
+        row = [strips[i][:, j * EDGE : (j + 1) * EDGE] * inv_scale for j in range(parts - i)]
+        row[0] = row[0] + loading
+        rest.append(row)
+    right = [steer_ref[pl.ds(i * EDGE, EDGE), :].astype(jnp.float32) for i in range(parts)]
+    turned = (((0,), (0,)), ((), ()))
     made = []
     for i in range(parts):
-        rows = pl.ds(i * EDGE, EDGE)
-        strips = [
-            work[pl.ds(i * EDGE + q * STEP, STEP), pl.ds(i * EDGE, EDGE)]
-            for q in range(EDGE // STEP)
-        ]
-        minus = negative_inverse(strips)
-        right = work[rows, pl.ds((i + 1) * EDGE, total - (i + 1) * EDGE)]
-        p = -fine(minus, right)
-        made.append(p)
-        for j in range(i + 1, parts):
-            lhs = work[rows, pl.ds(j * EDGE, EDGE)]
-            cut = p[:, (j - i - 1) * EDGE :]
-            span = pl.ds(j * EDGE, total - j * EDGE)
-            target = pl.ds(j * EDGE, EDGE)
-            work[target, span] = work[target, span] - fine(lhs, cut, (((0,), (0,)), ((), ())))
+        diag = rest[i][0]
+        minus = negative_inverse([diag[q : q + STEP] for q in range(0, EDGE, STEP)])
+        lhs = rest[i][1:]
+        plus = [None] * len(lhs)
+        for j in range(len(lhs)):
+            plus[j] = -fine(minus, lhs[j])
+            if j == 0:
+                rest[i + 1][0] = rest[i + 1][0] - fine(lhs[0], plus[0], turned)
+        last = -fine(minus, right[i])
+        for j in range(len(lhs)):
+            for k in range(j, len(lhs)):
+                if k > 0:
+                    rest[i + 1 + j][k - j] = rest[i + 1 + j][k - j] - fine(lhs[j], plus[k], turned)
+            right[i + 1 + j] = right[i + 1 + j] - fine(lhs[j], last, turned)
+        made.append((plus, last))
     found = [None] * parts
     for i in reversed(range(parts)):
-        x = made[i][:, (parts - i - 1) * EDGE :]
-        for j in range(i + 1, parts):
-            x = x - fine(made[i][:, (j - i - 1) * EDGE : (j - i) * EDGE], found[j])
+        plus, x = made[i]
+        for j, p in enumerate(plus):
+            x = x - fine(p, found[i + 1 + j])
         found[i] = x
     response = 0.0
     for i in range(parts):
@@ -238,7 +243,6 @@
         out_shape=jax.ShapeDtypeStruct((size, beams), jnp.bfloat16),
         in_specs=[pl.BlockSpec(memory_space=pltpu.SMEM), vmem, vmem, vmem],
         out_specs=vmem,
-        scratch_shapes=[pltpu.VMEM((size, size + beams), jnp.float32)],
         compiler_params=pltpu.CompilerParams(vmem_limit_bytes=VMEM_BYTES),
         cost_estimate=pl.CostEstimate(flops=10**9, bytes_accessed=2 * 10**6, transcendentals=0),
     )(count, own, other, steering)

time: 125 us -> 122 us (0.976)
  Pallas kernels: 16.2 us -> 13.8 us
    pallas_call x1, Pallas kernels: 11.3 us -> 8.94 us  [make_weights(): pl.pallas_call(solve_kernel, out_shape=jax.ShapeDtypeStruct((size, beams)...]
where the time goes in v4:
time: 122 us
  blocking collectives  73.7 us (60%)
  waiting for transfers between devices  22.4 us (18%)
  Pallas kernels  13.8 us (11%)
  starting transfers between devices  5.91 us (5%)
  local copies, waits for them, and re-layouts  2.24 us (2%)
  other arithmetic  1.77 us (1%)
  matrix products  1.4 us (1%)
    all_to_all x2, blocking collectives, exchange(): return lax.all_to_all(x, INNER, split_axis=0, concat_axis=0, tiled=True)  73.7 us
    ppermute x1, waiting for transfers between devices, body(): arrived = lax.ppermute(other_gram, 'half', peers)  11.8 us
    ppermute x1, waiting for transfers between devices, body(): other_weights = lax.ppermute(weights, 'half', peers)  9.31 us
    pallas_call x1, Pallas kernels, make_weights(): pl.pallas_call(solve_kernel, out_shape=jax.ShapeDtypeStruct((size, beams)...  8.94 us
    ppermute x1, starting transfers between devices, body(): other_list = lax.ppermute(train_list, 'half', peers)  4.04 us
    pallas_call x2, Pallas kernels, partial_gram(): pl.pallas_call(functools.partial(gram_kernel, which), out_shape=jax.Shape...  3.57 us
  transfers between devices with their start and end apart: 4, of which 3 were waited for; matrix products, arithmetic and copies ran while one was open for 1% of the time, Pallas kernels for 2%

profile of v4, /device:TPU:0, one launch (start us, length us, event | category | flops | bytes accessed | tf_op | source)
XLA Modules:
  0.0 121.9 jit_solution(12117762077756952468)
XLA Ops:
  0.0 4.0 %collective-permute-start = (s32[1,32]{1,0:T(1,128)}, s32[1,32]{1,0:T(1,128)S(1)}, u32[]{:S(2)}, u32[]{:S(2)}) collective-permute-start(s32[1,32]{1,0:T(1,128)} %list_ref.1), channel_id=1, source_target_pairs={{0,16},{16,0},{1,17},{17,1},{2,18},{18,2},{3,19},{19,3},{4,20},{20... | collective-permute-start | bytes 392 | tf_op jit(solution)/shard_map/ppermute | solution.py:288
  4.0 0.0 collective-permute-start.1
  4.1 0.1 pad_add_fusion.which_ref
  4.1 0.0 copy-start
  4.1 1.9 %copy-done = bf16[32,128,384]{2,1,0:T(8,128)(2,1)S(1)} copy-done((bf16[32,128,384]{2,1,0:T(8,128)(2,1)S(1)}, bf16[32,128,384]{2,1,0:T(8,128)(2,1)}, u32[]{:S(2)}) %copy-start) | copy-done | bytes 3145752
  6.0 1.3 %shard_map.46 = bf16[16,2,128,384]{3,2,1,0:T(8,128)(2,1)S(1)} custom-call(s32[2]{0:T(128)S(1)} %pad_add_fusion.which_ref, bf16[2,16,128,384]{3,2,1,0:T(8,128)(2,1)S(1)} %bitcast.32), custom_call_target="tpu_custom_call" | custom-call | bytes 3145728 | tf_op jit(solution)/shard_map/pallas_call | solution.py:258
  7.4 1.2 collective-permute-done.1.count_ref
  8.6 0.0 collective-permute-done.list_ref
  8.6 43.3 %all_to_all.10.blocks_ref = bf16[16,2,128,384]{3,2,1,0:T(8,128)(2,1)S(1)} all-to-all(bf16[16,2,128,384]{3,2,1,0:T(8,128)(2,1)S(1)} %shard_map.46), channel_id=1, replica_groups=mesh['half'=2,'inner'=4,'doppler'=4] {'inner','doppler'}, dimensions={0} | all-to-all | bytes 6291456 | tf_op jit(solution)/shard_map/all_to_all | solution.py:286
  51.8 0.0 copy-start.1
  51.8 2.1 %shard_map.48 = f32[584,128]{1,0:T(8,128)S(1)} custom-call(s32[1]{0:T(128)S(6)} %mul.3.base_ref, s32[1,32]{1,0:T(1,128)S(1)} %collective-permute-done.list_ref, s32[1]{0:T(128)} %collective-permute-done.1.count_ref, bf16[16,2,128,384]{3,2,1,0:T(8,128)(2,1)S(1)} %all_to_all.10.blocks_ref), custom_call_target="tpu_custom_call" | custom-call | flops 603979776 | bytes 1572864 | tf_op jit(solution)/shard_map/pallas_call | solution.py:63
  54.0 0.0 copy-start.2
  54.0 1.8 %collective-permute-start.2 = (f32[584,128]{1,0:T(8,128)S(1)}, f32[584,128]{1,0:T(8,128)S(1)}, u32[]{:S(2)}, u32[]{:S(2)}) collective-permute-start(f32[584,128]{1,0:T(8,128)S(1)} %shard_map.48), channel_id=1, source_target_pairs={{0,16},{16,0},{1,17},{17,1},{2,18},{18,2},{3,19},{19,3},{4,20},{20... | collective-permute-start | bytes 897032 | tf_op jit(solution)/shard_map/ppermute | solution.py:297
  56.4 0.0 copy-done.1
  56.4 1.4 %shard_map.47.own_ref = f32[584,128]{1,0:T(8,128)S(1)} custom-call(s32[1]{0:T(128)S(6)} %mul.3.base_ref, s32[1,32]{1,0:T(1,128)S(1)} %copy-done.1, s32[1]{0:T(128)S(6)} %copy.6.count_ref, bf16[16,2,128,384]{3,2,1,0:T(8,128)(2,1)S(1)} %all_to_all.10.blocks_ref), custom_call_target="tpu_custom_call" | custom-call | flops 603979776 | bytes 1572864 | tf_op jit(solution)/shard_map/pallas_call | solution.py:63
  57.9 11.8 %collective-permute-done.2.other_ref = f32[584,128]{1,0:T(8,128)S(1)} collective-permute-done((f32[584,128]{1,0:T(8,128)S(1)}, f32[584,128]{1,0:T(8,128)S(1)}, u32[]{:S(2)}, u32[]{:S(2)}) %collective-permute-start.2) | collective-permute-done | bytes 299040 | tf_op jit(solution)/shard_map/ppermute | solution.py:297
  69.7 0.0 copy-done.2
  69.7 8.9 %shard_map.49 = bf16[384,256]{1,0:T(8,128)(2,1)S(1)} custom-call(s32[1]{0:T(128)S(6)} %copy.6.count_ref, f32[584,128]{1,0:T(8,128)S(1)} %shard_map.47.own_ref, f32[584,128]{1,0:T(8,128)S(1)} %collective-permute-done.2.other_ref, bf16[384,256]{1,0:T(8,128)(2,1)S(1)} %bitcast.33), custom_call_target="tpu_custom_call" | custom-call | flops 1000000000 | bytes 2000000 | tf_op jit(solution)/shard_map/pallas_call | solution.py:241
  78.6 0.1 collective-permute-start.3
  78.7 0.7 fusion.5
  79.4 9.3 %collective-permute-done.3 = bf16[384,256]{1,0:T(8,128)(2,1)S(1)} collective-permute-done((bf16[384,256]{1,0:T(8,128)(2,1)S(1)}, bf16[384,256]{1,0:T(8,128)(2,1)S(1)}, u32[]{:S(2)}, u32[]{:S(2)}) %collective-permute-start.3) | collective-permute-done | bytes 196640 | tf_op jit(solution)/shard_map/ppermute | solution.py:300
  88.8 0.7 fusion.4
  89.5 0.2 pad_maximum_fusion
  89.7 0.2 copy.5
  89.9 30.4 %all_to_all.11 = bf16[16,2,128,256]{3,2,1,0:T(8,128)(2,1)S(1)} all-to-all(bf16[16,2,128,256]{3,2,1,0:T(8,128)(2,1)S(1)} %copy.5), channel_id=1, replica_groups=mesh['half'=2,'inner'=4,'doppler'=4] {'inner','doppler'}, dimensions={0} | all-to-all | bytes 4194304 | tf_op jit(solution)/shard_map/all_to_all | solution.py:286
  120.3 0.1 dynamic-slice_bitcast_fusion.1
  120.4 1.5 %pad_maximum_fusion.1 = bf16[32,128,256]{2,1,0:T(8,128)(2,1)} fusion(bf16[16,128,256]{2,1,0:T(8,128)(2,1)S(1)} %get-tuple-element.20, bf16[16,128,256]{2,1,0:T(8,128)(2,1)S(1)} %get-tuple-element.19), kind=kLoop, calls=%fused_computation.1 | loop fusion | flops 1048576 | bytes 4194304 | tf_op jit(solution)/shard_map/concatenate | solution.py:313
Async XLA Ops:
  0.0 8.6 %collective-permute-start = (s32[1,32]{1,0:T(1,128)}, s32[1,32]{1,0:T(1,128)S(1)}, u32[]{:S(2)}, u32[]{:S(2)}) collective-permute-start(s32[1,32]{1,0:T(1,128)} %list_ref.1), channel_id=1, source_target_pairs={{0,16},{16,0},{1,17},{17,1},{2,18},{18,2},{3,19},{19,3},{4,20},{20... | collective-permute-start | bytes 392 | tf_op jit(solution)/shard_map/ppermute | solution.py:288
  4.0 4.5 %collective-permute-start.1 = (s32[1]{0:T(128)}, s32[1]{0:T(128)}, u32[]{:S(2)}, u32[]{:S(2)}) collective-permute-start(s32[1]{0:T(128)} %param.7), channel_id=1, source_target_pairs={{0,16},{16,0},{1,17},{17,1},{2,18},{18,2},{3,19},{19,3},{4,20},{20... | collective-permute-start | bytes 20 | tf_op jit(solution)/shard_map/ppermute | solution.py:289
  4.1 1.9 %copy-start = (bf16[32,128,384]{2,1,0:T(8,128)(2,1)S(1)}, bf16[32,128,384]{2,1,0:T(8,128)(2,1)}, u32[]{:S(2)}) copy-start(bf16[32,128,384]{2,1,0:T(8,128)(2,1)} %param.4) | copy-start | bytes 9437188
  51.8 4.6 %copy-start.1 = (s32[1,32]{1,0:T(1,128)S(1)}, s32[1,32]{1,0:T(1,128)}, u32[]{:S(2)}) copy-start(s32[1,32]{1,0:T(1,128)} %list_ref.1) | copy-start | bytes 388
  54.0 15.7 %copy-start.2 = (bf16[1,384,256]{2,1,0:T(8,128)(2,1)S(1)}, bf16[1,384,256]{2,1,0:T(8,128)(2,1)}, u32[]{:S(2)}) copy-start(bf16[1,384,256]{2,1,0:T(8,128)(2,1)} %param.5) | copy-start | bytes 589828
  54.0 15.7 %collective-permute-start.2 = (f32[584,128]{1,0:T(8,128)S(1)}, f32[584,128]{1,0:T(8,128)S(1)}, u32[]{:S(2)}, u32[]{:S(2)}) collective-permute-start(f32[584,128]{1,0:T(8,128)S(1)} %shard_map.48), channel_id=1, source_target_pairs={{0,16},{16,0},{1,17},{17,1},{2,18},{18,2},{3,19},{19,3},{4,20},{20... | collective-permute-start | bytes 897032 | tf_op jit(solution)/shard_map/ppermute | solution.py:297
  78.6 10.1 %collective-permute-start.3 = (bf16[384,256]{1,0:T(8,128)(2,1)S(1)}, bf16[384,256]{1,0:T(8,128)(2,1)S(1)}, u32[]{:S(2)}, u32[]{:S(2)}) collective-permute-start(bf16[384,256]{1,0:T(8,128)(2,1)S(1)} %shard_map.49), channel_id=1, source_target_pairs={{0,16},{16,0},{1,17},{17,1},{2,18},{18,2},{3,19},{19,3},{4,20},{20... | collective-permute-start | bytes 589832 | tf_op jit(solution)/shard_map/ppermute | solution.py:300

commit v5 on v4

--- a/solution.py
+++ b/solution.py
@@ -12,7 +12,7 @@
 LOADING = 0.1
 EDGE = 128
 STEP = 16
-PACKED = 4 * EDGE + EDGE // 2 + 8
+PACKED = (EDGE, 2 * EDGE, EDGE + EDGE // 2 + 8)
 INNER = ("inner", "doppler")
 EVERY = ("half",) + INNER
 VMEM_BYTES = 16 * 1024 * 1024
@@ -23,7 +23,7 @@
     return lax.broadcasted_iota(jnp.int32, (rows, EDGE), dim)
 
 
-def gram_kernel(which, base_ref, list_ref, count_ref, blocks_ref, out_ref, chosen):
+def gram_kernel(which, base_ref, list_ref, count_ref, blocks_ref, corner_ref, side_ref, late_ref, chosen):
     group, _, rows, size = blocks_ref.shape
     for p in range(list_ref.shape[1]):
         chosen[list_ref[0, p]] = (p < count_ref[0]).astype(jnp.int32)
@@ -43,17 +43,17 @@
     half = EDGE // 2
     r, c = edge_iota(0), edge_iota(1)
     zero, one, two = strip(0), strip(1), strip(2)
-    out_ref[pl.ds(0, EDGE), :] = zero[:, EDGE : 2 * EDGE]
-    out_ref[pl.ds(EDGE, EDGE), :] = zero[:, 2 * EDGE :]
-    out_ref[pl.ds(2 * EDGE, EDGE), :] = one[:, EDGE:]
-    out_ref[pl.ds(3 * EDGE, EDGE), :] = jnp.where(r <= c, zero[:, :EDGE], one[:, :EDGE])
+    corner_ref[...] = jnp.where(r <= c, zero[:, :EDGE], one[:, :EDGE])
+    side_ref[pl.ds(0, EDGE), :] = zero[:, EDGE : 2 * EDGE]
+    side_ref[pl.ds(EDGE, EDGE), :] = zero[:, 2 * EDGE :]
+    late_ref[pl.ds(0, EDGE), :] = one[:, EDGE:]
     low = pltpu.roll(two[half:], half, axis=1)
     rh, ch = r[:half], c[:half]
-    out_ref[pl.ds(4 * EDGE, half), :] = jnp.where((ch < half) & (rh > ch), low, two[:half])
+    late_ref[pl.ds(EDGE, half), :] = jnp.where((ch < half) & (rh > ch), low, two[:half])
     first = jnp.sum(jnp.where(r == c, one[:, :EDGE], 0.0), axis=0, keepdims=True)
     second = jnp.sum(jnp.where(rh == ch, low, 0.0), axis=0, keepdims=True)
     s = edge_iota(0, 8)
-    out_ref[pl.ds(4 * EDGE + half, 8), :] = jnp.where(s == 0, first, jnp.where(s == 1, second, 0.0))
+    late_ref[pl.ds(EDGE + half, 8), :] = jnp.where(s == 0, first, jnp.where(s == 1, second, 0.0))
 
 
 def partial_gram(which, base, lists, counts, blocks):
@@ -62,9 +62,9 @@
     vmem = pl.BlockSpec(memory_space=pltpu.VMEM)
     return pl.pallas_call(
         functools.partial(gram_kernel, which),
-        out_shape=jax.ShapeDtypeStruct((PACKED, EDGE), jnp.float32),
+        out_shape=[jax.ShapeDtypeStruct((n, EDGE), jnp.float32) for n in PACKED],
         in_specs=[smem, smem, smem, vmem],
-        out_specs=vmem,
+        out_specs=[vmem] * len(PACKED),
         scratch_shapes=[pltpu.SMEM((lists.shape[1],), jnp.int32)],
         compiler_params=pltpu.CompilerParams(vmem_limit_bytes=3 * VMEM_BYTES),
         cost_estimate=pl.CostEstimate(
@@ -75,30 +75,18 @@
     )(base, lists, counts, blocks)
 
 
-def unpack(packed):
+def unpack_late(both, late):
     half = EDGE // 2
     r, c = edge_iota(0), edge_iota(1)
-    both = packed[3 * EDGE : 4 * EDGE]
-    turned = both.T
-    diag = packed[4 * EDGE + half : 4 * EDGE + half + 8]
-    zero = jnp.where(r <= c, both, turned)
-    one = jnp.where(r > c, both, jnp.where(r < c, turned, diag[0:1]))
-    top = packed[4 * EDGE : 4 * EDGE + half]
+    diag = late[EDGE + half :]
+    one = jnp.where(r > c, both, jnp.where(r < c, both.T, diag[0:1]))
+    top = late[EDGE : EDGE + half]
     side = jnp.concatenate([top, jnp.zeros_like(top)], axis=0).T
     rh, ch = r[:half], c[:half]
     upper = jnp.where((ch < half) & (rh > ch), side[:half], top)
-    low = jnp.where(
-        rh > ch,
-        top,
-        jnp.where(rh < ch, side[:half], diag[1:2]),
-    )
+    low = jnp.where(rh > ch, top, jnp.where(rh < ch, side[:half], diag[1:2]))
     lower = jnp.where(ch < half, side[half:], pltpu.roll(low, half, axis=1))
-    two = jnp.concatenate([upper, lower], axis=0)
-    return [
-        jnp.concatenate([zero, packed[:EDGE], packed[EDGE : 2 * EDGE]], axis=1),
-        jnp.concatenate([one, packed[2 * EDGE : 3 * EDGE]], axis=1),
-        two,
-    ]
+    return [one, late[:EDGE]], [jnp.concatenate([upper, lower], axis=0)]
 
 
 def fine(a, b, dims=(((1,), (0,)), ((), ()))):
@@ -191,61 +179,102 @@
     return jnp.concatenate(strips, axis=0)
 
 
-def solve_kernel(count_ref, own_ref, other_ref, steer_ref, out_ref):
-    size, beams = steer_ref.shape
-    parts = size // EDGE
+TURNED = (((0,), (0,)), ((), ()))
+
+
+def covariance_blocks(row, count_ref):
     inv_scale = 1.0 / (BLOCK * count_ref[0]).astype(jnp.float32)
-    strips = unpack(own_ref[...] + other_ref[...])
-    loading = jnp.where(edge_iota(0) == edge_iota(1), LOADING, 0.0)
-    rest = []
-    for i in range(parts):
-        row = [strips[i][:, j * EDGE : (j + 1) * EDGE] * inv_scale for j in range(parts - i)]
-        row[0] = row[0] + loading
-        rest.append(row)
-    right = [steer_ref[pl.ds(i * EDGE, EDGE), :].astype(jnp.float32) for i in range(parts)]
-    turned = (((0,), (0,)), ((), ()))
-    made = []
-    for i in range(parts):
-        diag = rest[i][0]
-        minus = negative_inverse([diag[q : q + STEP] for q in range(0, EDGE, STEP)])
-        lhs = rest[i][1:]
-        plus = [None] * len(lhs)
-        for j in range(len(lhs)):
-            plus[j] = -fine(minus, lhs[j])
-            if j == 0:
-                rest[i + 1][0] = rest[i + 1][0] - fine(lhs[0], plus[0], turned)
-        last = -fine(minus, right[i])
-        for j in range(len(lhs)):
-            for k in range(j, len(lhs)):
-                if k > 0:
-                    rest[i + 1 + j][k - j] = rest[i + 1 + j][k - j] - fine(lhs[j], plus[k], turned)
-            right[i + 1 + j] = right[i + 1 + j] - fine(lhs[j], last, turned)
-        made.append((plus, last))
-    found = [None] * parts
-    for i in reversed(range(parts)):
-        plus, x = made[i]
-        for j, p in enumerate(plus):
-            x = x - fine(p, found[i + 1 + j])
-        found[i] = x
+    row = [x * inv_scale for x in row]
+    row[0] = row[0] + jnp.where(edge_iota(0) == edge_iota(1), LOADING, 0.0)
+    return row
+
+
+def minus_inverse(block):
+    return negative_inverse([block[q : q + STEP] for q in range(0, EDGE, STEP)])
+
+
+def corner_kernel(count_ref, own_ref, other_ref, minus_ref):
+    both = own_ref[...] + other_ref[...]
+    block = jnp.where(edge_iota(0) <= edge_iota(1), both, both.T)
+    minus_ref[...] = minus_inverse(covariance_blocks([block], count_ref)[0])
+
+
+def side_kernel(count_ref, own_ref, other_ref, steer_ref, minus_ref, made_ref, less_ref):
+    inv_scale = 1.0 / (BLOCK * count_ref[0]).astype(jnp.float32)
+    side = (own_ref[...] + other_ref[...]) * inv_scale
+    near, far = side[:EDGE], side[EDGE:]
+    right = steer_ref[pl.ds(0, EDGE), :].astype(jnp.float32)
+    made = -fine(minus_ref[...], jnp.concatenate([near, far, right], axis=1))
+    made_ref[...] = made
+    less_ref[0] = fine(near, made, TURNED)
+    less_ref[1] = fine(far, made, TURNED)
+
+
+def late_kernel(
+    count_ref, own_corner, other_corner, own_late, other_late, steer_ref, made_ref, less_ref, out_ref
+):
+    size = steer_ref.shape[0]
+    strips = unpack_late(
+        own_corner[...] + other_corner[...], own_late[...] + other_late[...]
+    )
+    one, two = [covariance_blocks(list(x), count_ref) for x in strips]
+    one = [x - less_ref[0, :, pl.ds(i * EDGE, EDGE)] for i, x in enumerate(one)]
+    right = [
+        steer_ref[pl.ds(i * EDGE, EDGE), :].astype(jnp.float32) - less_ref[i - 1, :, 2 * EDGE :]
+        for i in (1, 2)
+    ]
+    minus = minus_inverse(one[0])
+    step = -fine(minus, one[1])
+    left = two[0] - less_ref[1, :, pl.ds(EDGE, EDGE)] - fine(one[1], step, TURNED)
+    middle = -fine(minus, right[0])
+    last = right[1] - fine(one[1], middle, TURNED)
+    found = [None, None, -fine(minus_inverse(left), last)]
+    found[1] = middle - fine(step, found[2])
+    made = made_ref[...]
+    found[0] = (
+        made[:, 2 * EDGE :] - fine(made[:, :EDGE], found[1]) - fine(made[:, EDGE : 2 * EDGE], found[2])
+    )
     response = 0.0
-    for i in range(parts):
+    for i in range(size // EDGE):
         steer = steer_ref[pl.ds(i * EDGE, EDGE), :].astype(jnp.float32)
         response = response + jnp.sum(steer * found[i], axis=0, keepdims=True)
-    for i in range(parts):
+    for i in range(size // EDGE):
         out_ref[pl.ds(i * EDGE, EDGE), :] = (found[i] / response).astype(out_ref.dtype)
 
 
 def make_weights(count, own, other, steering):
     size, beams = steering.shape
+    smem = pl.BlockSpec(memory_space=pltpu.SMEM)
     vmem = pl.BlockSpec(memory_space=pltpu.VMEM)
+    wide = 2 * EDGE + beams
+    params = pltpu.CompilerParams(vmem_limit_bytes=VMEM_BYTES)
+    minus = pl.pallas_call(
+        corner_kernel,
+        out_shape=jax.ShapeDtypeStruct((EDGE, EDGE), jnp.float32),
+        in_specs=[smem, vmem, vmem],
+        out_specs=vmem,
+        compiler_params=params,
+        cost_estimate=pl.CostEstimate(flops=10**9, bytes_accessed=10**6, transcendentals=0),
+    )(count, own[0], other[0])
+    made, less = pl.pallas_call(
+        side_kernel,
+        out_shape=[
+            jax.ShapeDtypeStruct((EDGE, wide), jnp.float32),
+            jax.ShapeDtypeStruct((2, EDGE, wide), jnp.float32),
+        ],
+        in_specs=[smem, vmem, vmem, vmem, vmem],
+        out_specs=[vmem, vmem],
+        compiler_params=params,
+        cost_estimate=pl.CostEstimate(flops=10**9, bytes_accessed=10**6, transcendentals=0),
+    )(count, own[1], other[1], steering, minus)
     return pl.pallas_call(
-        solve_kernel,
+        late_kernel,
         out_shape=jax.ShapeDtypeStruct((size, beams), jnp.bfloat16),
-        in_specs=[pl.BlockSpec(memory_space=pltpu.SMEM), vmem, vmem, vmem],
+        in_specs=[smem] + [vmem] * 7,
         out_specs=vmem,
-        compiler_params=pltpu.CompilerParams(vmem_limit_bytes=VMEM_BYTES),
+        compiler_params=params,
         cost_estimate=pl.CostEstimate(flops=10**9, bytes_accessed=2 * 10**6, transcendentals=0),
-    )(count, own, other, steering)
+    )(count, own[0], other[0], own[2], other[2], steering, made, less)
 
 
 def split_kernel(which_ref, x_ref, out_ref):
@@ -294,7 +323,7 @@
     blocks = exchange(outgoing)
 
     other_gram = partial_gram(1, base, other_list, other_count, blocks)
-    arrived = lax.ppermute(other_gram, "half", peers)
+    arrived = [lax.ppermute(x, "half", peers) for x in other_gram]
     own_gram = partial_gram(0, base, train_list, train_count, blocks)
     weights = make_weights(train_count, own_gram, arrived, steering[0])
     other_weights = lax.ppermute(weights, "half", peers)

time: 122 us -> 120 us (0.984)
  waiting for transfers between devices: 22.4 us -> 17.1 us
  starting transfers between devices: 5.91 us -> 8.75 us
    ppermute x1 -> x3, waiting for transfers between devices: 11.8 us -> 6.06 us  [body(): arrived = [lax.ppermute(x, 'half', peers) for x in other_gram]]
    ppermute x1 -> x3, starting transfers between devices: 1.77 us -> 4.61 us  [body(): arrived = [lax.ppermute(x, 'half', peers) for x in other_gram]]
    pallas_call x3 -> x5, Pallas kernels: 12.5 us -> 12.7 us  [the longest x1 6.07 us: make_weights(): pl.pallas_call(late_kernel, out_shape=jax.ShapeDtypeStruct((size, beams),...]
  transfers between devices with their start and end apart: 4 -> 6, of which waited for: 3 -> 5; matrix products, arithmetic and copies ran while one was open for 1% -> 1% of each run, Pallas kernels for 2% -> 5%
where the time goes in v5:
time: 120 us; the launch traced here: 119 us
  blocking collectives  73.3 us (61%)
  waiting for transfers between devices  17.1 us (14%)
  Pallas kernels  14 us (12%)
  starting transfers between devices  8.75 us (7%)
  local copies, waits for them, and re-layouts  2.24 us (2%)
  other arithmetic  1.77 us (1%)
  matrix products  1.4 us (1%)
    all_to_all x2, blocking collectives, exchange(): return lax.all_to_all(x, INNER, split_axis=0, concat_axis=0, tiled=True)  73.3 us
    ppermute x1, waiting for transfers between devices, body(): other_weights = lax.ppermute(weights, 'half', peers)  9.7 us
    pallas_call x1, Pallas kernels, make_weights(): pl.pallas_call(late_kernel, out_shape=jax.ShapeDtypeStruct((size, beams),...  6.07 us
    ppermute x3, waiting for transfers between devices, body(): arrived = [lax.ppermute(x, 'half', peers) for x in other_gram]  6.06 us
    ppermute x3, starting transfers between devices, body(): arrived = [lax.ppermute(x, 'half', peers) for x in other_gram]  4.61 us
    ppermute x1, starting transfers between devices, body(): other_list = lax.ppermute(train_list, 'half', peers)  4.04 us
    pallas_call x2, Pallas kernels, partial_gram(): pl.pallas_call(functools.partial(gram_kernel, which), out_shape=[jax.Shap...  3.45 us
  transfers between devices with their start and end apart: 6, of which 5 were waited for; matrix products, arithmetic and copies ran while one was open for 1% of the time, Pallas kernels for 5%

profile of v5, /device:TPU:0, one launch (start us, length us, event | category | flops | bytes accessed | tf_op | source)
XLA Modules:
  0.0 119.3 jit_solution(8489217243807967111)
XLA Ops:
  0.0 4.0 %collective-permute-start = (s32[1,32]{1,0:T(1,128)}, s32[1,32]{1,0:T(1,128)S(1)}, u32[]{:S(2)}, u32[]{:S(2)}) collective-permute-start(s32[1,32]{1,0:T(1,128)} %list_ref.1), channel_id=1, source_target_pairs={{0,16},{16,0},{1,17},{17,1},{2,18},{18,2},{3,19},{19,3},{4,20},{20... | collective-permute-start | bytes 392 | tf_op jit(solution)/shard_map/ppermute | solution.py:317
  4.0 0.0 collective-permute-start.1
  4.1 0.1 pad_add_fusion.which_ref
  4.1 0.0 copy-start
  4.1 1.9 %copy-done = bf16[32,128,384]{2,1,0:T(8,128)(2,1)S(1)} copy-done((bf16[32,128,384]{2,1,0:T(8,128)(2,1)S(1)}, bf16[32,128,384]{2,1,0:T(8,128)(2,1)}, u32[]{:S(2)}) %copy-start) | copy-done | bytes 3145752
  6.0 1.3 %shard_map.46 = bf16[16,2,128,384]{3,2,1,0:T(8,128)(2,1)S(1)} custom-call(s32[2]{0:T(128)S(1)} %pad_add_fusion.which_ref, bf16[2,16,128,384]{3,2,1,0:T(8,128)(2,1)S(1)} %bitcast.32), custom_call_target="tpu_custom_call" | custom-call | bytes 3145728 | tf_op jit(solution)/shard_map/pallas_call | solution.py:287
  7.4 1.4 %collective-permute-done.1.count_ref = s32[1]{0:T(128)} collective-permute-done((s32[1]{0:T(128)}, s32[1]{0:T(128)}, u32[]{:S(2)}, u32[]{:S(2)}) %collective-permute-start.1) | collective-permute-done | bytes 36 | tf_op jit(solution)/shard_map/ppermute | solution.py:318
  8.7 0.0 collective-permute-done.list_ref
  8.7 43.3 %all_to_all.10.blocks_ref = bf16[16,2,128,384]{3,2,1,0:T(8,128)(2,1)S(1)} all-to-all(bf16[16,2,128,384]{3,2,1,0:T(8,128)(2,1)S(1)} %shard_map.46), channel_id=1, replica_groups=mesh['half'=2,'inner'=4,'doppler'=4] {'inner','doppler'}, dimensions={0} | all-to-all | bytes 6291456 | tf_op jit(solution)/shard_map/all_to_all | solution.py:315
  52.0 2.0 %shard_map.48 = (f32[128,128]{1,0:T(8,128)S(1)}, f32[256,128]{1,0:T(8,128)S(1)}, f32[200,128]{1,0:T(8,128)S(1)}) custom-call(s32[1]{0:T(128)S(6)} %mul.3.base_ref, s32[1,32]{1,0:T(1,128)S(1)} %collective-permute-done.list_ref, s32[1]{0:T(128)} %collective-permute-done.1.count_ref, bf16[16,2,128,384]{3,2,1,0:T(8,128)(2,1)S(1)} %all_to_all.10.blocks_ref), custom_call_target="tpu_custom_call" | custom-call | flops 603979776 | bytes 1572864 | tf_op jit(solution)/shard_map/pallas_call | solution.py:63
  54.0 1.6 %collective-permute-start.2 = (f32[128,128]{1,0:T(8,128)S(1)}, f32[128,128]{1,0:T(8,128)S(1)}, u32[]{:S(2)}, u32[]{:S(2)}) collective-permute-start(f32[128,128]{1,0:T(8,128)S(1)} %get-tuple-element.25), channel_id=1, source_target_pairs={{0,16},{16,0},{1,17},{17,1},{2,18},{18,2},{3,19},{19,3},{4,20},{20... | collective-permute-start | bytes 196616 | tf_op jit(solution)/shard_map/ppermute | solution.py:326
  56.3 1.4 %collective-permute-start.4 = (f32[256,128]{1,0:T(8,128)S(1)}, f32[256,128]{1,0:T(8,128)S(1)}, u32[]{:S(2)}, u32[]{:S(2)}) collective-permute-start(f32[256,128]{1,0:T(8,128)S(1)} %get-tuple-element.29), channel_id=1, source_target_pairs={{0,16},{16,0},{1,17},{17,1},{2,18},{18,2},{3,19},{19,3},{4,20},{20... | collective-permute-start | bytes 393224 | tf_op jit(solution)/shard_map/ppermute | solution.py:326
  57.7 1.6 %collective-permute-start.3 = (f32[200,128]{1,0:T(8,128)S(1)}, f32[200,128]{1,0:T(8,128)S(1)}, u32[]{:S(2)}, u32[]{:S(2)}) collective-permute-start(f32[200,128]{1,0:T(8,128)S(1)} %get-tuple-element.27), channel_id=1, source_target_pairs={{0,16},{16,0},{1,17},{17,1},{2,18},{18,2},{3,19},{19,3},{4,20},{20... | collective-permute-start | bytes 307208 | tf_op jit(solution)/shard_map/ppermute | solution.py:326
  59.3 0.0 copy-done.1
  59.3 1.4 %shard_map.47 = (f32[128,128]{1,0:T(8,128)S(1)}, f32[256,128]{1,0:T(8,128)S(1)}, f32[200,128]{1,0:T(8,128)S(1)}) custom-call(s32[1]{0:T(128)S(6)} %mul.3.base_ref, s32[1,32]{1,0:T(1,128)S(1)} %copy-done.1, s32[1]{0:T(128)S(6)} %copy.6.count_ref, bf16[16,2,128,384]{3,2,1,0:T(8,128)(2,1)S(1)} %all_to_all.10.blocks_ref), custom_call_target="tpu_custom_call" | custom-call | flops 603979776 | bytes 1572864 | tf_op jit(solution)/shard_map/pallas_call | solution.py:63
  60.7 0.0 copy-start.2
  60.7 4.8 %collective-permute-done.2.other_ref.other_corner = f32[128,128]{1,0:T(8,128)S(1)} collective-permute-done((f32[128,128]{1,0:T(8,128)S(1)}, f32[128,128]{1,0:T(8,128)S(1)}, u32[]{:S(2)}, u32[]{:S(2)}) %collective-permute-start.2) | collective-permute-done | bytes 65568 | tf_op jit(solution)/shard_map/ppermute | solution.py:326
  65.5 2.2 %shard_map.49.minus_ref = f32[128,128]{1,0:T(8,128)S(1)} custom-call(s32[1]{0:T(128)S(6)} %copy.6.count_ref, f32[128,128]{1,0:T(8,128)S(1)} %get-tuple-element.22.own_ref.own_corner, f32[128,128]{1,0:T(8,128)S(1)} %collective-permute-done.2.other_ref.other_corner), custom_call_target="tpu_custom_call" | custom-call | flops 1000000000 | bytes 1000000 | tf_op jit(solution)/shard_map/pallas_call | solution.py:251
  67.8 0.6 collective-permute-done.4.other_ref
  68.3 0.0 copy-done.2
  68.3 0.9 shard_map.50
  69.3 0.7 collective-permute-done.3.other_late
  69.9 6.1 %shard_map.51 = bf16[384,256]{1,0:T(8,128)(2,1)S(1)} custom-call(s32[1]{0:T(128)S(6)} %copy.6.count_ref, f32[128,128]{1,0:T(8,128)S(1)} %get-tuple-element.22.own_ref.own_corner, f32[128,128]{1,0:T(8,128)S(1)} %collective-permute-done.2.other_ref.other_corner, f32[200,128]{1,0:T(8,128)S(1)} %get-tuple-element.26.own_late, ...), custom_call_target="tpu_custom_call" | custom-call | flops 1000000000 | bytes 2000000 | tf_op jit(solution)/shard_map/pallas_call | solution.py:270
  76.0 0.1 collective-permute-start.5
  76.1 0.7 fusion.5
  76.8 9.7 %collective-permute-done.5 = bf16[384,256]{1,0:T(8,128)(2,1)S(1)} collective-permute-done((bf16[384,256]{1,0:T(8,128)(2,1)S(1)}, bf16[384,256]{1,0:T(8,128)(2,1)S(1)}, u32[]{:S(2)}, u32[]{:S(2)}) %collective-permute-start.5) | collective-permute-done | bytes 196640 | tf_op jit(solution)/shard_map/ppermute | solution.py:329
  86.5 0.7 fusion.4
  87.2 0.2 pad_maximum_fusion
  87.4 0.2 copy.5
  87.6 30.0 %all_to_all.11 = bf16[16,2,128,256]{3,2,1,0:T(8,128)(2,1)S(1)} all-to-all(bf16[16,2,128,256]{3,2,1,0:T(8,128)(2,1)S(1)} %copy.5), channel_id=1, replica_groups=mesh['half'=2,'inner'=4,'doppler'=4] {'inner','doppler'}, dimensions={0} | all-to-all | bytes 4194304 | tf_op jit(solution)/shard_map/all_to_all | solution.py:315
  117.7 0.1 dynamic-slice_bitcast_fusion.1
  117.8 1.5 %pad_maximum_fusion.1 = bf16[32,128,256]{2,1,0:T(8,128)(2,1)} fusion(bf16[16,128,256]{2,1,0:T(8,128)(2,1)S(1)} %get-tuple-element.36, bf16[16,128,256]{2,1,0:T(8,128)(2,1)S(1)} %get-tuple-element.35), kind=kLoop, calls=%fused_computation.1 | loop fusion | flops 1048576 | bytes 4194304 | tf_op jit(solution)/shard_map/concatenate | solution.py:342
  (1 shorter events, 0.0 us)
Async XLA Ops:
  0.0 8.7 %collective-permute-start = (s32[1,32]{1,0:T(1,128)}, s32[1,32]{1,0:T(1,128)S(1)}, u32[]{:S(2)}, u32[]{:S(2)}) collective-permute-start(s32[1,32]{1,0:T(1,128)} %list_ref.1), channel_id=1, source_target_pairs={{0,16},{16,0},{1,17},{17,1},{2,18},{18,2},{3,19},{19,3},{4,20},{20... | collective-permute-start | bytes 392 | tf_op jit(solution)/shard_map/ppermute | solution.py:317
  4.0 4.7 %collective-permute-start.1 = (s32[1]{0:T(128)}, s32[1]{0:T(128)}, u32[]{:S(2)}, u32[]{:S(2)}) collective-permute-start(s32[1]{0:T(128)} %param.7), channel_id=1, source_target_pairs={{0,16},{16,0},{1,17},{17,1},{2,18},{18,2},{3,19},{19,3},{4,20},{20... | collective-permute-start | bytes 20 | tf_op jit(solution)/shard_map/ppermute | solution.py:318
  4.1 1.9 %copy-start = (bf16[32,128,384]{2,1,0:T(8,128)(2,1)S(1)}, bf16[32,128,384]{2,1,0:T(8,128)(2,1)}, u32[]{:S(2)}) copy-start(bf16[32,128,384]{2,1,0:T(8,128)(2,1)} %param.4) | copy-start | bytes 9437188
  52.0 7.3 %copy-start.1 = (s32[1,32]{1,0:T(1,128)S(1)}, s32[1,32]{1,0:T(1,128)}, u32[]{:S(2)}) copy-start(s32[1,32]{1,0:T(1,128)} %list_ref.1) | copy-start | bytes 388
  54.0 11.5 %collective-permute-start.2 = (f32[128,128]{1,0:T(8,128)S(1)}, f32[128,128]{1,0:T(8,128)S(1)}, u32[]{:S(2)}, u32[]{:S(2)}) collective-permute-start(f32[128,128]{1,0:T(8,128)S(1)} %get-tuple-element.25), channel_id=1, source_target_pairs={{0,16},{16,0},{1,17},{17,1},{2,18},{18,2},{3,19},{19,3},{4,20},{20... | collective-permute-start | bytes 196616 | tf_op jit(solution)/shard_map/ppermute | solution.py:326
  56.3 12.1 %collective-permute-start.4 = (f32[256,128]{1,0:T(8,128)S(1)}, f32[256,128]{1,0:T(8,128)S(1)}, u32[]{:S(2)}, u32[]{:S(2)}) collective-permute-start(f32[256,128]{1,0:T(8,128)S(1)} %get-tuple-element.29), channel_id=1, source_target_pairs={{0,16},{16,0},{1,17},{17,1},{2,18},{18,2},{3,19},{19,3},{4,20},{20... | collective-permute-start | bytes 393224 | tf_op jit(solution)/shard_map/ppermute | solution.py:326
  57.7 12.2 %collective-permute-start.3 = (f32[200,128]{1,0:T(8,128)S(1)}, f32[200,128]{1,0:T(8,128)S(1)}, u32[]{:S(2)}, u32[]{:S(2)}) collective-permute-start(f32[200,128]{1,0:T(8,128)S(1)} %get-tuple-element.27), channel_id=1, source_target_pairs={{0,16},{16,0},{1,17},{17,1},{2,18},{18,2},{3,19},{19,3},{4,20},{20... | collective-permute-start | bytes 307208 | tf_op jit(solution)/shard_map/ppermute | solution.py:326
  60.7 7.6 %copy-start.2 = (bf16[1,384,256]{2,1,0:T(8,128)(2,1)S(1)}, bf16[1,384,256]{2,1,0:T(8,128)(2,1)}, u32[]{:S(2)}) copy-start(bf16[1,384,256]{2,1,0:T(8,128)(2,1)} %param.5) | copy-start | bytes 589828
  76.0 10.5 %collective-permute-start.5 = (bf16[384,256]{1,0:T(8,128)(2,1)S(1)}, bf16[384,256]{1,0:T(8,128)(2,1)S(1)}, u32[]{:S(2)}, u32[]{:S(2)}) collective-permute-start(bf16[384,256]{1,0:T(8,128)(2,1)S(1)} %shard_map.51), channel_id=1, source_target_pairs={{0,16},{16,0},{1,17},{17,1},{2,18},{18,2},{3,19},{19,3},{4,20},{20... | collective-permute-start | bytes 589832 | tf_op jit(solution)/shard_map/ppermute | solution.py:329

commit v6 on v5

--- a/solution.py
+++ b/solution.py
@@ -12,7 +12,7 @@
 LOADING = 0.1
 EDGE = 128
 STEP = 16
-PACKED = (EDGE, 2 * EDGE, EDGE + EDGE // 2 + 8)
+PACKED = (EDGE, 2 * EDGE + 8, EDGE + EDGE // 2)
 INNER = ("inner", "doppler")
 EVERY = ("half",) + INNER
 VMEM_BYTES = 16 * 1024 * 1024
@@ -53,7 +53,7 @@
     first = jnp.sum(jnp.where(r == c, one[:, :EDGE], 0.0), axis=0, keepdims=True)
     second = jnp.sum(jnp.where(rh == ch, low, 0.0), axis=0, keepdims=True)
     s = edge_iota(0, 8)
-    late_ref[pl.ds(EDGE + half, 8), :] = jnp.where(s == 0, first, jnp.where(s == 1, second, 0.0))
+    side_ref[pl.ds(2 * EDGE, 8), :] = jnp.where(s == 0, first, jnp.where(s == 1, second, 0.0))
 
 
 def partial_gram(which, base, lists, counts, blocks):
@@ -75,18 +75,15 @@
     )(base, lists, counts, blocks)
 
 
-def unpack_late(both, late):
+def unpack_late(late, diag):
     half = EDGE // 2
-    r, c = edge_iota(0), edge_iota(1)
-    diag = late[EDGE + half :]
-    one = jnp.where(r > c, both, jnp.where(r < c, both.T, diag[0:1]))
-    top = late[EDGE : EDGE + half]
+    r, c = edge_iota(0, half), edge_iota(1, half)
+    top = late[EDGE:]
     side = jnp.concatenate([top, jnp.zeros_like(top)], axis=0).T
-    rh, ch = r[:half], c[:half]
-    upper = jnp.where((ch < half) & (rh > ch), side[:half], top)
-    low = jnp.where(rh > ch, top, jnp.where(rh < ch, side[:half], diag[1:2]))
-    lower = jnp.where(ch < half, side[half:], pltpu.roll(low, half, axis=1))
-    return [one, late[:EDGE]], [jnp.concatenate([upper, lower], axis=0)]
+    upper = jnp.where((c < half) & (r > c), side[:half], top)
+    low = jnp.where(r > c, top, jnp.where(r < c, side[:half], diag))
+    lower = jnp.where(c < half, side[half:], pltpu.roll(low, half, axis=1))
+    return late[:EDGE], jnp.concatenate([upper, lower], axis=0)
 
 
 def fine(a, b, dims=(((1,), (0,)), ((), ()))):
@@ -182,11 +179,12 @@
 TURNED = (((0,), (0,)), ((), ()))
 
 
-def covariance_blocks(row, count_ref):
-    inv_scale = 1.0 / (BLOCK * count_ref[0]).astype(jnp.float32)
-    row = [x * inv_scale for x in row]
-    row[0] = row[0] + jnp.where(edge_iota(0) == edge_iota(1), LOADING, 0.0)
-    return row
+def inverse_scale(count_ref):
+    return 1.0 / (BLOCK * count_ref[0]).astype(jnp.float32)
+
+
+def loading():
+    return jnp.where(edge_iota(0) == edge_iota(1), LOADING, 0.0)
 
 
 def minus_inverse(block):
@@ -196,85 +194,94 @@
 def corner_kernel(count_ref, own_ref, other_ref, minus_ref):
     both = own_ref[...] + other_ref[...]
     block = jnp.where(edge_iota(0) <= edge_iota(1), both, both.T)
-    minus_ref[...] = minus_inverse(covariance_blocks([block], count_ref)[0])
-
-
-def side_kernel(count_ref, own_ref, other_ref, steer_ref, minus_ref, made_ref, less_ref):
-    inv_scale = 1.0 / (BLOCK * count_ref[0]).astype(jnp.float32)
-    side = (own_ref[...] + other_ref[...]) * inv_scale
-    near, far = side[:EDGE], side[EDGE:]
+    minus_ref[...] = minus_inverse(block * inverse_scale(count_ref) + loading())
+
+
+def side_kernel(
+    count_ref, own_corner, other_corner, own_ref, other_ref, steer_ref, minus_ref,
+    made_ref, less_ref, next_ref,
+):
+    inv_scale = inverse_scale(count_ref)
+    side = own_ref[...] + other_ref[...]
+    near, far = side[:EDGE] * inv_scale, side[EDGE : 2 * EDGE] * inv_scale
+    minus = minus_ref[...]
+    r, c = edge_iota(0), edge_iota(1)
+    both = own_corner[...] + other_corner[...]
+    diag = side[2 * EDGE : 2 * EDGE + 1]
+    block = jnp.where(r > c, both, jnp.where(r < c, both.T, diag)) * inv_scale + loading()
+    close = -fine(minus, near)
+    taken = fine(near, close, TURNED)
+    next_ref[...] = minus_inverse(block - taken)
     right = steer_ref[pl.ds(0, EDGE), :].astype(jnp.float32)
-    made = -fine(minus_ref[...], jnp.concatenate([near, far, right], axis=1))
-    made_ref[...] = made
+    made = -fine(minus, jnp.concatenate([far, right], axis=1))
+    made_ref[:, :EDGE] = close
+    made_ref[:, EDGE:] = made
     less_ref[0] = fine(near, made, TURNED)
     less_ref[1] = fine(far, made, TURNED)
 
 
 def late_kernel(
-    count_ref, own_corner, other_corner, own_late, other_late, steer_ref, made_ref, less_ref, out_ref
+    count_ref, own_late, other_late, own_side, other_side, steer_ref, made_ref, less_ref,
+    minus_ref, out_ref,
 ):
-    size = steer_ref.shape[0]
-    strips = unpack_late(
-        own_corner[...] + other_corner[...], own_late[...] + other_late[...]
-    )
-    one, two = [covariance_blocks(list(x), count_ref) for x in strips]
-    one = [x - less_ref[0, :, pl.ds(i * EDGE, EDGE)] for i, x in enumerate(one)]
+    size, beams = steer_ref.shape
+    parts = size // EDGE
+    inv_scale = inverse_scale(count_ref)
+    diag = own_side[pl.ds(2 * EDGE, 8), :] + other_side[pl.ds(2 * EDGE, 8), :]
+    near, block = unpack_late(own_late[...] + other_late[...], diag[1:2])
+    near = near * inv_scale - less_ref[0, :, :EDGE]
+    block = block * inv_scale + loading() - less_ref[1, :, :EDGE]
+    minus = minus_ref[...]
+    step = -fine(minus, near)
+    block = block - fine(near, step, TURNED)
     right = [
-        steer_ref[pl.ds(i * EDGE, EDGE), :].astype(jnp.float32) - less_ref[i - 1, :, 2 * EDGE :]
+        steer_ref[pl.ds(i * EDGE, EDGE), :].astype(jnp.float32) - less_ref[i - 1, :, EDGE:]
         for i in (1, 2)
     ]
-    minus = minus_inverse(one[0])
-    step = -fine(minus, one[1])
-    left = two[0] - less_ref[1, :, pl.ds(EDGE, EDGE)] - fine(one[1], step, TURNED)
     middle = -fine(minus, right[0])
-    last = right[1] - fine(one[1], middle, TURNED)
-    found = [None, None, -fine(minus_inverse(left), last)]
-    found[1] = middle - fine(step, found[2])
+    last = right[1] - fine(near, middle, TURNED)
     made = made_ref[...]
-    found[0] = (
-        made[:, 2 * EDGE :] - fine(made[:, :EDGE], found[1]) - fine(made[:, EDGE : 2 * EDGE], found[2])
-    )
-    response = 0.0
-    for i in range(size // EDGE):
-        steer = steer_ref[pl.ds(i * EDGE, EDGE), :].astype(jnp.float32)
-        response = response + jnp.sum(steer * found[i], axis=0, keepdims=True)
-    for i in range(size // EDGE):
-        out_ref[pl.ds(i * EDGE, EDGE), :] = (found[i] / response).astype(out_ref.dtype)
+    close, far, right = made[:, :EDGE], made[:, EDGE : 2 * EDGE], made[:, 2 * EDGE :]
+    base = jnp.concatenate([right - fine(close, middle), middle], axis=0)
+    turn = jnp.concatenate([far - fine(close, step), step], axis=0)
+    x = -fine(minus_inverse(block), last)
+    found = jnp.concatenate([base - fine(turn, x), x], axis=0)
+    response = jnp.sum(steer_ref[...].astype(jnp.float32) * found, axis=0, keepdims=True)
+    out_ref[...] = (found / response).astype(out_ref.dtype)
 
 
 def make_weights(count, own, other, steering):
     size, beams = steering.shape
     smem = pl.BlockSpec(memory_space=pltpu.SMEM)
     vmem = pl.BlockSpec(memory_space=pltpu.VMEM)
-    wide = 2 * EDGE + beams
-    params = pltpu.CompilerParams(vmem_limit_bytes=VMEM_BYTES)
-    minus = pl.pallas_call(
-        corner_kernel,
-        out_shape=jax.ShapeDtypeStruct((EDGE, EDGE), jnp.float32),
-        in_specs=[smem, vmem, vmem],
-        out_specs=vmem,
-        compiler_params=params,
-        cost_estimate=pl.CostEstimate(flops=10**9, bytes_accessed=10**6, transcendentals=0),
-    )(count, own[0], other[0])
-    made, less = pl.pallas_call(
+    wide = EDGE + beams
+    square = jax.ShapeDtypeStruct((EDGE, EDGE), jnp.float32)
+
+    def call(kernel, out_shape, *args):
+        return pl.pallas_call(
+            kernel,
+            out_shape=out_shape,
+            in_specs=[smem] + [vmem] * len(args),
+            out_specs=jax.tree.map(lambda _: vmem, out_shape),
+            compiler_params=pltpu.CompilerParams(vmem_limit_bytes=VMEM_BYTES),
+            cost_estimate=pl.CostEstimate(flops=10**9, bytes_accessed=10**6, transcendentals=0),
+        )(count, *args)
+
+    corner = call(corner_kernel, square, own[0], other[0])
+    made, less, second = call(
         side_kernel,
-        out_shape=[
-            jax.ShapeDtypeStruct((EDGE, wide), jnp.float32),
+        [
+            jax.ShapeDtypeStruct((EDGE, EDGE + wide), jnp.float32),
             jax.ShapeDtypeStruct((2, EDGE, wide), jnp.float32),
+            square,
         ],
-        in_specs=[smem, vmem, vmem, vmem, vmem],
-        out_specs=[vmem, vmem],
-        compiler_params=params,
-        cost_estimate=pl.CostEstimate(flops=10**9, bytes_accessed=10**6, transcendentals=0),
-    )(count, own[1], other[1], steering, minus)
-    return pl.pallas_call(
+        own[0], other[0], own[1], other[1], steering, corner,
+    )
+    return call(
         late_kernel,
-        out_shape=jax.ShapeDtypeStruct((size, beams), jnp.bfloat16),
-        in_specs=[smem] + [vmem] * 7,
-        out_specs=vmem,
-        compiler_params=params,
-        cost_estimate=pl.CostEstimate(flops=10**9, bytes_accessed=2 * 10**6, transcendentals=0),
-    )(count, own[0], other[0], own[2], other[2], steering, made, less)
+        jax.ShapeDtypeStruct((size, beams), jnp.bfloat16),
+        own[2], other[2], own[1], other[1], steering, made, less, second,
+    )
 
 
 def split_kernel(which_ref, x_ref, out_ref):

time: 120 us -> 118 us (0.983)
  transfers between devices with their start and end apart: 6 -> 6, of which waited for: 5 -> 4; matrix products, arithmetic and copies ran while one was open for 1% -> 1% of each run, Pallas kernels for 5% -> 7%
where the time goes in v6:
time: 118 us
  blocking collectives  73.3 us (62%)
  waiting for transfers between devices  16 us (14%)
  Pallas kernels  14.1 us (12%)
  starting transfers between devices  8.75 us (7%)
  local copies, waits for them, and re-layouts  2.24 us (2%)
  other arithmetic  1.77 us (2%)
  matrix products  1.4 us (1%)
    all_to_all x2, blocking collectives, exchange(): return lax.all_to_all(x, INNER, split_axis=0, concat_axis=0, tiled=True)  73.3 us
    pallas_call x3, Pallas kernels, call(): pl.pallas_call(kernel, out_shape=out_shape, in_specs=[smem] + [vmem] * le...  9.32 us
    ppermute x1, waiting for transfers between devices, body(): other_weights = lax.ppermute(weights, 'half', peers)  9.1 us
    ppermute x3, waiting for transfers between devices, body(): arrived = [lax.ppermute(x, 'half', peers) for x in other_gram]  5.48 us
    ppermute x3, starting transfers between devices, body(): arrived = [lax.ppermute(x, 'half', peers) for x in other_gram]  4.61 us
    ppermute x1, starting transfers between devices, body(): other_list = lax.ppermute(train_list, 'half', peers)  4.04 us
    pallas_call x2, Pallas kernels, partial_gram(): pl.pallas_call(functools.partial(gram_kernel, which), out_shape=[jax.Shap...  3.45 us
  transfers between devices with their start and end apart: 6, of which 4 were waited for; matrix products, arithmetic and copies ran while one was open for 1% of the time, Pallas kernels for 7%

profile of v6, /device:TPU:0, one launch (start us, length us, event | category | flops | bytes accessed | tf_op | source)
XLA Modules:
  0.0 118.3 jit_solution(15198822436774927503)
XLA Ops:
  0.0 4.0 %collective-permute-start = (s32[1,32]{1,0:T(1,128)}, s32[1,32]{1,0:T(1,128)S(1)}, u32[]{:S(2)}, u32[]{:S(2)}) collective-permute-start(s32[1,32]{1,0:T(1,128)} %list_ref.1), channel_id=1, source_target_pairs={{0,16},{16,0},{1,17},{17,1},{2,18},{18,2},{3,19},{19,3},{4,20},{20... | collective-permute-start | bytes 392 | tf_op jit(solution)/shard_map/ppermute | solution.py:324
  4.0 0.0 collective-permute-start.1
  4.1 0.1 pad_add_fusion.which_ref
  4.1 0.0 copy-start
  4.1 1.9 %copy-done = bf16[32,128,384]{2,1,0:T(8,128)(2,1)S(1)} copy-done((bf16[32,128,384]{2,1,0:T(8,128)(2,1)S(1)}, bf16[32,128,384]{2,1,0:T(8,128)(2,1)}, u32[]{:S(2)}) %copy-start) | copy-done | bytes 3145752
  6.0 1.3 %shard_map.46 = bf16[16,2,128,384]{3,2,1,0:T(8,128)(2,1)S(1)} custom-call(s32[2]{0:T(128)S(1)} %pad_add_fusion.which_ref, bf16[2,16,128,384]{3,2,1,0:T(8,128)(2,1)S(1)} %bitcast.32), custom_call_target="tpu_custom_call" | custom-call | bytes 3145728 | tf_op jit(solution)/shard_map/pallas_call | solution.py:294
  7.4 1.4 %collective-permute-done.1.count_ref = s32[1]{0:T(128)} collective-permute-done((s32[1]{0:T(128)}, s32[1]{0:T(128)}, u32[]{:S(2)}, u32[]{:S(2)}) %collective-permute-start.1) | collective-permute-done | bytes 36 | tf_op jit(solution)/shard_map/ppermute | solution.py:325
  8.7 0.0 collective-permute-done.list_ref
  8.7 43.3 %all_to_all.10.blocks_ref = bf16[16,2,128,384]{3,2,1,0:T(8,128)(2,1)S(1)} all-to-all(bf16[16,2,128,384]{3,2,1,0:T(8,128)(2,1)S(1)} %shard_map.46), channel_id=1, replica_groups=mesh['half'=2,'inner'=4,'doppler'=4] {'inner','doppler'}, dimensions={0} | all-to-all | bytes 6291456 | tf_op jit(solution)/shard_map/all_to_all | solution.py:322
  52.0 2.0 %shard_map.48 = (f32[128,128]{1,0:T(8,128)S(1)}, f32[264,128]{1,0:T(8,128)S(1)}, f32[192,128]{1,0:T(8,128)S(1)}) custom-call(s32[1]{0:T(128)S(6)} %mul.3.base_ref, s32[1,32]{1,0:T(1,128)S(1)} %collective-permute-done.list_ref, s32[1]{0:T(128)} %collective-permute-done.1.count_ref, bf16[16,2,128,384]{3,2,1,0:T(8,128)(2,1)S(1)} %all_to_all.10.blocks_ref), custom_call_target="tpu_custom_call" | custom-call | flops 603979776 | bytes 1572864 | tf_op jit(solution)/shard_map/pallas_call | solution.py:63
  54.0 1.6 %collective-permute-start.4 = (f32[128,128]{1,0:T(8,128)S(1)}, f32[128,128]{1,0:T(8,128)S(1)}, u32[]{:S(2)}, u32[]{:S(2)}) collective-permute-start(f32[128,128]{1,0:T(8,128)S(1)} %get-tuple-element.30), channel_id=1, source_target_pairs={{0,16},{16,0},{1,17},{17,1},{2,18},{18,2},{3,19},{19,3},{4,20},{20... | collective-permute-start | bytes 196616 | tf_op jit(solution)/shard_map/ppermute | solution.py:333
  56.3 1.4 %collective-permute-start.3 = (f32[264,128]{1,0:T(8,128)S(1)}, f32[264,128]{1,0:T(8,128)S(1)}, u32[]{:S(2)}, u32[]{:S(2)}) collective-permute-start(f32[264,128]{1,0:T(8,128)S(1)} %get-tuple-element.28), channel_id=1, source_target_pairs={{0,16},{16,0},{1,17},{17,1},{2,18},{18,2},{3,19},{19,3},{4,20},{20... | collective-permute-start | bytes 405512 | tf_op jit(solution)/shard_map/ppermute | solution.py:333
  57.7 1.6 %collective-permute-start.2 = (f32[192,128]{1,0:T(8,128)S(1)}, f32[192,128]{1,0:T(8,128)S(1)}, u32[]{:S(2)}, u32[]{:S(2)}) collective-permute-start(f32[192,128]{1,0:T(8,128)S(1)} %get-tuple-element.26), channel_id=1, source_target_pairs={{0,16},{16,0},{1,17},{17,1},{2,18},{18,2},{3,19},{19,3},{4,20},{20... | collective-permute-start | bytes 294920 | tf_op jit(solution)/shard_map/ppermute | solution.py:333
  59.3 0.0 copy-done.1
  59.3 1.4 %shard_map.47 = (f32[128,128]{1,0:T(8,128)S(1)}, f32[264,128]{1,0:T(8,128)S(1)}, f32[192,128]{1,0:T(8,128)S(1)}) custom-call(s32[1]{0:T(128)S(6)} %mul.3.base_ref, s32[1,32]{1,0:T(1,128)S(1)} %copy-done.1, s32[1]{0:T(128)S(6)} %copy.6.count_ref, bf16[16,2,128,384]{3,2,1,0:T(8,128)(2,1)S(1)} %all_to_all.10.blocks_ref), custom_call_target="tpu_custom_call" | custom-call | flops 603979776 | bytes 1572864 | tf_op jit(solution)/shard_map/pallas_call | solution.py:63
  60.7 0.0 copy-start.2
  60.7 4.8 %collective-permute-done.4.other_ref.other_corner = f32[128,128]{1,0:T(8,128)S(1)} collective-permute-done((f32[128,128]{1,0:T(8,128)S(1)}, f32[128,128]{1,0:T(8,128)S(1)}, u32[]{:S(2)}, u32[]{:S(2)}) %collective-permute-start.4) | collective-permute-done | bytes 65568 | tf_op jit(solution)/shard_map/ppermute | solution.py:333
  65.5 2.2 %shard_map.49.minus_ref = f32[128,128]{1,0:T(8,128)S(1)} custom-call(s32[1]{0:T(128)S(6)} %copy.6.count_ref, f32[128,128]{1,0:T(8,128)S(1)} %get-tuple-element.29.own_ref.own_corner, f32[128,128]{1,0:T(8,128)S(1)} %collective-permute-done.4.other_ref.other_corner), custom_call_target="tpu_custom_call" | custom-call | flops 1000000000 | bytes 1000000 | tf_op jit(solution)/shard_map/pallas_call | solution.py:261
  67.8 0.7 collective-permute-done.3.other_ref.other_side
  68.4 0.0 copy-done.2
  68.4 3.3 %shard_map.50 = (f32[128,512]{1,0:T(8,128)S(1)}, f32[2,128,384]{2,1,0:T(8,128)S(1)}, f32[128,128]{1,0:T(8,128)S(1)}) custom-call(s32[1]{0:T(128)S(6)} %copy.6.count_ref, f32[128,128]{1,0:T(8,128)S(1)} %get-tuple-element.29.own_ref.own_corner, f32[128,128]{1,0:T(8,128)S(1)} %collective-permute-done.4.other_ref.other_corner, ...), custom_call_target="tpu_custom_call" | custom-call | flops 1000000000 | bytes 1000000 | tf_op jit(solution)/shard_map/pallas_call | solution.py:261
  71.8 0.0 collective-permute-done.2.other_late
  71.8 3.8 %shard_map.51 = bf16[384,256]{1,0:T(8,128)(2,1)S(1)} custom-call(s32[1]{0:T(128)S(6)} %copy.6.count_ref, f32[192,128]{1,0:T(8,128)S(1)} %get-tuple-element.23.own_late, f32[192,128]{1,0:T(8,128)S(1)} %collective-permute-done.2.other_late, f32[264,128]{1,0:T(8,128)S(1)} %get-tuple-element.27.own_ref.own_side, ...), custom_call_target="tpu_custom_call" | custom-call | flops 1000000000 | bytes 1000000 | tf_op jit(solution)/shard_map/pallas_call | solution.py:261
  75.6 0.1 collective-permute-start.5
  75.6 0.7 fusion.5
  76.3 9.1 %collective-permute-done.5 = bf16[384,256]{1,0:T(8,128)(2,1)S(1)} collective-permute-done((bf16[384,256]{1,0:T(8,128)(2,1)S(1)}, bf16[384,256]{1,0:T(8,128)(2,1)S(1)}, u32[]{:S(2)}, u32[]{:S(2)}) %collective-permute-start.5) | collective-permute-done | bytes 196640 | tf_op jit(solution)/shard_map/ppermute | solution.py:336
  85.5 0.7 fusion.4
  86.2 0.2 pad_maximum_fusion
  86.4 0.2 copy.5
  86.6 30.0 %all_to_all.11 = bf16[16,2,128,256]{3,2,1,0:T(8,128)(2,1)S(1)} all-to-all(bf16[16,2,128,256]{3,2,1,0:T(8,128)(2,1)S(1)} %copy.5), channel_id=1, replica_groups=mesh['half'=2,'inner'=4,'doppler'=4] {'inner','doppler'}, dimensions={0} | all-to-all | bytes 4194304 | tf_op jit(solution)/shard_map/all_to_all | solution.py:322
  116.6 0.1 dynamic-slice_bitcast_fusion.1
  116.8 1.5 %pad_maximum_fusion.1 = bf16[32,128,256]{2,1,0:T(8,128)(2,1)} fusion(bf16[16,128,256]{2,1,0:T(8,128)(2,1)S(1)} %get-tuple-element.38, bf16[16,128,256]{2,1,0:T(8,128)(2,1)S(1)} %get-tuple-element.37), kind=kLoop, calls=%fused_computation.1 | loop fusion | flops 1048576 | bytes 4194304 | tf_op jit(solution)/shard_map/concatenate | solution.py:349
  (1 shorter events, 0.0 us)
Async XLA Ops:
  0.0 8.7 %collective-permute-start = (s32[1,32]{1,0:T(1,128)}, s32[1,32]{1,0:T(1,128)S(1)}, u32[]{:S(2)}, u32[]{:S(2)}) collective-permute-start(s32[1,32]{1,0:T(1,128)} %list_ref.1), channel_id=1, source_target_pairs={{0,16},{16,0},{1,17},{17,1},{2,18},{18,2},{3,19},{19,3},{4,20},{20... | collective-permute-start | bytes 392 | tf_op jit(solution)/shard_map/ppermute | solution.py:324
  4.0 4.7 %collective-permute-start.1 = (s32[1]{0:T(128)}, s32[1]{0:T(128)}, u32[]{:S(2)}, u32[]{:S(2)}) collective-permute-start(s32[1]{0:T(128)} %param.7), channel_id=1, source_target_pairs={{0,16},{16,0},{1,17},{17,1},{2,18},{18,2},{3,19},{19,3},{4,20},{20... | collective-permute-start | bytes 20 | tf_op jit(solution)/shard_map/ppermute | solution.py:325
  4.1 1.9 %copy-start = (bf16[32,128,384]{2,1,0:T(8,128)(2,1)S(1)}, bf16[32,128,384]{2,1,0:T(8,128)(2,1)}, u32[]{:S(2)}) copy-start(bf16[32,128,384]{2,1,0:T(8,128)(2,1)} %param.4) | copy-start | bytes 9437188
  52.0 7.3 %copy-start.1 = (s32[1,32]{1,0:T(1,128)S(1)}, s32[1,32]{1,0:T(1,128)}, u32[]{:S(2)}) copy-start(s32[1,32]{1,0:T(1,128)} %list_ref.1) | copy-start | bytes 388
  54.0 11.5 %collective-permute-start.4 = (f32[128,128]{1,0:T(8,128)S(1)}, f32[128,128]{1,0:T(8,128)S(1)}, u32[]{:S(2)}, u32[]{:S(2)}) collective-permute-start(f32[128,128]{1,0:T(8,128)S(1)} %get-tuple-element.30), channel_id=1, source_target_pairs={{0,16},{16,0},{1,17},{17,1},{2,18},{18,2},{3,19},{19,3},{4,20},{20... | collective-permute-start | bytes 196616 | tf_op jit(solution)/shard_map/ppermute | solution.py:333
  56.3 12.2 %collective-permute-start.3 = (f32[264,128]{1,0:T(8,128)S(1)}, f32[264,128]{1,0:T(8,128)S(1)}, u32[]{:S(2)}, u32[]{:S(2)}) collective-permute-start(f32[264,128]{1,0:T(8,128)S(1)} %get-tuple-element.28), channel_id=1, source_target_pairs={{0,16},{16,0},{1,17},{17,1},{2,18},{18,2},{3,19},{19,3},{4,20},{20... | collective-permute-start | bytes 405512 | tf_op jit(solution)/shard_map/ppermute | solution.py:333
  57.7 14.0 %collective-permute-start.2 = (f32[192,128]{1,0:T(8,128)S(1)}, f32[192,128]{1,0:T(8,128)S(1)}, u32[]{:S(2)}, u32[]{:S(2)}) collective-permute-start(f32[192,128]{1,0:T(8,128)S(1)} %get-tuple-element.26), channel_id=1, source_target_pairs={{0,16},{16,0},{1,17},{17,1},{2,18},{18,2},{3,19},{19,3},{4,20},{20... | collective-permute-start | bytes 294920 | tf_op jit(solution)/shard_map/ppermute | solution.py:333
  60.7 7.7 %copy-start.2 = (bf16[1,384,256]{2,1,0:T(8,128)(2,1)S(1)}, bf16[1,384,256]{2,1,0:T(8,128)(2,1)}, u32[]{:S(2)}) copy-start(bf16[1,384,256]{2,1,0:T(8,128)(2,1)} %param.5) | copy-start | bytes 589828
  75.6 9.9 %collective-permute-start.5 = (bf16[384,256]{1,0:T(8,128)(2,1)S(1)}, bf16[384,256]{1,0:T(8,128)(2,1)S(1)}, u32[]{:S(2)}, u32[]{:S(2)}) collective-permute-start(bf16[384,256]{1,0:T(8,128)(2,1)S(1)} %shard_map.51), channel_id=1, source_target_pairs={{0,16},{16,0},{1,17},{17,1},{2,18},{18,2},{3,19},{19,3},{4,20},{20... | collective-permute-start | bytes 589832 | tf_op jit(solution)/shard_map/ppermute | solution.py:336

commit v7 on v6

--- a/solution.py
+++ b/solution.py
@@ -139,7 +139,7 @@
     return rows
 
 
-def negative_inverse(strips):
+def negative_inverse(strips, beside=()):
     full = (STEP, EDGE)
     panels = EDGE // STEP
     sub = lax.broadcasted_iota(jnp.int32, full, 0)
@@ -166,6 +166,8 @@
                 terms = [x + y for x, y in zip(terms[::2], terms[1::2])]
             rows = jnp.where(inside, 0.0, strips[p + 1]) - terms[0]
         change = outer(swept, solved)
+        if p < len(beside):
+            beside[p]()
         strips = [
             rows
             if q == p + 1
@@ -187,8 +189,8 @@
     return jnp.where(edge_iota(0) == edge_iota(1), LOADING, 0.0)
 
 
-def minus_inverse(block):
-    return negative_inverse([block[q : q + STEP] for q in range(0, EDGE, STEP)])
+def minus_inverse(block, beside=()):
+    return negative_inverse([block[q : q + STEP] for q in range(0, EDGE, STEP)], beside)
 
 
 def corner_kernel(count_ref, own_ref, other_ref, minus_ref):
@@ -210,14 +212,29 @@
     diag = side[2 * EDGE : 2 * EDGE + 1]
     block = jnp.where(r > c, both, jnp.where(r < c, both.T, diag)) * inv_scale + loading()
     close = -fine(minus, near)
-    taken = fine(near, close, TURNED)
-    next_ref[...] = minus_inverse(block - taken)
+    block = block - fine(near, close, TURNED)
+    made_ref[:, :EDGE] = close
     right = steer_ref[pl.ds(0, EDGE), :].astype(jnp.float32)
-    made = -fine(minus, jnp.concatenate([far, right], axis=1))
-    made_ref[:, :EDGE] = close
-    made_ref[:, EDGE:] = made
-    less_ref[0] = fine(near, made, TURNED)
-    less_ref[1] = fine(far, made, TURNED)
+    made = {}
+
+    def solve(name, x, at):
+        made[name] = -fine(minus, x)
+        made_ref[:, at : at + x.shape[1]] = made[name]
+
+    def take(i, lhs, name, at):
+        less_ref[i, :, at : at + made[name].shape[1]] = fine(lhs, made[name], TURNED)
+
+    next_ref[...] = minus_inverse(
+        block,
+        [
+            lambda: solve("far", far, EDGE),
+            lambda: solve("right", right, 2 * EDGE),
+            lambda: take(0, near, "far", 0),
+            lambda: take(1, far, "far", 0),
+            lambda: take(0, near, "right", EDGE),
+            lambda: take(1, far, "right", EDGE),
+        ],
+    )
 
 
 def late_kernel(
@@ -238,16 +255,27 @@
         steer_ref[pl.ds(i * EDGE, EDGE), :].astype(jnp.float32) - less_ref[i - 1, :, EDGE:]
         for i in (1, 2)
     ]
-    middle = -fine(minus, right[0])
-    last = right[1] - fine(near, middle, TURNED)
     made = made_ref[...]
-    close, far, right = made[:, :EDGE], made[:, EDGE : 2 * EDGE], made[:, 2 * EDGE :]
-    base = jnp.concatenate([right - fine(close, middle), middle], axis=0)
-    turn = jnp.concatenate([far - fine(close, step), step], axis=0)
-    x = -fine(minus_inverse(block), last)
+    close, far, top = made[:, :EDGE], made[:, EDGE : 2 * EDGE], made[:, 2 * EDGE :]
+    got = {}
+
+    def middle():
+        got["middle"] = -fine(minus, right[0])
+
+    def last():
+        got["last"] = right[1] - fine(near, got["middle"], TURNED)
+
+    def base():
+        got["base"] = jnp.concatenate([top - fine(close, got["middle"]), got["middle"]], axis=0)
+
+    def turn():
+        got["turn"] = jnp.concatenate([far - fine(close, step), step], axis=0)
+
+    x = -fine(minus_inverse(block, [middle, last, base, turn]), got["last"])
+    base, turn = got["base"], got["turn"]
     found = jnp.concatenate([base - fine(turn, x), x], axis=0)
     response = jnp.sum(steer_ref[...].astype(jnp.float32) * found, axis=0, keepdims=True)
-    out_ref[...] = (found / response).astype(out_ref.dtype)
+    out_ref[...] = (found * (1.0 / response)).astype(out_ref.dtype)
 
 
 def make_weights(count, own, other, steering):

time: 118 us -> 118 us (level)
  no operation moved by 1% of the time
where the time goes in v7:
time: 118 us
  blocking collectives  73.3 us (62%)
  waiting for transfers between devices  16 us (14%)
  Pallas kernels  13.5 us (11%)
  starting transfers between devices  8.75 us (7%)
  local copies, waits for them, and re-layouts  2.24 us (2%)
  other arithmetic  1.77 us (2%)
  matrix products  1.4 us (1%)
    all_to_all x2, blocking collectives, exchange(): return lax.all_to_all(x, INNER, split_axis=0, concat_axis=0, tiled=True)  73.3 us
    ppermute x1, waiting for transfers between devices, body(): other_weights = lax.ppermute(weights, 'half', peers)  9.1 us
    pallas_call x3, Pallas kernels, call(): pl.pallas_call(kernel, out_shape=out_shape, in_specs=[smem] + [vmem] * le...  8.74 us
    ppermute x3, waiting for transfers between devices, body(): arrived = [lax.ppermute(x, 'half', peers) for x in other_gram]  5.48 us
    ppermute x3, starting transfers between devices, body(): arrived = [lax.ppermute(x, 'half', peers) for x in other_gram]  4.61 us
    ppermute x1, starting transfers between devices, body(): other_list = lax.ppermute(train_list, 'half', peers)  4.04 us
    pallas_call x2, Pallas kernels, partial_gram(): pl.pallas_call(functools.partial(gram_kernel, which), out_shape=[jax.Shap...  3.45 us
  transfers between devices with their start and end apart: 6, of which 4 were waited for; matrix products, arithmetic and copies ran while one was open for 1% of the time, Pallas kernels for 7%

profile of v7, /device:TPU:0, one launch (start us, length us, event | category | flops | bytes accessed | tf_op | source)
XLA Modules:
  0.0 117.7 jit_solution(8187324500782346489)
XLA Ops:
  0.0 4.0 %collective-permute-start = (s32[1,32]{1,0:T(1,128)}, s32[1,32]{1,0:T(1,128)S(1)}, u32[]{:S(2)}, u32[]{:S(2)}) collective-permute-start(s32[1,32]{1,0:T(1,128)} %list_ref.1), channel_id=1, source_target_pairs={{0,16},{16,0},{1,17},{17,1},{2,18},{18,2},{3,19},{19,3},{4,20},{20... | collective-permute-start | bytes 392 | tf_op jit(solution)/shard_map/ppermute | solution.py:352
  4.0 0.0 collective-permute-start.1
  4.1 0.1 pad_add_fusion.which_ref
  4.1 0.0 copy-start
  4.1 1.9 %copy-done = bf16[32,128,384]{2,1,0:T(8,128)(2,1)S(1)} copy-done((bf16[32,128,384]{2,1,0:T(8,128)(2,1)S(1)}, bf16[32,128,384]{2,1,0:T(8,128)(2,1)}, u32[]{:S(2)}) %copy-start) | copy-done | bytes 3145752
  6.0 1.3 %shard_map.46 = bf16[16,2,128,384]{3,2,1,0:T(8,128)(2,1)S(1)} custom-call(s32[2]{0:T(128)S(1)} %pad_add_fusion.which_ref, bf16[2,16,128,384]{3,2,1,0:T(8,128)(2,1)S(1)} %bitcast.32), custom_call_target="tpu_custom_call" | custom-call | bytes 3145728 | tf_op jit(solution)/shard_map/pallas_call | solution.py:322
  7.4 1.4 %collective-permute-done.1.count_ref = s32[1]{0:T(128)} collective-permute-done((s32[1]{0:T(128)}, s32[1]{0:T(128)}, u32[]{:S(2)}, u32[]{:S(2)}) %collective-permute-start.1) | collective-permute-done | bytes 36 | tf_op jit(solution)/shard_map/ppermute | solution.py:353
  8.7 0.0 collective-permute-done.list_ref
  8.7 43.3 %all_to_all.10.blocks_ref = bf16[16,2,128,384]{3,2,1,0:T(8,128)(2,1)S(1)} all-to-all(bf16[16,2,128,384]{3,2,1,0:T(8,128)(2,1)S(1)} %shard_map.46), channel_id=1, replica_groups=mesh['half'=2,'inner'=4,'doppler'=4] {'inner','doppler'}, dimensions={0} | all-to-all | bytes 6291456 | tf_op jit(solution)/shard_map/all_to_all | solution.py:350
  52.0 2.0 %shard_map.48 = (f32[128,128]{1,0:T(8,128)S(1)}, f32[264,128]{1,0:T(8,128)S(1)}, f32[192,128]{1,0:T(8,128)S(1)}) custom-call(s32[1]{0:T(128)S(6)} %mul.3.base_ref, s32[1,32]{1,0:T(1,128)S(1)} %collective-permute-done.list_ref, s32[1]{0:T(128)} %collective-permute-done.1.count_ref, bf16[16,2,128,384]{3,2,1,0:T(8,128)(2,1)S(1)} %all_to_all.10.blocks_ref), custom_call_target="tpu_custom_call" | custom-call | flops 603979776 | bytes 1572864 | tf_op jit(solution)/shard_map/pallas_call | solution.py:63
  54.0 1.6 %collective-permute-start.4 = (f32[128,128]{1,0:T(8,128)S(1)}, f32[128,128]{1,0:T(8,128)S(1)}, u32[]{:S(2)}, u32[]{:S(2)}) collective-permute-start(f32[128,128]{1,0:T(8,128)S(1)} %get-tuple-element.30), channel_id=1, source_target_pairs={{0,16},{16,0},{1,17},{17,1},{2,18},{18,2},{3,19},{19,3},{4,20},{20... | collective-permute-start | bytes 196616 | tf_op jit(solution)/shard_map/ppermute | solution.py:361
  56.3 1.4 %collective-permute-start.3 = (f32[264,128]{1,0:T(8,128)S(1)}, f32[264,128]{1,0:T(8,128)S(1)}, u32[]{:S(2)}, u32[]{:S(2)}) collective-permute-start(f32[264,128]{1,0:T(8,128)S(1)} %get-tuple-element.28), channel_id=1, source_target_pairs={{0,16},{16,0},{1,17},{17,1},{2,18},{18,2},{3,19},{19,3},{4,20},{20... | collective-permute-start | bytes 405512 | tf_op jit(solution)/shard_map/ppermute | solution.py:361
  57.7 1.6 %collective-permute-start.2 = (f32[192,128]{1,0:T(8,128)S(1)}, f32[192,128]{1,0:T(8,128)S(1)}, u32[]{:S(2)}, u32[]{:S(2)}) collective-permute-start(f32[192,128]{1,0:T(8,128)S(1)} %get-tuple-element.26), channel_id=1, source_target_pairs={{0,16},{16,0},{1,17},{17,1},{2,18},{18,2},{3,19},{19,3},{4,20},{20... | collective-permute-start | bytes 294920 | tf_op jit(solution)/shard_map/ppermute | solution.py:361
  59.3 0.0 copy-done.1
  59.3 1.4 %shard_map.47 = (f32[128,128]{1,0:T(8,128)S(1)}, f32[264,128]{1,0:T(8,128)S(1)}, f32[192,128]{1,0:T(8,128)S(1)}) custom-call(s32[1]{0:T(128)S(6)} %mul.3.base_ref, s32[1,32]{1,0:T(1,128)S(1)} %copy-done.1, s32[1]{0:T(128)S(6)} %copy.6.count_ref, bf16[16,2,128,384]{3,2,1,0:T(8,128)(2,1)S(1)} %all_to_all.10.blocks_ref), custom_call_target="tpu_custom_call" | custom-call | flops 603979776 | bytes 1572864 | tf_op jit(solution)/shard_map/pallas_call | solution.py:63
  60.7 0.0 copy-start.2
  60.7 4.8 %collective-permute-done.4.other_ref.other_corner = f32[128,128]{1,0:T(8,128)S(1)} collective-permute-done((f32[128,128]{1,0:T(8,128)S(1)}, f32[128,128]{1,0:T(8,128)S(1)}, u32[]{:S(2)}, u32[]{:S(2)}) %collective-permute-start.4) | collective-permute-done | bytes 65568 | tf_op jit(solution)/shard_map/ppermute | solution.py:361
  65.5 2.2 %shard_map.49.minus_ref = f32[128,128]{1,0:T(8,128)S(1)} custom-call(s32[1]{0:T(128)S(6)} %copy.6.count_ref, f32[128,128]{1,0:T(8,128)S(1)} %get-tuple-element.29.own_ref.own_corner, f32[128,128]{1,0:T(8,128)S(1)} %collective-permute-done.4.other_ref.other_corner), custom_call_target="tpu_custom_call" | custom-call | flops 1000000000 | bytes 1000000 | tf_op jit(solution)/shard_map/pallas_call | solution.py:289
  67.8 0.7 collective-permute-done.3.other_ref.other_side
  68.4 0.0 copy-done.2
  68.4 2.8 %shard_map.50 = (f32[128,512]{1,0:T(8,128)S(1)}, f32[2,128,384]{2,1,0:T(8,128)S(1)}, f32[128,128]{1,0:T(8,128)S(1)}) custom-call(s32[1]{0:T(128)S(6)} %copy.6.count_ref, f32[128,128]{1,0:T(8,128)S(1)} %get-tuple-element.29.own_ref.own_corner, f32[128,128]{1,0:T(8,128)S(1)} %collective-permute-done.4.other_ref.other_corner, ...), custom_call_target="tpu_custom_call" | custom-call | flops 1000000000 | bytes 1000000 | tf_op jit(solution)/shard_map/pallas_call | solution.py:289
  71.2 0.0 collective-permute-done.2.other_late
  71.2 3.7 %shard_map.51 = bf16[384,256]{1,0:T(8,128)(2,1)S(1)} custom-call(s32[1]{0:T(128)S(6)} %copy.6.count_ref, f32[192,128]{1,0:T(8,128)S(1)} %get-tuple-element.23.own_late, f32[192,128]{1,0:T(8,128)S(1)} %collective-permute-done.2.other_late, f32[264,128]{1,0:T(8,128)S(1)} %get-tuple-element.27.own_ref.own_side, ...), custom_call_target="tpu_custom_call" | custom-call | flops 1000000000 | bytes 1000000 | tf_op jit(solution)/shard_map/pallas_call | solution.py:289
  75.0 0.1 collective-permute-start.5
  75.1 0.7 fusion.5
  75.8 9.1 %collective-permute-done.5 = bf16[384,256]{1,0:T(8,128)(2,1)S(1)} collective-permute-done((bf16[384,256]{1,0:T(8,128)(2,1)S(1)}, bf16[384,256]{1,0:T(8,128)(2,1)S(1)}, u32[]{:S(2)}, u32[]{:S(2)}) %collective-permute-start.5) | collective-permute-done | bytes 196640 | tf_op jit(solution)/shard_map/ppermute | solution.py:364
  84.9 0.7 fusion.4
  85.6 0.2 pad_maximum_fusion
  85.8 0.2 copy.5
  86.0 30.0 %all_to_all.11 = bf16[16,2,128,256]{3,2,1,0:T(8,128)(2,1)S(1)} all-to-all(bf16[16,2,128,256]{3,2,1,0:T(8,128)(2,1)S(1)} %copy.5), channel_id=1, replica_groups=mesh['half'=2,'inner'=4,'doppler'=4] {'inner','doppler'}, dimensions={0} | all-to-all | bytes 4194304 | tf_op jit(solution)/shard_map/all_to_all | solution.py:350
  116.0 0.1 dynamic-slice_bitcast_fusion.1
  116.2 1.5 %pad_maximum_fusion.1 = bf16[32,128,256]{2,1,0:T(8,128)(2,1)} fusion(bf16[16,128,256]{2,1,0:T(8,128)(2,1)S(1)} %get-tuple-element.38, bf16[16,128,256]{2,1,0:T(8,128)(2,1)S(1)} %get-tuple-element.37), kind=kLoop, calls=%fused_computation.1 | loop fusion | flops 1048576 | bytes 4194304 | tf_op jit(solution)/shard_map/concatenate | solution.py:377
  (1 shorter events, 0.0 us)
Async XLA Ops:
  0.0 8.7 %collective-permute-start = (s32[1,32]{1,0:T(1,128)}, s32[1,32]{1,0:T(1,128)S(1)}, u32[]{:S(2)}, u32[]{:S(2)}) collective-permute-start(s32[1,32]{1,0:T(1,128)} %list_ref.1), channel_id=1, source_target_pairs={{0,16},{16,0},{1,17},{17,1},{2,18},{18,2},{3,19},{19,3},{4,20},{20... | collective-permute-start | bytes 392 | tf_op jit(solution)/shard_map/ppermute | solution.py:352
  4.0 4.7 %collective-permute-start.1 = (s32[1]{0:T(128)}, s32[1]{0:T(128)}, u32[]{:S(2)}, u32[]{:S(2)}) collective-permute-start(s32[1]{0:T(128)} %param.7), channel_id=1, source_target_pairs={{0,16},{16,0},{1,17},{17,1},{2,18},{18,2},{3,19},{19,3},{4,20},{20... | collective-permute-start | bytes 20 | tf_op jit(solution)/shard_map/ppermute | solution.py:353
  4.1 1.9 %copy-start = (bf16[32,128,384]{2,1,0:T(8,128)(2,1)S(1)}, bf16[32,128,384]{2,1,0:T(8,128)(2,1)}, u32[]{:S(2)}) copy-start(bf16[32,128,384]{2,1,0:T(8,128)(2,1)} %param.4) | copy-start | bytes 9437188
  52.0 7.3 %copy-start.1 = (s32[1,32]{1,0:T(1,128)S(1)}, s32[1,32]{1,0:T(1,128)}, u32[]{:S(2)}) copy-start(s32[1,32]{1,0:T(1,128)} %list_ref.1) | copy-start | bytes 388
  54.0 11.5 %collective-permute-start.4 = (f32[128,128]{1,0:T(8,128)S(1)}, f32[128,128]{1,0:T(8,128)S(1)}, u32[]{:S(2)}, u32[]{:S(2)}) collective-permute-start(f32[128,128]{1,0:T(8,128)S(1)} %get-tuple-element.30), channel_id=1, source_target_pairs={{0,16},{16,0},{1,17},{17,1},{2,18},{18,2},{3,19},{19,3},{4,20},{20... | collective-permute-start | bytes 196616 | tf_op jit(solution)/shard_map/ppermute | solution.py:361
  56.3 12.2 %collective-permute-start.3 = (f32[264,128]{1,0:T(8,128)S(1)}, f32[264,128]{1,0:T(8,128)S(1)}, u32[]{:S(2)}, u32[]{:S(2)}) collective-permute-start(f32[264,128]{1,0:T(8,128)S(1)} %get-tuple-element.28), channel_id=1, source_target_pairs={{0,16},{16,0},{1,17},{17,1},{2,18},{18,2},{3,19},{19,3},{4,20},{20... | collective-permute-start | bytes 405512 | tf_op jit(solution)/shard_map/ppermute | solution.py:361
  57.7 13.5 %collective-permute-start.2 = (f32[192,128]{1,0:T(8,128)S(1)}, f32[192,128]{1,0:T(8,128)S(1)}, u32[]{:S(2)}, u32[]{:S(2)}) collective-permute-start(f32[192,128]{1,0:T(8,128)S(1)} %get-tuple-element.26), channel_id=1, source_target_pairs={{0,16},{16,0},{1,17},{17,1},{2,18},{18,2},{3,19},{19,3},{4,20},{20... | collective-permute-start | bytes 294920 | tf_op jit(solution)/shard_map/ppermute | solution.py:361
  60.7 7.7 %copy-start.2 = (bf16[1,384,256]{2,1,0:T(8,128)(2,1)S(1)}, bf16[1,384,256]{2,1,0:T(8,128)(2,1)}, u32[]{:S(2)}) copy-start(bf16[1,384,256]{2,1,0:T(8,128)(2,1)} %param.5) | copy-start | bytes 589828
  75.0 9.9 %collective-permute-start.5 = (bf16[384,256]{1,0:T(8,128)(2,1)S(1)}, bf16[384,256]{1,0:T(8,128)(2,1)S(1)}, u32[]{:S(2)}, u32[]{:S(2)}) collective-permute-start(bf16[384,256]{1,0:T(8,128)(2,1)S(1)} %shard_map.51), channel_id=1, source_target_pairs={{0,16},{16,0},{1,17},{17,1},{2,18},{18,2},{3,19},{19,3},{4,20},{20... | collective-permute-start | bytes 589832 | tf_op jit(solution)/shard_map/ppermute | solution.py:364

commit v8 on v7

--- a/solution.py
+++ b/solution.py
@@ -16,6 +16,7 @@
 INNER = ("inner", "doppler")
 EVERY = ("half",) + INNER
 VMEM_BYTES = 16 * 1024 * 1024
+TURNED = (((0,), (0,)), ((), ()))
 SPLIT_BYTES = 16 * 1024 * 1024
 
 
@@ -86,12 +87,6 @@
     return late[:EDGE], jnp.concatenate([upper, lower], axis=0)
 
 
-def fine(a, b, dims=(((1,), (0,)), ((), ()))):
-    return lax.dot_general(
-        a, b, dims, precision=lax.Precision.HIGHEST, preferred_element_type=jnp.float32
-    )
-
-
 def thirds(x):
     hi = x.astype(jnp.bfloat16)
     rest = x - hi.astype(jnp.float32)
@@ -100,14 +95,12 @@
     return hi, mid, low
 
 
-def outer(a, b):
+def fine(a, b, dims=(((1,), (0,)), ((), ()))):
     ah, am, al = thirds(a)
     bh, bm, bl = thirds(b)
-    left = jnp.concatenate([ah, ah, ah, am, am, al], axis=0)
-    right = jnp.concatenate([bh, bm, bl, bh, bm, bh], axis=0)
-    return lax.dot_general(
-        left, right, (((0,), (0,)), ((), ())), preferred_element_type=jnp.float32
-    )
+    left = jnp.concatenate([ah, ah, ah, am, am, al], axis=dims[0][0][0])
+    right = jnp.concatenate([bh, bm, bl, bh, bm, bh], axis=dims[0][1][0])
+    return lax.dot_general(left, right, dims, preferred_element_type=jnp.float32)
 
 
 def eliminate(rows, cols):
@@ -165,7 +158,7 @@
             while len(terms) > 1:
                 terms = [x + y for x, y in zip(terms[::2], terms[1::2])]
             rows = jnp.where(inside, 0.0, strips[p + 1]) - terms[0]
-        change = outer(swept, solved)
+        change = fine(swept, solved, TURNED)
         if p < len(beside):
             beside[p]()
         strips = [
@@ -176,9 +169,6 @@
             for q in range(panels)
         ]
     return jnp.concatenate(strips, axis=0)
-
-
-TURNED = (((0,), (0,)), ((), ()))
 
 
 def inverse_scale(count_ref):

time: 118 us -> 117 us (level)
  no operation moved by 1% of the time
where the time goes in v8:
time: 117 us
  blocking collectives  73.3 us (63%)
  waiting for transfers between devices  16 us (14%)
  Pallas kernels  13.1 us (11%)
  starting transfers between devices  8.75 us (7%)
  local copies, waits for them, and re-layouts  2.24 us (2%)
  other arithmetic  1.77 us (2%)
  matrix products  1.4 us (1%)
    all_to_all x2, blocking collectives, exchange(): return lax.all_to_all(x, INNER, split_axis=0, concat_axis=0, tiled=True)  73.3 us
    ppermute x1, waiting for transfers between devices, body(): other_weights = lax.ppermute(weights, 'half', peers)  9.1 us
    pallas_call x3, Pallas kernels, call(): pl.pallas_call(kernel, out_shape=out_shape, in_specs=[smem] + [vmem] * le...  8.33 us
    ppermute x3, waiting for transfers between devices, body(): arrived = [lax.ppermute(x, 'half', peers) for x in other_gram]  5.48 us
    ppermute x3, starting transfers between devices, body(): arrived = [lax.ppermute(x, 'half', peers) for x in other_gram]  4.61 us
    ppermute x1, starting transfers between devices, body(): other_list = lax.ppermute(train_list, 'half', peers)  4.04 us
    pallas_call x2, Pallas kernels, partial_gram(): pl.pallas_call(functools.partial(gram_kernel, which), out_shape=[jax.Shap...  3.45 us
  transfers between devices with their start and end apart: 6, of which 4 were waited for; matrix products, arithmetic and copies ran while one was open for 1% of the time, Pallas kernels for 7%

profile of v8, /device:TPU:0, one launch (start us, length us, event | category | flops | bytes accessed | tf_op | source)
XLA Modules:
  0.0 117.3 jit_solution(12928475946184052484)
XLA Ops:
  0.0 4.0 %collective-permute-start = (s32[1,32]{1,0:T(1,128)}, s32[1,32]{1,0:T(1,128)S(1)}, u32[]{:S(2)}, u32[]{:S(2)}) collective-permute-start(s32[1,32]{1,0:T(1,128)} %list_ref.1), channel_id=1, source_target_pairs={{0,16},{16,0},{1,17},{17,1},{2,18},{18,2},{3,19},{19,3},{4,20},{20... | collective-permute-start | bytes 392 | tf_op jit(solution)/shard_map/ppermute | solution.py:342
  4.0 0.0 collective-permute-start.1
  4.1 0.1 pad_add_fusion.which_ref
  4.1 0.0 copy-start
  4.1 1.9 %copy-done = bf16[32,128,384]{2,1,0:T(8,128)(2,1)S(1)} copy-done((bf16[32,128,384]{2,1,0:T(8,128)(2,1)S(1)}, bf16[32,128,384]{2,1,0:T(8,128)(2,1)}, u32[]{:S(2)}) %copy-start) | copy-done | bytes 3145752
  6.0 1.3 %shard_map.46 = bf16[16,2,128,384]{3,2,1,0:T(8,128)(2,1)S(1)} custom-call(s32[2]{0:T(128)S(1)} %pad_add_fusion.which_ref, bf16[2,16,128,384]{3,2,1,0:T(8,128)(2,1)S(1)} %bitcast.32), custom_call_target="tpu_custom_call" | custom-call | bytes 3145728 | tf_op jit(solution)/shard_map/pallas_call | solution.py:312
  7.4 1.4 %collective-permute-done.1.count_ref = s32[1]{0:T(128)} collective-permute-done((s32[1]{0:T(128)}, s32[1]{0:T(128)}, u32[]{:S(2)}, u32[]{:S(2)}) %collective-permute-start.1) | collective-permute-done | bytes 36 | tf_op jit(solution)/shard_map/ppermute | solution.py:343
  8.7 0.0 collective-permute-done.list_ref
  8.7 43.3 %all_to_all.10.blocks_ref = bf16[16,2,128,384]{3,2,1,0:T(8,128)(2,1)S(1)} all-to-all(bf16[16,2,128,384]{3,2,1,0:T(8,128)(2,1)S(1)} %shard_map.46), channel_id=1, replica_groups=mesh['half'=2,'inner'=4,'doppler'=4] {'inner','doppler'}, dimensions={0} | all-to-all | bytes 6291456 | tf_op jit(solution)/shard_map/all_to_all | solution.py:340
  52.0 2.0 %shard_map.48 = (f32[128,128]{1,0:T(8,128)S(1)}, f32[264,128]{1,0:T(8,128)S(1)}, f32[192,128]{1,0:T(8,128)S(1)}) custom-call(s32[1]{0:T(128)S(6)} %mul.3.base_ref, s32[1,32]{1,0:T(1,128)S(1)} %collective-permute-done.list_ref, s32[1]{0:T(128)} %collective-permute-done.1.count_ref, bf16[16,2,128,384]{3,2,1,0:T(8,128)(2,1)S(1)} %all_to_all.10.blocks_ref), custom_call_target="tpu_custom_call" | custom-call | flops 603979776 | bytes 1572864 | tf_op jit(solution)/shard_map/pallas_call | solution.py:64
  54.0 1.6 %collective-permute-start.4 = (f32[128,128]{1,0:T(8,128)S(1)}, f32[128,128]{1,0:T(8,128)S(1)}, u32[]{:S(2)}, u32[]{:S(2)}) collective-permute-start(f32[128,128]{1,0:T(8,128)S(1)} %get-tuple-element.30), channel_id=1, source_target_pairs={{0,16},{16,0},{1,17},{17,1},{2,18},{18,2},{3,19},{19,3},{4,20},{20... | collective-permute-start | bytes 196616 | tf_op jit(solution)/shard_map/ppermute | solution.py:351
  56.3 1.4 %collective-permute-start.3 = (f32[264,128]{1,0:T(8,128)S(1)}, f32[264,128]{1,0:T(8,128)S(1)}, u32[]{:S(2)}, u32[]{:S(2)}) collective-permute-start(f32[264,128]{1,0:T(8,128)S(1)} %get-tuple-element.28), channel_id=1, source_target_pairs={{0,16},{16,0},{1,17},{17,1},{2,18},{18,2},{3,19},{19,3},{4,20},{20... | collective-permute-start | bytes 405512 | tf_op jit(solution)/shard_map/ppermute | solution.py:351
  57.7 1.6 %collective-permute-start.2 = (f32[192,128]{1,0:T(8,128)S(1)}, f32[192,128]{1,0:T(8,128)S(1)}, u32[]{:S(2)}, u32[]{:S(2)}) collective-permute-start(f32[192,128]{1,0:T(8,128)S(1)} %get-tuple-element.26), channel_id=1, source_target_pairs={{0,16},{16,0},{1,17},{17,1},{2,18},{18,2},{3,19},{19,3},{4,20},{20... | collective-permute-start | bytes 294920 | tf_op jit(solution)/shard_map/ppermute | solution.py:351
  59.3 0.0 copy-done.1
  59.3 1.4 %shard_map.47 = (f32[128,128]{1,0:T(8,128)S(1)}, f32[264,128]{1,0:T(8,128)S(1)}, f32[192,128]{1,0:T(8,128)S(1)}) custom-call(s32[1]{0:T(128)S(6)} %mul.3.base_ref, s32[1,32]{1,0:T(1,128)S(1)} %copy-done.1, s32[1]{0:T(128)S(6)} %copy.6.count_ref, bf16[16,2,128,384]{3,2,1,0:T(8,128)(2,1)S(1)} %all_to_all.10.blocks_ref), custom_call_target="tpu_custom_call" | custom-call | flops 603979776 | bytes 1572864 | tf_op jit(solution)/shard_map/pallas_call | solution.py:64
  60.7 0.0 copy-start.2
  60.7 4.8 %collective-permute-done.4.other_ref.other_corner = f32[128,128]{1,0:T(8,128)S(1)} collective-permute-done((f32[128,128]{1,0:T(8,128)S(1)}, f32[128,128]{1,0:T(8,128)S(1)}, u32[]{:S(2)}, u32[]{:S(2)}) %collective-permute-start.4) | collective-permute-done | bytes 65568 | tf_op jit(solution)/shard_map/ppermute | solution.py:351
  65.5 2.2 %shard_map.49.minus_ref = f32[128,128]{1,0:T(8,128)S(1)} custom-call(s32[1]{0:T(128)S(6)} %copy.6.count_ref, f32[128,128]{1,0:T(8,128)S(1)} %get-tuple-element.29.own_ref.own_corner, f32[128,128]{1,0:T(8,128)S(1)} %collective-permute-done.4.other_ref.other_corner), custom_call_target="tpu_custom_call" | custom-call | flops 1000000000 | bytes 1000000 | tf_op jit(solution)/shard_map/pallas_call | solution.py:279
  67.8 0.7 collective-permute-done.3.other_ref.other_side
  68.4 0.0 copy-done.2
  68.4 2.7 %shard_map.50 = (f32[128,512]{1,0:T(8,128)S(1)}, f32[2,128,384]{2,1,0:T(8,128)S(1)}, f32[128,128]{1,0:T(8,128)S(1)}) custom-call(s32[1]{0:T(128)S(6)} %copy.6.count_ref, f32[128,128]{1,0:T(8,128)S(1)} %get-tuple-element.29.own_ref.own_corner, f32[128,128]{1,0:T(8,128)S(1)} %collective-permute-done.4.other_ref.other_corner, ...), custom_call_target="tpu_custom_call" | custom-call | flops 1000000000 | bytes 1000000 | tf_op jit(solution)/shard_map/pallas_call | solution.py:279
  71.1 0.0 collective-permute-done.2.other_late
  71.1 3.4 %shard_map.51 = bf16[384,256]{1,0:T(8,128)(2,1)S(1)} custom-call(s32[1]{0:T(128)S(6)} %copy.6.count_ref, f32[192,128]{1,0:T(8,128)S(1)} %get-tuple-element.23.own_late, f32[192,128]{1,0:T(8,128)S(1)} %collective-permute-done.2.other_late, f32[264,128]{1,0:T(8,128)S(1)} %get-tuple-element.27.own_ref.own_side, ...), custom_call_target="tpu_custom_call" | custom-call | flops 1000000000 | bytes 1000000 | tf_op jit(solution)/shard_map/pallas_call | solution.py:279
  74.6 0.1 collective-permute-start.5
  74.6 0.7 fusion.5
  75.3 9.1 %collective-permute-done.5 = bf16[384,256]{1,0:T(8,128)(2,1)S(1)} collective-permute-done((bf16[384,256]{1,0:T(8,128)(2,1)S(1)}, bf16[384,256]{1,0:T(8,128)(2,1)S(1)}, u32[]{:S(2)}, u32[]{:S(2)}) %collective-permute-start.5) | collective-permute-done | bytes 196640 | tf_op jit(solution)/shard_map/ppermute | solution.py:354
  84.4 0.7 fusion.4
  85.2 0.2 pad_maximum_fusion
  85.4 0.2 copy.5
  85.6 30.0 %all_to_all.11 = bf16[16,2,128,256]{3,2,1,0:T(8,128)(2,1)S(1)} all-to-all(bf16[16,2,128,256]{3,2,1,0:T(8,128)(2,1)S(1)} %copy.5), channel_id=1, replica_groups=mesh['half'=2,'inner'=4,'doppler'=4] {'inner','doppler'}, dimensions={0} | all-to-all | bytes 4194304 | tf_op jit(solution)/shard_map/all_to_all | solution.py:340
  115.6 0.1 dynamic-slice_bitcast_fusion.1
  115.8 1.5 %pad_maximum_fusion.1 = bf16[32,128,256]{2,1,0:T(8,128)(2,1)} fusion(bf16[16,128,256]{2,1,0:T(8,128)(2,1)S(1)} %get-tuple-element.38, bf16[16,128,256]{2,1,0:T(8,128)(2,1)S(1)} %get-tuple-element.37), kind=kLoop, calls=%fused_computation.1 | loop fusion | flops 1048576 | bytes 4194304 | tf_op jit(solution)/shard_map/concatenate | solution.py:367
  (1 shorter events, 0.0 us)
Async XLA Ops:
  0.0 8.7 %collective-permute-start = (s32[1,32]{1,0:T(1,128)}, s32[1,32]{1,0:T(1,128)S(1)}, u32[]{:S(2)}, u32[]{:S(2)}) collective-permute-start(s32[1,32]{1,0:T(1,128)} %list_ref.1), channel_id=1, source_target_pairs={{0,16},{16,0},{1,17},{17,1},{2,18},{18,2},{3,19},{19,3},{4,20},{20... | collective-permute-start | bytes 392 | tf_op jit(solution)/shard_map/ppermute | solution.py:342
  4.0 4.7 %collective-permute-start.1 = (s32[1]{0:T(128)}, s32[1]{0:T(128)}, u32[]{:S(2)}, u32[]{:S(2)}) collective-permute-start(s32[1]{0:T(128)} %param.7), channel_id=1, source_target_pairs={{0,16},{16,0},{1,17},{17,1},{2,18},{18,2},{3,19},{19,3},{4,20},{20... | collective-permute-start | bytes 20 | tf_op jit(solution)/shard_map/ppermute | solution.py:343
  4.1 1.9 %copy-start = (bf16[32,128,384]{2,1,0:T(8,128)(2,1)S(1)}, bf16[32,128,384]{2,1,0:T(8,128)(2,1)}, u32[]{:S(2)}) copy-start(bf16[32,128,384]{2,1,0:T(8,128)(2,1)} %param.4) | copy-start | bytes 9437188
  52.0 7.3 %copy-start.1 = (s32[1,32]{1,0:T(1,128)S(1)}, s32[1,32]{1,0:T(1,128)}, u32[]{:S(2)}) copy-start(s32[1,32]{1,0:T(1,128)} %list_ref.1) | copy-start | bytes 388
  54.0 11.5 %collective-permute-start.4 = (f32[128,128]{1,0:T(8,128)S(1)}, f32[128,128]{1,0:T(8,128)S(1)}, u32[]{:S(2)}, u32[]{:S(2)}) collective-permute-start(f32[128,128]{1,0:T(8,128)S(1)} %get-tuple-element.30), channel_id=1, source_target_pairs={{0,16},{16,0},{1,17},{17,1},{2,18},{18,2},{3,19},{19,3},{4,20},{20... | collective-permute-start | bytes 196616 | tf_op jit(solution)/shard_map/ppermute | solution.py:351
  56.3 12.2 %collective-permute-start.3 = (f32[264,128]{1,0:T(8,128)S(1)}, f32[264,128]{1,0:T(8,128)S(1)}, u32[]{:S(2)}, u32[]{:S(2)}) collective-permute-start(f32[264,128]{1,0:T(8,128)S(1)} %get-tuple-element.28), channel_id=1, source_target_pairs={{0,16},{16,0},{1,17},{17,1},{2,18},{18,2},{3,19},{19,3},{4,20},{20... | collective-permute-start | bytes 405512 | tf_op jit(solution)/shard_map/ppermute | solution.py:351
  57.7 13.4 %collective-permute-start.2 = (f32[192,128]{1,0:T(8,128)S(1)}, f32[192,128]{1,0:T(8,128)S(1)}, u32[]{:S(2)}, u32[]{:S(2)}) collective-permute-start(f32[192,128]{1,0:T(8,128)S(1)} %get-tuple-element.26), channel_id=1, source_target_pairs={{0,16},{16,0},{1,17},{17,1},{2,18},{18,2},{3,19},{19,3},{4,20},{20... | collective-permute-start | bytes 294920 | tf_op jit(solution)/shard_map/ppermute | solution.py:351
  60.7 7.7 %copy-start.2 = (bf16[1,384,256]{2,1,0:T(8,128)(2,1)S(1)}, bf16[1,384,256]{2,1,0:T(8,128)(2,1)}, u32[]{:S(2)}) copy-start(bf16[1,384,256]{2,1,0:T(8,128)(2,1)} %param.5) | copy-start | bytes 589828
  74.6 9.9 %collective-permute-start.5 = (bf16[384,256]{1,0:T(8,128)(2,1)S(1)}, bf16[384,256]{1,0:T(8,128)(2,1)S(1)}, u32[]{:S(2)}, u32[]{:S(2)}) collective-permute-start(bf16[384,256]{1,0:T(8,128)(2,1)S(1)} %shard_map.51), channel_id=1, source_target_pairs={{0,16},{16,0},{1,17},{17,1},{2,18},{18,2},{3,19},{19,3},{4,20},{20... | collective-permute-start | bytes 589832 | tf_op jit(solution)/shard_map/ppermute | solution.py:354

commit v9 on v8

--- a/solution.py
+++ b/solution.py
@@ -103,72 +103,65 @@
     return lax.dot_general(left, right, dims, preferred_element_type=jnp.float32)
 
 
-def eliminate(rows, cols):
+def spread(x, at):
     full = (STEP, EDGE)
-    sub = lax.broadcasted_iota(jnp.int32, full, 0)
-
-    def row(x, k):
-        return jnp.broadcast_to(x[k : k + 1], full)
-
-    cols = list(cols)
-    for k in range(0, STEP, 2):
-        one, two = sub == k, sub == k + 1
-        here = one | two
-        a, b, c = row(cols[k], k), row(cols[k + 1], k), row(cols[k + 1], k + 1)
-        inv = 1.0 / (a * c - b * b)
-        first = jnp.where(one, 1.0, jnp.where(two, 0.0, -cols[k]))
-        second = jnp.where(two, 1.0, jnp.where(one, 0.0, -cols[k + 1]))
-
-        left = (first * c - second * b) * inv
-        after = (second * a - first * b) * inv
-
-        def step(x):
-            r, s = row(x, k), row(x, k + 1)
-            return jnp.where(here, 0.0, x) + (left * r + after * s)
-
-        for i in range(k + 2, STEP):
-            cols[i] = step(cols[i])
-        rows = step(rows)
-    return rows
-
-
-def negative_inverse(strips, beside=()):
+    return [
+        jnp.take_along_axis(x, jnp.full(full, at + i, jnp.int32), axis=1, mode="promise_in_bounds")
+        for i in range(STEP)
+    ]
+
+
+def lower_inverse(block, beside=()):
     full = (STEP, EDGE)
     panels = EDGE // STEP
     sub = lax.broadcasted_iota(jnp.int32, full, 0)
     lane = lax.broadcasted_iota(jnp.int32, full, 1)
 
-    def spread(x, at):
-        return [
-            jnp.take_along_axis(
-                x, jnp.full(full, at + i, jnp.int32), axis=1, mode="promise_in_bounds"
-            )
-            for i in range(STEP)
-        ]
-
+    def row(x, k):
+        return jnp.broadcast_to(x[k : k + 1], full)
+
+    strips = [block[q : q + STEP] for q in range(0, EDGE, STEP)]
     rows = strips[0]
     for p in range(panels):
         at = p * STEP
         inside = (lane >= at) & (lane < at + STEP)
-        swept = jnp.where(inside, jnp.where(lane == sub + at, -1.0, 0.0), rows)
-        weights = spread(strips[p + 1], at) if p + 1 < panels else None
-        solved = eliminate(swept, spread(rows, at))
-        if weights is not None:
-            terms = [w * jnp.broadcast_to(solved[k : k + 1], full) for k, w in enumerate(weights)]
+        cols = spread(rows, at)
+        ahead = spread(strips[p + 1], at) if p + 1 < panels else None
+        rows = jnp.where(inside, jnp.where(lane == sub + at, 1.0, 0.0), rows)
+        pivots = jnp.zeros(full, jnp.float32)
+        terms = []
+        for k in range(STEP):
+            inv = 1.0 / row(cols[k], k)
+            pivots = jnp.where(sub == k, cols[k], pivots)
+            factor = jnp.where(sub > k, cols[k] * inv, 0.0)
+            if ahead is not None:
+                terms.append(ahead[k] * (row(rows, k) * inv))
+            for i in range(k + 1, STEP):
+                value = row(cols[i], k)
+                cols[i] = cols[i] - factor * value
+                if ahead is not None:
+                    ahead[i] = ahead[i] - ahead[k] * (value * inv)
+            rows = rows - factor * row(rows, k)
+        made = rows * lax.rsqrt(pivots)
+        if ahead is not None:
             while len(terms) > 1:
                 terms = [x + y for x, y in zip(terms[::2], terms[1::2])]
             rows = jnp.where(inside, 0.0, strips[p + 1]) - terms[0]
-        change = fine(swept, solved, TURNED)
-        if p < len(beside):
-            beside[p]()
+            change = fine(made, made, TURNED)
+        for call in beside[p : p + 1] if p + 1 < panels else beside[p:]:
+            call()
         strips = [
-            rows
+            made
+            if q == p
+            else strips[q]
+            if q < p
+            else rows
             if q == p + 1
-            else (jnp.zeros(full, jnp.float32) if q == p else jnp.where(inside, 0.0, strips[q]))
-            - change[q * STEP : (q + 1) * STEP]
+            else jnp.where(inside, 0.0, strips[q]) - change[q * STEP : (q + 1) * STEP]
             for q in range(panels)
         ]
-    return jnp.concatenate(strips, axis=0)
+    inverse = jnp.concatenate(strips, axis=0)
+    return jnp.where(edge_iota(0) >= edge_iota(1), inverse, 0.0)
 
 
 def inverse_scale(count_ref):
@@ -179,68 +172,68 @@
     return jnp.where(edge_iota(0) == edge_iota(1), LOADING, 0.0)
 
 
-def minus_inverse(block, beside=()):
-    return negative_inverse([block[q : q + STEP] for q in range(0, EDGE, STEP)], beside)
-
-
-def corner_kernel(count_ref, own_ref, other_ref, minus_ref):
+def corner_kernel(count_ref, own_ref, other_ref, lower_ref):
     both = own_ref[...] + other_ref[...]
     block = jnp.where(edge_iota(0) <= edge_iota(1), both, both.T)
-    minus_ref[...] = minus_inverse(block * inverse_scale(count_ref) + loading())
+    lower_ref[...] = lower_inverse(block * inverse_scale(count_ref) + loading())
 
 
 def side_kernel(
-    count_ref, own_corner, other_corner, own_ref, other_ref, steer_ref, minus_ref,
+    count_ref, own_corner, other_corner, own_ref, other_ref, steer_ref, lower_ref,
     made_ref, less_ref, next_ref,
 ):
     inv_scale = inverse_scale(count_ref)
     side = own_ref[...] + other_ref[...]
     near, far = side[:EDGE] * inv_scale, side[EDGE : 2 * EDGE] * inv_scale
-    minus = minus_ref[...]
+    lower = lower_ref[...]
     r, c = edge_iota(0), edge_iota(1)
     both = own_corner[...] + other_corner[...]
     diag = side[2 * EDGE : 2 * EDGE + 1]
     block = jnp.where(r > c, both, jnp.where(r < c, both.T, diag)) * inv_scale + loading()
-    close = -fine(minus, near)
-    block = block - fine(near, close, TURNED)
-    made_ref[:, :EDGE] = close
+    half = {"near": fine(lower, near)}
+    block = block - fine(half["near"], half["near"], TURNED)
     right = steer_ref[pl.ds(0, EDGE), :].astype(jnp.float32)
-    made = {}
-
-    def solve(name, x, at):
-        made[name] = -fine(minus, x)
-        made_ref[:, at : at + x.shape[1]] = made[name]
+
+    def forward(name, x):
+        half[name] = fine(lower, x)
+
+    def back(name, at):
+        x = half[name]
+        made_ref[:, at : at + x.shape[1]] = fine(lower, x, TURNED)
 
     def take(i, lhs, name, at):
-        less_ref[i, :, at : at + made[name].shape[1]] = fine(lhs, made[name], TURNED)
-
-    next_ref[...] = minus_inverse(
+        x = half[name]
+        less_ref[i, :, at : at + x.shape[1]] = fine(half[lhs], x, TURNED)
+
+    next_ref[...] = lower_inverse(
         block,
         [
-            lambda: solve("far", far, EDGE),
-            lambda: solve("right", right, 2 * EDGE),
-            lambda: take(0, near, "far", 0),
-            lambda: take(1, far, "far", 0),
-            lambda: take(0, near, "right", EDGE),
-            lambda: take(1, far, "right", EDGE),
+            lambda: forward("far", far),
+            lambda: forward("right", right),
+            lambda: take(0, "near", "far", 0),
+            lambda: take(1, "far", "far", 0),
+            lambda: take(0, "near", "right", EDGE),
+            lambda: take(1, "far", "right", EDGE),
+            lambda: back("near", 0),
+            lambda: back("far", EDGE),
+            lambda: back("right", 2 * EDGE),
         ],
     )
 
 
 def late_kernel(
     count_ref, own_late, other_late, own_side, other_side, steer_ref, made_ref, less_ref,
-    minus_ref, out_ref,
+    lower_ref, out_ref,
 ):
     size, beams = steer_ref.shape
-    parts = size // EDGE
     inv_scale = inverse_scale(count_ref)
     diag = own_side[pl.ds(2 * EDGE, 8), :] + other_side[pl.ds(2 * EDGE, 8), :]
     near, block = unpack_late(own_late[...] + other_late[...], diag[1:2])
     near = near * inv_scale - less_ref[0, :, :EDGE]
     block = block * inv_scale + loading() - less_ref[1, :, :EDGE]
-    minus = minus_ref[...]
-    step = -fine(minus, near)
-    block = block - fine(near, step, TURNED)
+    lower = lower_ref[...]
+    near = fine(lower, near)
+    block = block - fine(near, near, TURNED)
     right = [
         steer_ref[pl.ds(i * EDGE, EDGE), :].astype(jnp.float32) - less_ref[i - 1, :, EDGE:]
         for i in (1, 2)
@@ -249,21 +242,27 @@
     close, far, top = made[:, :EDGE], made[:, EDGE : 2 * EDGE], made[:, 2 * EDGE :]
     got = {}
 
+    def forward():
+        got["half"] = fine(lower, right[0])
+
+    def last():
+        got["last"] = right[1] - fine(near, got["half"], TURNED)
+
     def middle():
-        got["middle"] = -fine(minus, right[0])
-
-    def last():
-        got["last"] = right[1] - fine(near, got["middle"], TURNED)
+        got["middle"] = fine(lower, got["half"], TURNED)
+
+    def step():
+        got["step"] = fine(lower, near, TURNED)
 
     def base():
         got["base"] = jnp.concatenate([top - fine(close, got["middle"]), got["middle"]], axis=0)
 
     def turn():
-        got["turn"] = jnp.concatenate([far - fine(close, step), step], axis=0)
-
-    x = -fine(minus_inverse(block, [middle, last, base, turn]), got["last"])
-    base, turn = got["base"], got["turn"]
-    found = jnp.concatenate([base - fine(turn, x), x], axis=0)
+        got["turn"] = jnp.concatenate([far - fine(close, got["step"]), got["step"]], axis=0)
+
+    end = lower_inverse(block, [forward, last, middle, step, base, turn])
+    x = fine(end, fine(end, got["last"]), TURNED)
+    found = jnp.concatenate([got["base"] - fine(got["turn"], x), x], axis=0)
     response = jnp.sum(steer_ref[...].astype(jnp.float32) * found, axis=0, keepdims=True)
     out_ref[...] = (found * (1.0 / response)).astype(out_ref.dtype)
 

time: 117 us -> 118 us (level)
  Pallas kernels: 13.1 us -> 14.3 us
    pallas_call x3, Pallas kernels: 8.33 us -> 9.55 us  [call(): pl.pallas_call(kernel, out_shape=out_shape, in_specs=[smem] + [vmem] * le...]
where the time goes in v9:
time: 118 us
  blocking collectives  73.3 us (62%)
  waiting for transfers between devices  15.6 us (13%)
  Pallas kernels  14.3 us (12%)
  starting transfers between devices  8.75 us (7%)
  local copies, waits for them, and re-layouts  2.24 us (2%)
  other arithmetic  1.77 us (2%)
  matrix products  1.4 us (1%)
    all_to_all x2, blocking collectives, exchange(): return lax.all_to_all(x, INNER, split_axis=0, concat_axis=0, tiled=True)  73.3 us
    pallas_call x3, Pallas kernels, call(): pl.pallas_call(kernel, out_shape=out_shape, in_specs=[smem] + [vmem] * le...  9.55 us
    ppermute x1, waiting for transfers between devices, body(): other_weights = lax.ppermute(weights, 'half', peers)  9.1 us
    ppermute x3, waiting for transfers between devices, body(): arrived = [lax.ppermute(x, 'half', peers) for x in other_gram]  5.11 us
    ppermute x3, starting transfers between devices, body(): arrived = [lax.ppermute(x, 'half', peers) for x in other_gram]  4.61 us
    ppermute x1, starting transfers between devices, body(): other_list = lax.ppermute(train_list, 'half', peers)  4.04 us
    pallas_call x2, Pallas kernels, partial_gram(): pl.pallas_call(functools.partial(gram_kernel, which), out_shape=[jax.Shap...  3.45 us
  transfers between devices with their start and end apart: 6, of which 4 were waited for; matrix products, arithmetic and copies ran while one was open for 1% of the time, Pallas kernels for 7%

profile of v9, /device:TPU:0, one launch (start us, length us, event | category | flops | bytes accessed | tf_op | source)
XLA Modules:
  0.0 118.1 jit_solution(14018461492794945160)
XLA Ops:
  0.0 4.0 %collective-permute-start = (s32[1,32]{1,0:T(1,128)}, s32[1,32]{1,0:T(1,128)S(1)}, u32[]{:S(2)}, u32[]{:S(2)}) collective-permute-start(s32[1,32]{1,0:T(1,128)} %list_ref.1), channel_id=1, source_target_pairs={{0,16},{16,0},{1,17},{17,1},{2,18},{18,2},{3,19},{19,3},{4,20},{20... | collective-permute-start | bytes 392 | tf_op jit(solution)/shard_map/ppermute | solution.py:341
  4.0 0.0 collective-permute-start.1
  4.1 0.1 pad_add_fusion.which_ref
  4.1 0.0 copy-start
  4.1 1.9 %copy-done = bf16[32,128,384]{2,1,0:T(8,128)(2,1)S(1)} copy-done((bf16[32,128,384]{2,1,0:T(8,128)(2,1)S(1)}, bf16[32,128,384]{2,1,0:T(8,128)(2,1)}, u32[]{:S(2)}) %copy-start) | copy-done | bytes 3145752
  6.0 1.3 %shard_map.46 = bf16[16,2,128,384]{3,2,1,0:T(8,128)(2,1)S(1)} custom-call(s32[2]{0:T(128)S(1)} %pad_add_fusion.which_ref, bf16[2,16,128,384]{3,2,1,0:T(8,128)(2,1)S(1)} %bitcast.32), custom_call_target="tpu_custom_call" | custom-call | bytes 3145728 | tf_op jit(solution)/shard_map/pallas_call | solution.py:311
  7.4 1.4 %collective-permute-done.1.count_ref = s32[1]{0:T(128)} collective-permute-done((s32[1]{0:T(128)}, s32[1]{0:T(128)}, u32[]{:S(2)}, u32[]{:S(2)}) %collective-permute-start.1) | collective-permute-done | bytes 36 | tf_op jit(solution)/shard_map/ppermute | solution.py:342
  8.7 0.0 collective-permute-done.list_ref
  8.7 43.3 %all_to_all.10.blocks_ref = bf16[16,2,128,384]{3,2,1,0:T(8,128)(2,1)S(1)} all-to-all(bf16[16,2,128,384]{3,2,1,0:T(8,128)(2,1)S(1)} %shard_map.46), channel_id=1, replica_groups=mesh['half'=2,'inner'=4,'doppler'=4] {'inner','doppler'}, dimensions={0} | all-to-all | bytes 6291456 | tf_op jit(solution)/shard_map/all_to_all | solution.py:339
  52.0 2.0 %shard_map.48 = (f32[128,128]{1,0:T(8,128)S(1)}, f32[264,128]{1,0:T(8,128)S(1)}, f32[192,128]{1,0:T(8,128)S(1)}) custom-call(s32[1]{0:T(128)S(6)} %mul.3.base_ref, s32[1,32]{1,0:T(1,128)S(1)} %collective-permute-done.list_ref, s32[1]{0:T(128)} %collective-permute-done.1.count_ref, bf16[16,2,128,384]{3,2,1,0:T(8,128)(2,1)S(1)} %all_to_all.10.blocks_ref), custom_call_target="tpu_custom_call" | custom-call | flops 603979776 | bytes 1572864 | tf_op jit(solution)/shard_map/pallas_call | solution.py:64
  54.0 1.6 %collective-permute-start.4 = (f32[128,128]{1,0:T(8,128)S(1)}, f32[128,128]{1,0:T(8,128)S(1)}, u32[]{:S(2)}, u32[]{:S(2)}) collective-permute-start(f32[128,128]{1,0:T(8,128)S(1)} %get-tuple-element.30), channel_id=1, source_target_pairs={{0,16},{16,0},{1,17},{17,1},{2,18},{18,2},{3,19},{19,3},{4,20},{20... | collective-permute-start | bytes 196616 | tf_op jit(solution)/shard_map/ppermute | solution.py:350
  56.3 1.4 %collective-permute-start.3 = (f32[264,128]{1,0:T(8,128)S(1)}, f32[264,128]{1,0:T(8,128)S(1)}, u32[]{:S(2)}, u32[]{:S(2)}) collective-permute-start(f32[264,128]{1,0:T(8,128)S(1)} %get-tuple-element.28), channel_id=1, source_target_pairs={{0,16},{16,0},{1,17},{17,1},{2,18},{18,2},{3,19},{19,3},{4,20},{20... | collective-permute-start | bytes 405512 | tf_op jit(solution)/shard_map/ppermute | solution.py:350
  57.7 1.6 %collective-permute-start.2 = (f32[192,128]{1,0:T(8,128)S(1)}, f32[192,128]{1,0:T(8,128)S(1)}, u32[]{:S(2)}, u32[]{:S(2)}) collective-permute-start(f32[192,128]{1,0:T(8,128)S(1)} %get-tuple-element.26), channel_id=1, source_target_pairs={{0,16},{16,0},{1,17},{17,1},{2,18},{18,2},{3,19},{19,3},{4,20},{20... | collective-permute-start | bytes 294920 | tf_op jit(solution)/shard_map/ppermute | solution.py:350
  59.3 0.0 copy-done.1
  59.3 1.4 %shard_map.47 = (f32[128,128]{1,0:T(8,128)S(1)}, f32[264,128]{1,0:T(8,128)S(1)}, f32[192,128]{1,0:T(8,128)S(1)}) custom-call(s32[1]{0:T(128)S(6)} %mul.3.base_ref, s32[1,32]{1,0:T(1,128)S(1)} %copy-done.1, s32[1]{0:T(128)S(6)} %copy.6.count_ref, bf16[16,2,128,384]{3,2,1,0:T(8,128)(2,1)S(1)} %all_to_all.10.blocks_ref), custom_call_target="tpu_custom_call" | custom-call | flops 603979776 | bytes 1572864 | tf_op jit(solution)/shard_map/pallas_call | solution.py:64
  60.7 0.0 copy-start.2
  60.7 4.8 %collective-permute-done.4.other_ref.other_corner = f32[128,128]{1,0:T(8,128)S(1)} collective-permute-done((f32[128,128]{1,0:T(8,128)S(1)}, f32[128,128]{1,0:T(8,128)S(1)}, u32[]{:S(2)}, u32[]{:S(2)}) %collective-permute-start.4) | collective-permute-done | bytes 65568 | tf_op jit(solution)/shard_map/ppermute | solution.py:350
  65.5 2.6 %shard_map.49.lower_ref = f32[128,128]{1,0:T(8,128)S(1)} custom-call(s32[1]{0:T(128)S(6)} %copy.6.count_ref, f32[128,128]{1,0:T(8,128)S(1)} %get-tuple-element.29.own_ref.own_corner, f32[128,128]{1,0:T(8,128)S(1)} %collective-permute-done.4.other_ref.other_corner), custom_call_target="tpu_custom_call" | custom-call | flops 1000000000 | bytes 1000000 | tf_op jit(solution)/shard_map/pallas_call | solution.py:278
  68.1 0.3 collective-permute-done.3.other_ref.other_side
  68.4 0.0 copy-done.2
  68.4 3.0 %shard_map.50 = (f32[128,512]{1,0:T(8,128)S(1)}, f32[2,128,384]{2,1,0:T(8,128)S(1)}, f32[128,128]{1,0:T(8,128)S(1)}) custom-call(s32[1]{0:T(128)S(6)} %copy.6.count_ref, f32[128,128]{1,0:T(8,128)S(1)} %get-tuple-element.29.own_ref.own_corner, f32[128,128]{1,0:T(8,128)S(1)} %collective-permute-done.4.other_ref.other_corner, ...), custom_call_target="tpu_custom_call" | custom-call | flops 1000000000 | bytes 1000000 | tf_op jit(solution)/shard_map/pallas_call | solution.py:278
  71.5 0.0 collective-permute-done.2.other_late
  71.5 3.9 %shard_map.51 = bf16[384,256]{1,0:T(8,128)(2,1)S(1)} custom-call(s32[1]{0:T(128)S(6)} %copy.6.count_ref, f32[192,128]{1,0:T(8,128)S(1)} %get-tuple-element.23.own_late, f32[192,128]{1,0:T(8,128)S(1)} %collective-permute-done.2.other_late, f32[264,128]{1,0:T(8,128)S(1)} %get-tuple-element.27.own_ref.own_side, ...), custom_call_target="tpu_custom_call" | custom-call | flops 1000000000 | bytes 1000000 | tf_op jit(solution)/shard_map/pallas_call | solution.py:278
  75.4 0.1 collective-permute-start.5
  75.5 0.7 fusion.5
  76.2 9.1 %collective-permute-done.5 = bf16[384,256]{1,0:T(8,128)(2,1)S(1)} collective-permute-done((bf16[384,256]{1,0:T(8,128)(2,1)S(1)}, bf16[384,256]{1,0:T(8,128)(2,1)S(1)}, u32[]{:S(2)}, u32[]{:S(2)}) %collective-permute-start.5) | collective-permute-done | bytes 196640 | tf_op jit(solution)/shard_map/ppermute | solution.py:353
  85.3 0.7 fusion.4
  86.0 0.2 pad_maximum_fusion
  86.2 0.2 copy.5
  86.4 30.0 %all_to_all.11 = bf16[16,2,128,256]{3,2,1,0:T(8,128)(2,1)S(1)} all-to-all(bf16[16,2,128,256]{3,2,1,0:T(8,128)(2,1)S(1)} %copy.5), channel_id=1, replica_groups=mesh['half'=2,'inner'=4,'doppler'=4] {'inner','doppler'}, dimensions={0} | all-to-all | bytes 4194304 | tf_op jit(solution)/shard_map/all_to_all | solution.py:339
  116.5 0.1 dynamic-slice_bitcast_fusion.1
  116.6 1.5 %pad_maximum_fusion.1 = bf16[32,128,256]{2,1,0:T(8,128)(2,1)} fusion(bf16[16,128,256]{2,1,0:T(8,128)(2,1)S(1)} %get-tuple-element.38, bf16[16,128,256]{2,1,0:T(8,128)(2,1)S(1)} %get-tuple-element.37), kind=kLoop, calls=%fused_computation.1 | loop fusion | flops 1048576 | bytes 4194304 | tf_op jit(solution)/shard_map/concatenate | solution.py:366
  (1 shorter events, 0.0 us)
Async XLA Ops:
  0.0 8.7 %collective-permute-start = (s32[1,32]{1,0:T(1,128)}, s32[1,32]{1,0:T(1,128)S(1)}, u32[]{:S(2)}, u32[]{:S(2)}) collective-permute-start(s32[1,32]{1,0:T(1,128)} %list_ref.1), channel_id=1, source_target_pairs={{0,16},{16,0},{1,17},{17,1},{2,18},{18,2},{3,19},{19,3},{4,20},{20... | collective-permute-start | bytes 392 | tf_op jit(solution)/shard_map/ppermute | solution.py:341
  4.0 4.7 %collective-permute-start.1 = (s32[1]{0:T(128)}, s32[1]{0:T(128)}, u32[]{:S(2)}, u32[]{:S(2)}) collective-permute-start(s32[1]{0:T(128)} %param.7), channel_id=1, source_target_pairs={{0,16},{16,0},{1,17},{17,1},{2,18},{18,2},{3,19},{19,3},{4,20},{20... | collective-permute-start | bytes 20 | tf_op jit(solution)/shard_map/ppermute | solution.py:342
  4.1 1.9 %copy-start = (bf16[32,128,384]{2,1,0:T(8,128)(2,1)S(1)}, bf16[32,128,384]{2,1,0:T(8,128)(2,1)}, u32[]{:S(2)}) copy-start(bf16[32,128,384]{2,1,0:T(8,128)(2,1)} %param.4) | copy-start | bytes 9437188
  52.0 7.3 %copy-start.1 = (s32[1,32]{1,0:T(1,128)S(1)}, s32[1,32]{1,0:T(1,128)}, u32[]{:S(2)}) copy-start(s32[1,32]{1,0:T(1,128)} %list_ref.1) | copy-start | bytes 388
  54.0 11.5 %collective-permute-start.4 = (f32[128,128]{1,0:T(8,128)S(1)}, f32[128,128]{1,0:T(8,128)S(1)}, u32[]{:S(2)}, u32[]{:S(2)}) collective-permute-start(f32[128,128]{1,0:T(8,128)S(1)} %get-tuple-element.30), channel_id=1, source_target_pairs={{0,16},{16,0},{1,17},{17,1},{2,18},{18,2},{3,19},{19,3},{4,20},{20... | collective-permute-start | bytes 196616 | tf_op jit(solution)/shard_map/ppermute | solution.py:350
  56.3 12.2 %collective-permute-start.3 = (f32[264,128]{1,0:T(8,128)S(1)}, f32[264,128]{1,0:T(8,128)S(1)}, u32[]{:S(2)}, u32[]{:S(2)}) collective-permute-start(f32[264,128]{1,0:T(8,128)S(1)} %get-tuple-element.28), channel_id=1, source_target_pairs={{0,16},{16,0},{1,17},{17,1},{2,18},{18,2},{3,19},{19,3},{4,20},{20... | collective-permute-start | bytes 405512 | tf_op jit(solution)/shard_map/ppermute | solution.py:350
  57.7 13.8 %collective-permute-start.2 = (f32[192,128]{1,0:T(8,128)S(1)}, f32[192,128]{1,0:T(8,128)S(1)}, u32[]{:S(2)}, u32[]{:S(2)}) collective-permute-start(f32[192,128]{1,0:T(8,128)S(1)} %get-tuple-element.26), channel_id=1, source_target_pairs={{0,16},{16,0},{1,17},{17,1},{2,18},{18,2},{3,19},{19,3},{4,20},{20... | collective-permute-start | bytes 294920 | tf_op jit(solution)/shard_map/ppermute | solution.py:350
  60.7 7.7 %copy-start.2 = (bf16[1,384,256]{2,1,0:T(8,128)(2,1)S(1)}, bf16[1,384,256]{2,1,0:T(8,128)(2,1)}, u32[]{:S(2)}) copy-start(bf16[1,384,256]{2,1,0:T(8,128)(2,1)} %param.5) | copy-start | bytes 589828
  75.4 9.9 %collective-permute-start.5 = (bf16[384,256]{1,0:T(8,128)(2,1)S(1)}, bf16[384,256]{1,0:T(8,128)(2,1)S(1)}, u32[]{:S(2)}, u32[]{:S(2)}) collective-permute-start(bf16[384,256]{1,0:T(8,128)(2,1)S(1)} %shard_map.51), channel_id=1, source_target_pairs={{0,16},{16,0},{1,17},{17,1},{2,18},{18,2},{3,19},{19,3},{4,20},{20... | collective-permute-start | bytes 589832 | tf_op jit(solution)/shard_map/ppermute | solution.py:353

commit v10 on v9

--- a/solution.py
+++ b/solution.py
@@ -17,7 +17,6 @@
 EVERY = ("half",) + INNER
 VMEM_BYTES = 16 * 1024 * 1024
 TURNED = (((0,), (0,)), ((), ()))
-SPLIT_BYTES = 16 * 1024 * 1024
 
 
 def edge_iota(dim, rows=EDGE):
@@ -117,8 +116,13 @@
     sub = lax.broadcasted_iota(jnp.int32, full, 0)
     lane = lax.broadcasted_iota(jnp.int32, full, 1)
 
+    piece = lax.broadcasted_iota(jnp.int32, (8, EDGE), 0)
+
     def row(x, k):
-        return jnp.broadcast_to(x[k : k + 1], full)
+        return jnp.broadcast_to(x[k : k + 1], (8, EDGE))
+
+    def cut(x):
+        return [x[q : q + 8] for q in range(0, STEP, 8)]
 
     strips = [block[q : q + STEP] for q in range(0, EDGE, STEP)]
     rows = strips[0]
@@ -128,20 +132,30 @@
         cols = spread(rows, at)
         ahead = spread(strips[p + 1], at) if p + 1 < panels else None
         rows = jnp.where(inside, jnp.where(lane == sub + at, 1.0, 0.0), rows)
-        pivots = jnp.zeros(full, jnp.float32)
+        cols = [cut(x) for x in cols]
+        done = cut(rows)
+        pivots = cut(jnp.zeros(full, jnp.float32))
         terms = []
         for k in range(STEP):
-            inv = 1.0 / row(cols[k], k)
-            pivots = jnp.where(sub == k, cols[k], pivots)
-            factor = jnp.where(sub > k, cols[k] * inv, 0.0)
+            own, at_k = divmod(k, 8)
+            inv = 1.0 / row(cols[k][own], at_k)
+            pivots[own] = jnp.where(piece == at_k, cols[k][own], pivots[own])
+            factors = {own: jnp.where(piece > at_k, cols[k][own] * inv, 0.0)}
+            for q in range(own + 1, STEP // 8):
+                factors[q] = cols[k][q] * inv
+            used = row(done[own], at_k)
             if ahead is not None:
-                terms.append(ahead[k] * (row(rows, k) * inv))
+                terms.append(ahead[k] * jnp.concatenate([used * inv] * (STEP // 8), axis=0))
             for i in range(k + 1, STEP):
-                value = row(cols[i], k)
-                cols[i] = cols[i] - factor * value
+                value = row(cols[i][own], at_k)
+                for q, factor in factors.items():
+                    cols[i][q] = cols[i][q] - factor * value
                 if ahead is not None:
-                    ahead[i] = ahead[i] - ahead[k] * (value * inv)
-            rows = rows - factor * row(rows, k)
+                    scaled = jnp.concatenate([value * inv] * (STEP // 8), axis=0)
+                    ahead[i] = ahead[i] - ahead[k] * scaled
+            for q, factor in factors.items():
+                done[q] = done[q] - factor * used
+        rows, pivots = jnp.concatenate(done, axis=0), jnp.concatenate(pivots, axis=0)
         made = rows * lax.rsqrt(pivots)
         if ahead is not None:
             while len(terms) > 1:
@@ -301,29 +315,33 @@
     )
 
 
-def split_kernel(which_ref, x_ref, out_ref):
-    out_ref[:, 0] = x_ref[0]
+def split_kernel(which_ref, x_ref, out_ref, sems):
+    halves, group = x_ref.shape[:2]
+    chunk = group // 4
+    copies = []
+    for s in range(halves):
+        for i in range(4):
+            part = pl.ds(i * chunk, chunk)
+            copies.append(
+                pltpu.make_async_copy(
+                    x_ref.at[which_ref[s], part], out_ref.at[part, s], sems.at[s, i]
+                )
+            )
+    for copy in copies:
+        copy.start()
+    for copy in copies:
+        copy.wait()
 
 
 def split(which, x):
     halves, group, rows, wide = x.shape
-    chunks = 4
     return pl.pallas_call(
         split_kernel,
         out_shape=jax.ShapeDtypeStruct((group, halves, rows, wide), x.dtype),
-        grid_spec=pltpu.PrefetchScalarGridSpec(
-            num_scalar_prefetch=1,
-            grid=(halves, chunks),
-            in_specs=[
-                pl.BlockSpec(
-                    (1, group // chunks, rows, wide), lambda s, i, which: (which[s], i, 0, 0)
-                )
-            ],
-            out_specs=pl.BlockSpec(
-                (group // chunks, 1, rows, wide), lambda s, i, which: (i, s, 0, 0)
-            ),
-        ),
-        compiler_params=pltpu.CompilerParams(vmem_limit_bytes=SPLIT_BYTES),
+        in_specs=[pl.BlockSpec(memory_space=pltpu.SMEM), pl.BlockSpec(memory_space=pltpu.HBM)],
+        out_specs=pl.BlockSpec(memory_space=pltpu.VMEM),
+        scratch_shapes=[pltpu.SemaphoreType.DMA((halves, 4))],
+        compiler_params=pltpu.CompilerParams(vmem_limit_bytes=2 * VMEM_BYTES),
         cost_estimate=pl.CostEstimate(flops=0, bytes_accessed=2 * x.size, transcendentals=0),
     )(which, x)
 

time: 118 us -> 118 us (level)
  no operation moved by 1% of the time
where the time goes in v10:
time: 118 us
  blocking collectives  73.3 us (62%)
  waiting for transfers between devices  15.9 us (13%)
  Pallas kernels  14 us (12%)
  starting transfers between devices  8.55 us (7%)
  local copies, waits for them, and re-layouts  2.24 us (2%)
  other arithmetic  1.77 us (2%)
  matrix products  1.4 us (1%)
    all_to_all x2, blocking collectives, exchange(): return lax.all_to_all(x, INNER, split_axis=0, concat_axis=0, tiled=True)  73.3 us
    pallas_call x3, Pallas kernels, call(): pl.pallas_call(kernel, out_shape=out_shape, in_specs=[smem] + [vmem] * le...  9.46 us
    ppermute x1, waiting for transfers between devices, body(): other_weights = lax.ppermute(weights, 'half', peers)  9.02 us
    ppermute x3, waiting for transfers between devices, body(): arrived = [lax.ppermute(x, 'half', peers) for x in other_gram]  5.35 us
    ppermute x3, starting transfers between devices, body(): arrived = [lax.ppermute(x, 'half', peers) for x in other_gram]  4.41 us
    ppermute x1, starting transfers between devices, body(): other_list = lax.ppermute(train_list, 'half', peers)  4.04 us
    pallas_call x2, Pallas kernels, partial_gram(): pl.pallas_call(functools.partial(gram_kernel, which), out_shape=[jax.Shap...  3.45 us
  transfers between devices with their start and end apart: 6, of which 4 were waited for; matrix products, arithmetic and copies ran while one was open for 1% of the time, Pallas kernels for 7%

profile of v10, /device:TPU:0, one launch (start us, length us, event | category | flops | bytes accessed | tf_op | source)
XLA Modules:
  0.0 118.0 jit_solution(1017919477480950735)
XLA Ops:
  0.0 4.0 %collective-permute-start = (s32[1,32]{1,0:T(1,128)}, s32[1,32]{1,0:T(1,128)S(1)}, u32[]{:S(2)}, u32[]{:S(2)}) collective-permute-start(s32[1,32]{1,0:T(1,128)} %list_ref.1), channel_id=1, source_target_pairs={{0,16},{16,0},{1,17},{17,1},{2,18},{18,2},{3,19},{19,3},{4,20},{20... | collective-permute-start | bytes 392 | tf_op jit(solution)/shard_map/ppermute | solution.py:359
  4.0 0.0 collective-permute-start.1
  4.1 0.1 pad_add_fusion.which_ref
  4.1 0.0 copy-start
  4.1 1.9 %copy-done = bf16[32,128,384]{2,1,0:T(8,128)(2,1)S(1)} copy-done((bf16[32,128,384]{2,1,0:T(8,128)(2,1)S(1)}, bf16[32,128,384]{2,1,0:T(8,128)(2,1)}, u32[]{:S(2)}) %copy-start) | copy-done | bytes 3145752
  6.0 1.1 shard_map.46
  7.2 1.6 %collective-permute-done.1.count_ref = s32[1]{0:T(128)} collective-permute-done((s32[1]{0:T(128)}, s32[1]{0:T(128)}, u32[]{:S(2)}, u32[]{:S(2)}) %collective-permute-start.1) | collective-permute-done | bytes 36 | tf_op jit(solution)/shard_map/ppermute | solution.py:360
  8.7 0.0 collective-permute-done.list_ref
  8.7 43.3 %all_to_all.10.blocks_ref = bf16[16,2,128,384]{3,2,1,0:T(8,128)(2,1)S(1)} all-to-all(bf16[16,2,128,384]{3,2,1,0:T(8,128)(2,1)S(1)} %shard_map.46), channel_id=1, replica_groups=mesh['half'=2,'inner'=4,'doppler'=4] {'inner','doppler'}, dimensions={0} | all-to-all | bytes 6291456 | tf_op jit(solution)/shard_map/all_to_all | solution.py:357
  52.0 2.0 %shard_map.48 = (f32[128,128]{1,0:T(8,128)S(1)}, f32[264,128]{1,0:T(8,128)S(1)}, f32[192,128]{1,0:T(8,128)S(1)}) custom-call(s32[1]{0:T(128)S(6)} %mul.3.base_ref, s32[1,32]{1,0:T(1,128)S(1)} %collective-permute-done.list_ref, s32[1]{0:T(128)} %collective-permute-done.1.count_ref, bf16[16,2,128,384]{3,2,1,0:T(8,128)(2,1)S(1)} %all_to_all.10.blocks_ref), custom_call_target="tpu_custom_call" | custom-call | flops 603979776 | bytes 1572864 | tf_op jit(solution)/shard_map/pallas_call | solution.py:63
  54.0 1.4 %collective-permute-start.4 = (f32[128,128]{1,0:T(8,128)S(1)}, f32[128,128]{1,0:T(8,128)S(1)}, u32[]{:S(2)}, u32[]{:S(2)}) collective-permute-start(f32[128,128]{1,0:T(8,128)S(1)} %get-tuple-element.30), channel_id=1, source_target_pairs={{0,16},{16,0},{1,17},{17,1},{2,18},{18,2},{3,19},{19,3},{4,20},{20... | collective-permute-start | bytes 196616 | tf_op jit(solution)/shard_map/ppermute | solution.py:368
  56.1 1.6 %collective-permute-start.3 = (f32[264,128]{1,0:T(8,128)S(1)}, f32[264,128]{1,0:T(8,128)S(1)}, u32[]{:S(2)}, u32[]{:S(2)}) collective-permute-start(f32[264,128]{1,0:T(8,128)S(1)} %get-tuple-element.28), channel_id=1, source_target_pairs={{0,16},{16,0},{1,17},{17,1},{2,18},{18,2},{3,19},{19,3},{4,20},{20... | collective-permute-start | bytes 405512 | tf_op jit(solution)/shard_map/ppermute | solution.py:368
  57.7 1.4 %collective-permute-start.2 = (f32[192,128]{1,0:T(8,128)S(1)}, f32[192,128]{1,0:T(8,128)S(1)}, u32[]{:S(2)}, u32[]{:S(2)}) collective-permute-start(f32[192,128]{1,0:T(8,128)S(1)} %get-tuple-element.26), channel_id=1, source_target_pairs={{0,16},{16,0},{1,17},{17,1},{2,18},{18,2},{3,19},{19,3},{4,20},{20... | collective-permute-start | bytes 294920 | tf_op jit(solution)/shard_map/ppermute | solution.py:368
  59.1 0.0 copy-done.1
  59.1 1.4 %shard_map.47 = (f32[128,128]{1,0:T(8,128)S(1)}, f32[264,128]{1,0:T(8,128)S(1)}, f32[192,128]{1,0:T(8,128)S(1)}) custom-call(s32[1]{0:T(128)S(6)} %mul.3.base_ref, s32[1,32]{1,0:T(1,128)S(1)} %copy-done.1, s32[1]{0:T(128)S(6)} %copy.6.count_ref, bf16[16,2,128,384]{3,2,1,0:T(8,128)(2,1)S(1)} %all_to_all.10.blocks_ref), custom_call_target="tpu_custom_call" | custom-call | flops 603979776 | bytes 1572864 | tf_op jit(solution)/shard_map/pallas_call | solution.py:63
  60.5 0.0 copy-start.2
  60.5 5.0 %collective-permute-done.4.other_ref.other_corner = f32[128,128]{1,0:T(8,128)S(1)} collective-permute-done((f32[128,128]{1,0:T(8,128)S(1)}, f32[128,128]{1,0:T(8,128)S(1)}, u32[]{:S(2)}, u32[]{:S(2)}) %collective-permute-start.4) | collective-permute-done | bytes 65568 | tf_op jit(solution)/shard_map/ppermute | solution.py:368
  65.5 2.6 %shard_map.49.lower_ref = f32[128,128]{1,0:T(8,128)S(1)} custom-call(s32[1]{0:T(128)S(6)} %copy.6.count_ref, f32[128,128]{1,0:T(8,128)S(1)} %get-tuple-element.29.own_ref.own_corner, f32[128,128]{1,0:T(8,128)S(1)} %collective-permute-done.4.other_ref.other_corner), custom_call_target="tpu_custom_call" | custom-call | flops 1000000000 | bytes 1000000 | tf_op jit(solution)/shard_map/pallas_call | solution.py:292
  68.1 0.3 collective-permute-done.3.other_ref.other_side
  68.4 0.0 copy-done.2
  68.4 3.0 %shard_map.50 = (f32[128,512]{1,0:T(8,128)S(1)}, f32[2,128,384]{2,1,0:T(8,128)S(1)}, f32[128,128]{1,0:T(8,128)S(1)}) custom-call(s32[1]{0:T(128)S(6)} %copy.6.count_ref, f32[128,128]{1,0:T(8,128)S(1)} %get-tuple-element.29.own_ref.own_corner, f32[128,128]{1,0:T(8,128)S(1)} %collective-permute-done.4.other_ref.other_corner, ...), custom_call_target="tpu_custom_call" | custom-call | flops 1000000000 | bytes 1000000 | tf_op jit(solution)/shard_map/pallas_call | solution.py:292
  71.4 0.0 collective-permute-done.2.other_late
  71.5 3.9 %shard_map.51 = bf16[384,256]{1,0:T(8,128)(2,1)S(1)} custom-call(s32[1]{0:T(128)S(6)} %copy.6.count_ref, f32[192,128]{1,0:T(8,128)S(1)} %get-tuple-element.23.own_late, f32[192,128]{1,0:T(8,128)S(1)} %collective-permute-done.2.other_late, f32[264,128]{1,0:T(8,128)S(1)} %get-tuple-element.27.own_ref.own_side, ...), custom_call_target="tpu_custom_call" | custom-call | flops 1000000000 | bytes 1000000 | tf_op jit(solution)/shard_map/pallas_call | solution.py:292
  75.4 0.1 collective-permute-start.5
  75.4 0.7 fusion.5
  76.2 9.0 %collective-permute-done.5 = bf16[384,256]{1,0:T(8,128)(2,1)S(1)} collective-permute-done((bf16[384,256]{1,0:T(8,128)(2,1)S(1)}, bf16[384,256]{1,0:T(8,128)(2,1)S(1)}, u32[]{:S(2)}, u32[]{:S(2)}) %collective-permute-start.5) | collective-permute-done | bytes 196640 | tf_op jit(solution)/shard_map/ppermute | solution.py:371
  85.2 0.7 fusion.4
  85.9 0.2 pad_maximum_fusion
  86.1 0.2 copy.5
  86.3 30.0 %all_to_all.11 = bf16[16,2,128,256]{3,2,1,0:T(8,128)(2,1)S(1)} all-to-all(bf16[16,2,128,256]{3,2,1,0:T(8,128)(2,1)S(1)} %copy.5), channel_id=1, replica_groups=mesh['half'=2,'inner'=4,'doppler'=4] {'inner','doppler'}, dimensions={0} | all-to-all | bytes 4194304 | tf_op jit(solution)/shard_map/all_to_all | solution.py:357
  116.3 0.1 dynamic-slice_bitcast_fusion.1
  116.5 1.5 %pad_maximum_fusion.1 = bf16[32,128,256]{2,1,0:T(8,128)(2,1)} fusion(bf16[16,128,256]{2,1,0:T(8,128)(2,1)S(1)} %get-tuple-element.38, bf16[16,128,256]{2,1,0:T(8,128)(2,1)S(1)} %get-tuple-element.37), kind=kLoop, calls=%fused_computation.1 | loop fusion | flops 1048576 | bytes 4194304 | tf_op jit(solution)/shard_map/concatenate | solution.py:384
  (1 shorter events, 0.0 us)
Async XLA Ops:
  0.0 8.7 %collective-permute-start = (s32[1,32]{1,0:T(1,128)}, s32[1,32]{1,0:T(1,128)S(1)}, u32[]{:S(2)}, u32[]{:S(2)}) collective-permute-start(s32[1,32]{1,0:T(1,128)} %list_ref.1), channel_id=1, source_target_pairs={{0,16},{16,0},{1,17},{17,1},{2,18},{18,2},{3,19},{19,3},{4,20},{20... | collective-permute-start | bytes 392 | tf_op jit(solution)/shard_map/ppermute | solution.py:359
  4.0 4.7 %collective-permute-start.1 = (s32[1]{0:T(128)}, s32[1]{0:T(128)}, u32[]{:S(2)}, u32[]{:S(2)}) collective-permute-start(s32[1]{0:T(128)} %param.7), channel_id=1, source_target_pairs={{0,16},{16,0},{1,17},{17,1},{2,18},{18,2},{3,19},{19,3},{4,20},{20... | collective-permute-start | bytes 20 | tf_op jit(solution)/shard_map/ppermute | solution.py:360
  4.1 1.9 %copy-start = (bf16[32,128,384]{2,1,0:T(8,128)(2,1)S(1)}, bf16[32,128,384]{2,1,0:T(8,128)(2,1)}, u32[]{:S(2)}) copy-start(bf16[32,128,384]{2,1,0:T(8,128)(2,1)} %param.4) | copy-start | bytes 9437188
  52.0 7.1 %copy-start.1 = (s32[1,32]{1,0:T(1,128)S(1)}, s32[1,32]{1,0:T(1,128)}, u32[]{:S(2)}) copy-start(s32[1,32]{1,0:T(1,128)} %list_ref.1) | copy-start | bytes 388
  54.0 11.5 %collective-permute-start.4 = (f32[128,128]{1,0:T(8,128)S(1)}, f32[128,128]{1,0:T(8,128)S(1)}, u32[]{:S(2)}, u32[]{:S(2)}) collective-permute-start(f32[128,128]{1,0:T(8,128)S(1)} %get-tuple-element.30), channel_id=1, source_target_pairs={{0,16},{16,0},{1,17},{17,1},{2,18},{18,2},{3,19},{19,3},{4,20},{20... | collective-permute-start | bytes 196616 | tf_op jit(solution)/shard_map/ppermute | solution.py:368
  56.1 12.4 %collective-permute-start.3 = (f32[264,128]{1,0:T(8,128)S(1)}, f32[264,128]{1,0:T(8,128)S(1)}, u32[]{:S(2)}, u32[]{:S(2)}) collective-permute-start(f32[264,128]{1,0:T(8,128)S(1)} %get-tuple-element.28), channel_id=1, source_target_pairs={{0,16},{16,0},{1,17},{17,1},{2,18},{18,2},{3,19},{19,3},{4,20},{20... | collective-permute-start | bytes 405512 | tf_op jit(solution)/shard_map/ppermute | solution.py:368
  57.7 13.7 %collective-permute-start.2 = (f32[192,128]{1,0:T(8,128)S(1)}, f32[192,128]{1,0:T(8,128)S(1)}, u32[]{:S(2)}, u32[]{:S(2)}) collective-permute-start(f32[192,128]{1,0:T(8,128)S(1)} %get-tuple-element.26), channel_id=1, source_target_pairs={{0,16},{16,0},{1,17},{17,1},{2,18},{18,2},{3,19},{19,3},{4,20},{20... | collective-permute-start | bytes 294920 | tf_op jit(solution)/shard_map/ppermute | solution.py:368
  60.5 7.9 %copy-start.2 = (bf16[1,384,256]{2,1,0:T(8,128)(2,1)S(1)}, bf16[1,384,256]{2,1,0:T(8,128)(2,1)}, u32[]{:S(2)}) copy-start(bf16[1,384,256]{2,1,0:T(8,128)(2,1)} %param.5) | copy-start | bytes 589828
  75.4 9.8 %collective-permute-start.5 = (bf16[384,256]{1,0:T(8,128)(2,1)S(1)}, bf16[384,256]{1,0:T(8,128)(2,1)S(1)}, u32[]{:S(2)}, u32[]{:S(2)}) collective-permute-start(bf16[384,256]{1,0:T(8,128)(2,1)S(1)} %shard_map.51), channel_id=1, source_target_pairs={{0,16},{16,0},{1,17},{17,1},{2,18},{18,2},{3,19},{19,3},{4,20},{20... | collective-permute-start | bytes 589832 | tf_op jit(solution)/shard_map/ppermute | solution.py:371

commit v11 on v10

--- a/solution.py
+++ b/solution.py
@@ -362,11 +362,14 @@
     outgoing, other_list, other_count, base = lax.optimization_barrier(
         (outgoing, other_list, other_count, base)
     )
-    blocks = exchange(outgoing)
+    blocks, train_list, train_count = lax.optimization_barrier(
+        (exchange(outgoing), train_list, train_count)
+    )
 
     other_gram = partial_gram(1, base, other_list, other_count, blocks)
-    arrived = [lax.ppermute(x, "half", peers) for x in other_gram]
     own_gram = partial_gram(0, base, train_list, train_count, blocks)
+    last, own_gram = lax.optimization_barrier((other_gram[2], own_gram))
+    arrived = [lax.ppermute(x, "half", peers) for x in (other_gram[0], other_gram[1], last)]
     weights = make_weights(train_count, own_gram, arrived, steering[0])
     other_weights = lax.ppermute(weights, "half", peers)
 

time: 118 us -> 118 us (level)
  no operation moved by 1% of the time
where the time goes in v11:
time: 118 us
  blocking collectives  73.3 us (62%)
  waiting for transfers between devices  15.9 us (13%)
  Pallas kernels  14 us (12%)
  starting transfers between devices  8.62 us (7%)
  local copies, waits for them, and re-layouts  2.24 us (2%)
  other arithmetic  1.77 us (2%)
  matrix products  1.4 us (1%)
    all_to_all x2, blocking collectives, exchange(): return lax.all_to_all(x, INNER, split_axis=0, concat_axis=0, tiled=True)  73.3 us
    pallas_call x3, Pallas kernels, call(): pl.pallas_call(kernel, out_shape=out_shape, in_specs=[smem] + [vmem] * le...  9.46 us
    ppermute x1, waiting for transfers between devices, body(): other_weights = lax.ppermute(weights, 'half', peers)  9.02 us
    ppermute x3, waiting for transfers between devices, body(): lax.ppermute(x, 'half', peers)  5.28 us
    ppermute x3, starting transfers between devices, body(): lax.ppermute(x, 'half', peers)  4.48 us
    ppermute x1, starting transfers between devices, body(): other_list = lax.ppermute(train_list, 'half', peers)  4.04 us
    pallas_call x2, Pallas kernels, partial_gram(): pl.pallas_call(functools.partial(gram_kernel, which), out_shape=[jax.Shap...  3.45 us
  transfers between devices with their start and end apart: 6, of which 4 were waited for; matrix products, arithmetic and copies ran while one was open for 1% of the time, Pallas kernels for 7%

profile of v11, /device:TPU:0, one launch (start us, length us, event | category | flops | bytes accessed | tf_op | source)
XLA Modules:
  0.0 118.0 jit_solution(12008914117510244943)
XLA Ops:
  0.0 4.0 %collective-permute-start = (s32[1,32]{1,0:T(1,128)}, s32[1,32]{1,0:T(1,128)S(1)}, u32[]{:S(2)}, u32[]{:S(2)}) collective-permute-start(s32[1,32]{1,0:T(1,128)} %list_ref), channel_id=1, source_target_pairs={{0,16},{16,0},{1,17},{17,1},{2,18},{18,2},{3,19},{19,3},{4,20},{20... | collective-permute-start | bytes 392 | tf_op jit(solution)/shard_map/ppermute | solution.py:359
  4.0 0.0 collective-permute-start.1
  4.1 0.1 pad_add_fusion.which_ref
  4.1 0.0 copy-start
  4.1 1.9 %copy-done = bf16[32,128,384]{2,1,0:T(8,128)(2,1)S(1)} copy-done((bf16[32,128,384]{2,1,0:T(8,128)(2,1)S(1)}, bf16[32,128,384]{2,1,0:T(8,128)(2,1)}, u32[]{:S(2)}) %copy-start) | copy-done | bytes 3145752
  6.0 1.1 shard_map.46
  7.2 1.6 %collective-permute-done.1.count_ref = s32[1]{0:T(128)} collective-permute-done((s32[1]{0:T(128)}, s32[1]{0:T(128)}, u32[]{:S(2)}, u32[]{:S(2)}) %collective-permute-start.1) | collective-permute-done | bytes 36 | tf_op jit(solution)/shard_map/ppermute | solution.py:360
  8.7 0.0 collective-permute-done.list_ref
  8.7 43.3 %all_to_all.10.blocks_ref = bf16[16,2,128,384]{3,2,1,0:T(8,128)(2,1)S(1)} all-to-all(bf16[16,2,128,384]{3,2,1,0:T(8,128)(2,1)S(1)} %shard_map.46), channel_id=1, replica_groups=mesh['half'=2,'inner'=4,'doppler'=4] {'inner','doppler'}, dimensions={0} | all-to-all | bytes 6291456 | tf_op jit(solution)/shard_map/all_to_all | solution.py:357
  52.0 2.0 %shard_map.47 = (f32[128,128]{1,0:T(8,128)S(1)}, f32[264,128]{1,0:T(8,128)S(1)}, f32[192,128]{1,0:T(8,128)S(1)}) custom-call(s32[1]{0:T(128)S(6)} %mul.3.base_ref, s32[1,32]{1,0:T(1,128)S(1)} %collective-permute-done.list_ref, s32[1]{0:T(128)} %collective-permute-done.1.count_ref, bf16[16,2,128,384]{3,2,1,0:T(8,128)(2,1)S(1)} %all_to_all.10.blocks_ref), custom_call_target="tpu_custom_call" | custom-call | flops 603979776 | bytes 1572864 | tf_op jit(solution)/shard_map/pallas_call | solution.py:63
  54.0 1.4 %collective-permute-start.4 = (f32[128,128]{1,0:T(8,128)S(1)}, f32[128,128]{1,0:T(8,128)S(1)}, u32[]{:S(2)}, u32[]{:S(2)}) collective-permute-start(f32[128,128]{1,0:T(8,128)S(1)} %get-tuple-element.44), channel_id=1, source_target_pairs={{0,16},{16,0},{1,17},{17,1},{2,18},{18,2},{3,19},{19,3},{4,20},{20... | collective-permute-start | bytes 196616 | tf_op jit(solution)/shard_map/ppermute | solution.py:372
  56.1 1.6 %collective-permute-start.3 = (f32[264,128]{1,0:T(8,128)S(1)}, f32[264,128]{1,0:T(8,128)S(1)}, u32[]{:S(2)}, u32[]{:S(2)}) collective-permute-start(f32[264,128]{1,0:T(8,128)S(1)} %get-tuple-element.42), channel_id=1, source_target_pairs={{0,16},{16,0},{1,17},{17,1},{2,18},{18,2},{3,19},{19,3},{4,20},{20... | collective-permute-start | bytes 405512 | tf_op jit(solution)/shard_map/ppermute | solution.py:372
  57.7 0.0 copy-done.1
  57.7 1.4 %shard_map.48 = (f32[128,128]{1,0:T(8,128)S(1)}, f32[264,128]{1,0:T(8,128)S(1)}, f32[192,128]{1,0:T(8,128)S(1)}) custom-call(s32[1]{0:T(128)S(6)} %mul.3.base_ref, s32[1,32]{1,0:T(1,128)S(1)} %copy-done.1, s32[1]{0:T(128)S(6)} %copy.6.count_ref, bf16[16,2,128,384]{3,2,1,0:T(8,128)(2,1)S(1)} %all_to_all.10.blocks_ref), custom_call_target="tpu_custom_call" | custom-call | flops 603979776 | bytes 1572864 | tf_op jit(solution)/shard_map/pallas_call | solution.py:63
  59.2 0.0 copy-start.2
  59.2 1.4 %collective-permute-start.2 = (f32[192,128]{1,0:T(8,128)S(1)}, f32[192,128]{1,0:T(8,128)S(1)}, u32[]{:S(2)}, u32[]{:S(2)}) collective-permute-start(f32[192,128]{1,0:T(8,128)S(1)} %get-tuple-element.40), channel_id=1, source_target_pairs={{0,16},{16,0},{1,17},{17,1},{2,18},{18,2},{3,19},{19,3},{4,20},{20... | collective-permute-start | bytes 294920 | tf_op jit(solution)/shard_map/ppermute | solution.py:372
  60.6 4.9 %collective-permute-done.4.other_ref.other_corner = f32[128,128]{1,0:T(8,128)S(1)} collective-permute-done((f32[128,128]{1,0:T(8,128)S(1)}, f32[128,128]{1,0:T(8,128)S(1)}, u32[]{:S(2)}, u32[]{:S(2)}) %collective-permute-start.4) | collective-permute-done | bytes 65568 | tf_op jit(solution)/shard_map/ppermute | solution.py:372
  65.5 2.6 %shard_map.49.lower_ref = f32[128,128]{1,0:T(8,128)S(1)} custom-call(s32[1]{0:T(128)S(6)} %copy.6.count_ref, f32[128,128]{1,0:T(8,128)S(1)} %get-tuple-element.43.own_ref.own_corner, f32[128,128]{1,0:T(8,128)S(1)} %collective-permute-done.4.other_ref.other_corner), custom_call_target="tpu_custom_call" | custom-call | flops 1000000000 | bytes 1000000 | tf_op jit(solution)/shard_map/pallas_call | solution.py:292
  68.1 0.3 collective-permute-done.3.other_ref.other_side
  68.4 0.0 copy-done.2
  68.4 3.0 %shard_map.50 = (f32[128,512]{1,0:T(8,128)S(1)}, f32[2,128,384]{2,1,0:T(8,128)S(1)}, f32[128,128]{1,0:T(8,128)S(1)}) custom-call(s32[1]{0:T(128)S(6)} %copy.6.count_ref, f32[128,128]{1,0:T(8,128)S(1)} %get-tuple-element.43.own_ref.own_corner, f32[128,128]{1,0:T(8,128)S(1)} %collective-permute-done.4.other_ref.other_corner, ...), custom_call_target="tpu_custom_call" | custom-call | flops 1000000000 | bytes 1000000 | tf_op jit(solution)/shard_map/pallas_call | solution.py:292
  71.4 0.0 collective-permute-done.2.other_late
  71.5 3.9 %shard_map.51 = bf16[384,256]{1,0:T(8,128)(2,1)S(1)} custom-call(s32[1]{0:T(128)S(6)} %copy.6.count_ref, f32[192,128]{1,0:T(8,128)S(1)} %get-tuple-element.39.own_late, f32[192,128]{1,0:T(8,128)S(1)} %collective-permute-done.2.other_late, f32[264,128]{1,0:T(8,128)S(1)} %get-tuple-element.41.own_ref.own_side, ...), custom_call_target="tpu_custom_call" | custom-call | flops 1000000000 | bytes 1000000 | tf_op jit(solution)/shard_map/pallas_call | solution.py:292
  75.4 0.1 collective-permute-start.5
  75.4 0.7 fusion.15
  76.2 9.0 %collective-permute-done.5 = bf16[384,256]{1,0:T(8,128)(2,1)S(1)} collective-permute-done((bf16[384,256]{1,0:T(8,128)(2,1)S(1)}, bf16[384,256]{1,0:T(8,128)(2,1)S(1)}, u32[]{:S(2)}, u32[]{:S(2)}) %collective-permute-start.5) | collective-permute-done | bytes 196640 | tf_op jit(solution)/shard_map/ppermute | solution.py:374
  85.2 0.7 fusion.12
  85.9 0.2 pad_maximum_fusion
  86.1 0.2 copy.5
  86.3 30.0 %all_to_all.11 = bf16[16,2,128,256]{3,2,1,0:T(8,128)(2,1)S(1)} all-to-all(bf16[16,2,128,256]{3,2,1,0:T(8,128)(2,1)S(1)} %copy.5), channel_id=1, replica_groups=mesh['half'=2,'inner'=4,'doppler'=4] {'inner','doppler'}, dimensions={0} | all-to-all | bytes 4194304 | tf_op jit(solution)/shard_map/all_to_all | solution.py:357
  116.3 0.1 dynamic-slice_bitcast_fusion.1
  116.5 1.5 %pad_maximum_fusion.1 = bf16[32,128,256]{2,1,0:T(8,128)(2,1)} fusion(bf16[16,128,256]{2,1,0:T(8,128)(2,1)S(1)} %get-tuple-element.52, bf16[16,128,256]{2,1,0:T(8,128)(2,1)S(1)} %get-tuple-element.51), kind=kLoop, calls=%fused_computation.1 | loop fusion | flops 1048576 | bytes 4194304 | tf_op jit(solution)/shard_map/concatenate | solution.py:387
  (1 shorter events, 0.0 us)
Async XLA Ops:
  0.0 8.7 %collective-permute-start = (s32[1,32]{1,0:T(1,128)}, s32[1,32]{1,0:T(1,128)S(1)}, u32[]{:S(2)}, u32[]{:S(2)}) collective-permute-start(s32[1,32]{1,0:T(1,128)} %list_ref), channel_id=1, source_target_pairs={{0,16},{16,0},{1,17},{17,1},{2,18},{18,2},{3,19},{19,3},{4,20},{20... | collective-permute-start | bytes 392 | tf_op jit(solution)/shard_map/ppermute | solution.py:359
  4.0 4.7 %collective-permute-start.1 = (s32[1]{0:T(128)}, s32[1]{0:T(128)}, u32[]{:S(2)}, u32[]{:S(2)}) collective-permute-start(s32[1]{0:T(128)} %param.7), channel_id=1, source_target_pairs={{0,16},{16,0},{1,17},{17,1},{2,18},{18,2},{3,19},{19,3},{4,20},{20... | collective-permute-start | bytes 20 | tf_op jit(solution)/shard_map/ppermute | solution.py:360
  4.1 1.9 %copy-start = (bf16[32,128,384]{2,1,0:T(8,128)(2,1)S(1)}, bf16[32,128,384]{2,1,0:T(8,128)(2,1)}, u32[]{:S(2)}) copy-start(bf16[32,128,384]{2,1,0:T(8,128)(2,1)} %param.4) | copy-start | bytes 9437188
  52.0 5.7 %copy-start.1 = (s32[1,32]{1,0:T(1,128)S(1)}, s32[1,32]{1,0:T(1,128)}, u32[]{:S(2)}) copy-start(s32[1,32]{1,0:T(1,128)} %list_ref) | copy-start | bytes 388
  54.0 11.5 %collective-permute-start.4 = (f32[128,128]{1,0:T(8,128)S(1)}, f32[128,128]{1,0:T(8,128)S(1)}, u32[]{:S(2)}, u32[]{:S(2)}) collective-permute-start(f32[128,128]{1,0:T(8,128)S(1)} %get-tuple-element.44), channel_id=1, source_target_pairs={{0,16},{16,0},{1,17},{17,1},{2,18},{18,2},{3,19},{19,3},{4,20},{20... | collective-permute-start | bytes 196616 | tf_op jit(solution)/shard_map/ppermute | solution.py:372
  56.1 12.4 %collective-permute-start.3 = (f32[264,128]{1,0:T(8,128)S(1)}, f32[264,128]{1,0:T(8,128)S(1)}, u32[]{:S(2)}, u32[]{:S(2)}) collective-permute-start(f32[264,128]{1,0:T(8,128)S(1)} %get-tuple-element.42), channel_id=1, source_target_pairs={{0,16},{16,0},{1,17},{17,1},{2,18},{18,2},{3,19},{19,3},{4,20},{20... | collective-permute-start | bytes 405512 | tf_op jit(solution)/shard_map/ppermute | solution.py:372
  59.2 9.3 %copy-start.2 = (bf16[1,384,256]{2,1,0:T(8,128)(2,1)S(1)}, bf16[1,384,256]{2,1,0:T(8,128)(2,1)}, u32[]{:S(2)}) copy-start(bf16[1,384,256]{2,1,0:T(8,128)(2,1)} %param.5) | copy-start | bytes 589828
  59.2 12.3 %collective-permute-start.2 = (f32[192,128]{1,0:T(8,128)S(1)}, f32[192,128]{1,0:T(8,128)S(1)}, u32[]{:S(2)}, u32[]{:S(2)}) collective-permute-start(f32[192,128]{1,0:T(8,128)S(1)} %get-tuple-element.40), channel_id=1, source_target_pairs={{0,16},{16,0},{1,17},{17,1},{2,18},{18,2},{3,19},{19,3},{4,20},{20... | collective-permute-start | bytes 294920 | tf_op jit(solution)/shard_map/ppermute | solution.py:372
  75.4 9.8 %collective-permute-start.5 = (bf16[384,256]{1,0:T(8,128)(2,1)S(1)}, bf16[384,256]{1,0:T(8,128)(2,1)S(1)}, u32[]{:S(2)}, u32[]{:S(2)}) collective-permute-start(bf16[384,256]{1,0:T(8,128)(2,1)S(1)} %shard_map.51), channel_id=1, source_target_pairs={{0,16},{16,0},{1,17},{17,1},{2,18},{18,2},{3,19},{19,3},{4,20},{20... | collective-permute-start | bytes 589832 | tf_op jit(solution)/shard_map/ppermute | solution.py:374
